TPU v7x, 32 devices: a whole 2x2x4 slice. The times are simulated.
32 devices in a mesh: blk: 4 (over y, x), seq: 8 (over z, core).
Axes of the slice: x: 2, y: 2, z: 4, core: 2. Of those that a mesh axis runs over, the one named last changes fastest.
Arguments:
- tokens: bfloat16 [4, 2048, 1024], P('blk', 'seq'), may hold values from -128 to 128
- expert_ids: int32 [4, 2048, 1], P('blk', 'seq'), may hold values from 0 to 7; in each aligned block of 256 rows (0 to 255, 256 to 511, ..., all dimensions but the last counted through in order) at most 64 rows name the same one
- expert_capacity: int32 [8], replicated, may hold values from 32 to 64, as said below
- kernel_weight: bfloat16 [1024, 496], replicated, may hold values from -1 to 1
- norm_gain: bfloat16 [1024], replicated, may hold values from 0.25 to 1.75
- router: bfloat16 [1024, 8], replicated, may hold values from -0.1875 to 0.1875
- expert_gate: bfloat16 [8, 1024, 2048], P('seq', None, 'blk'), may hold values from -0.1875 to 0.1875
- expert_up: bfloat16 [8, 1024, 2048], P('seq', None, 'blk'), may hold values from -0.1875 to 0.1875
- expert_down: bfloat16 [8, 1024, 2048], P('seq', None, 'blk'), may hold values from -0.125 to 0.125
Outputs:
- result: bfloat16 [4, 2048, 1024], P('blk', 'seq')
Inputs may be any that keep to these rules, and one draw needn't show every extreme that they name: `expert_ids`: in each aligned block of 256 positions (the positions of one device) no expert is named more than 64 times, a bound that some block reaches. `expert_capacity`: some expert has capacity exactly 64.
All inputs are finite; a program needn't handle non-finite values.
Results may differ from a plain program's by a relative error of at most 0.004.
Values may be sent and summed in bfloat16 or wider, within the bound.
No kernel may reach another device: no remote copies, remote signals or barrier semaphores. Data moves between devices by JAX's collectives and lax.ppermute only.
A program may use at most 128 MiB of HBM per device.

v0:
```python
import jax
import jax.numpy as jnp
from jax import lax
from jax.sharding import PartitionSpec as P

HEADS = 16
TAPS = 31


EPS = 1e-06


def padded_2(block, sides, width):
    for axis, dim in sides:
        count = lax.axis_size(axis)
        forward = [(i, i + 1) for i in range(count - 1)]
        backward = [(target, source) for source, target in forward]
        low = lax.ppermute(
            lax.slice_in_dim(block, block.shape[dim] - width, None, axis=dim), axis, forward
        )
        high = lax.ppermute(lax.slice_in_dim(block, 0, width, axis=dim), axis, backward)
        block = jnp.concatenate([low, block, high], axis=dim)
    return block


def expert_rows(rows, gate_piece, up_piece, down_piece):
    gated = jnp.dot(rows, gate_piece, preferred_element_type=jnp.float32)
    lifted = jnp.dot(rows, up_piece, preferred_element_type=jnp.float32)
    act = (jax.nn.silu(gated) * lifted).astype(jnp.bfloat16)
    return lax.dot_general(
        act, down_piece, (((1,), (1,)), ((), ())), preferred_element_type=jnp.float32
    )


def on_device(
    tokens,
    expert_ids,
    expert_capacity,
    kernel_weight,
    norm_gain,
    router,
    expert_gate,
    expert_up,
    expert_down,
):
    local = tokens[0]
    count, width = local.shape
    head_width = width // HEADS
    padded = padded_2(tokens, (("seq", 1),), TAPS // 2)[0]
    logits = jnp.dot(local, kernel_weight, preferred_element_type=jnp.float32).reshape(
        count, HEADS, TAPS
    )
    probs = jax.nn.softmax(logits, axis=-1).astype(jnp.bfloat16)
    mixed = local.astype(jnp.float32)
    for k in range(TAPS):
        weight = jnp.repeat(probs[:, :, k].astype(jnp.float32), head_width, axis=1)
        mixed = mixed + weight * padded[k : k + count].astype(jnp.float32)
    scale = lax.rsqrt(jnp.mean(mixed * mixed, axis=-1, keepdims=True) + EPS)
    normed = (mixed * scale * norm_gain.astype(jnp.float32)).astype(jnp.bfloat16)
    experts = expert_capacity.shape[0]
    depth = max(2, 2 * count // experts)
    ids = expert_ids[0, :, 0]
    onehot = (ids[:, None] == jnp.arange(experts, dtype=jnp.int32)[None, :]).astype(jnp.int32)
    rank = jnp.sum((jnp.cumsum(onehot, axis=0) - 1) * onehot, axis=1)
    limit = jnp.sum(onehot * expert_capacity[None, :], axis=1)
    kept = rank < limit
    slot = jnp.where(kept, ids * depth + rank, -1)
    select = (slot[:, None] == jnp.arange(experts * depth, dtype=jnp.int32)[None, :]).astype(
        jnp.bfloat16
    )
    gate_all = jnp.dot(normed, router, preferred_element_type=jnp.float32)
    gate = jax.nn.sigmoid(jnp.sum(gate_all * onehot.astype(jnp.float32), axis=1))
    packed = lax.dot_general(
        select, normed, (((0,), (0,)), ((), ())), preferred_element_type=jnp.float32
    )
    packed = packed.astype(jnp.bfloat16).reshape(experts, depth, width)
    arrived = lax.all_to_all(packed, "seq", split_axis=0, concat_axis=0, tiled=True)
    rows = arrived.reshape(-1, width)
    produced = expert_rows(
        rows,
        lax.all_gather(expert_gate, "blk", axis=2, tiled=True)[0],
        lax.all_gather(expert_up, "blk", axis=2, tiled=True)[0],
        lax.all_gather(expert_down, "blk", axis=2, tiled=True)[0],
    )
    sent = produced.astype(jnp.bfloat16).reshape(arrived.shape)
    back = lax.all_to_all(sent, "seq", split_axis=0, concat_axis=0, tiled=True).reshape(
        experts * depth, width
    )
    token_out = jnp.dot(select, back, preferred_element_type=jnp.float32)
    result = mixed + gate[:, None] * token_out
    return result.astype(jnp.bfloat16)[None]


def solution(mesh):
    placed = (
        P("blk", "seq", None),
        P("blk", "seq", None),
        P(),
        P(),
        P(),
        P(),
        P("seq", None, "blk"),
        P("seq", None, "blk"),
        P("seq", None, "blk"),
    )
    return jax.shard_map(
        on_device, mesh=mesh, in_specs=placed, out_specs=P("blk", "seq", None), check_vma=False
    )
```

profile of v0, /device:TPU:0, one launch (start us, length us, event | category | flops | bytes accessed | tf_op | source)
XLA Modules:
  0.0 222.6 jit_solution(5647180167767657653)
XLA Ops:
  8.1 1.4 fusion.89
  9.5 1.3 collective-permute-start.1
  10.8 3.6 %collective-permute-start = (bf16[1,15,1024]{2,1,0:T(8,128)(2,1)}, bf16[1,15,1024]{2,1,0:T(8,128)(2,1)}, u32[]{:S(2)}, u32[]{:S(2)}) collective-permute-start(bf16[1,15,1024]{2,1,0:T(8,128)(2,1)} %get-tuple-element.9), channel_id=1, source_target_pairs={{0,1},{1,2},{2,3},{3,4},{4,5},{5,6},{6,7},{8,9},{9,10},{10,11},{11... | collective-permute-start | bytes 92168 | tf_op jit(solution)/shard_map/ppermute | solution.py:18
  14.4 1.5 dot_general.26
  16.6 0.9 slice_convert_fusion.30
  22.2 0.8 broadcast_in_dim.123
  23.0 1.4 copy.55
  24.4 0.8 broadcast_in_dim.124
  25.2 1.3 copy.56
  26.5 0.8 broadcast_in_dim.125
  27.3 1.3 copy.57
  28.6 0.8 broadcast_in_dim.126
  29.4 1.3 copy.58
  30.7 0.8 broadcast_in_dim.127
  31.5 1.3 copy.59
  33.6 1.3 copy.60
  35.8 1.4 copy.61
  37.2 1.3 copy.62
  38.6 1.3 copy.63
  40.0 1.3 copy.64
  41.4 1.4 copy.65
  42.9 1.4 copy.66
  44.4 1.3 copy.67
  45.8 1.3 copy.68
  47.2 1.3 copy.69
  48.6 1.3 copy.70
  50.0 1.3 copy.71
  51.4 1.3 copy.42
  52.8 1.4 copy.43
  54.3 1.3 copy.44
  55.7 1.3 copy.45
  57.0 1.3 copy.46
  58.5 1.4 copy.47
  59.9 1.3 copy.48
  61.3 1.3 copy.49
  62.7 1.3 copy.50
  64.1 1.3 copy.51
  65.5 1.3 copy.52
  66.9 1.3 copy.53
  68.3 1.4 copy.41
  70.5 13.9 %multiply_reduce_fusion = (f32[256]{0:T(256)S(1)}, f32[256,1024]{1,0:T(8,128)S(1)}) fusion(f32[256,1024]{1,0:T(8,128)} %copy.71, bf16[1,271,1024]{2,1,0:T(8,128)(2,1)S(1)} %constant_dynamic-update-slice_fusion, f32[256,1024]{1,0:T(8,128)} %copy.70, f32[256,1024]{1,0:T(8,128)} %copy.69, f32[256,1024]{1,0:T(8,128)} %copy.68, f32[256,1024]{1,0:T(8,128)} %copy.67, ...), kind=kLoop, calls=%fused_computation.95 | loop fusion | flops 40632064 | bytes 41974784 | tf_op jit(solution)/shard_map/reduce_sum | solution.py:58
  85.0 32.6 %all_to_all.10 = bf16[8,64,1024]{2,1,0:T(8,128)(2,1)S(1)} all-to-all(bf16[8,64,1024]{2,1,0:T(8,128)(2,1)S(1)} %bitcast.319), channel_id=1, replica_groups=mesh['blk'=4,'seq'=8] {'seq'}, dimensions={0} | all-to-all | bytes 2097152 | tf_op jit(solution)/shard_map/all_to_all | solution.py:77
  117.6 6.4 %fusion.5 = f32[512,2048]{1,0:T(8,128)} fusion(bf16[512,1024]{1,0:T(8,128)(2,1)S(1)} %bitcast.352, bf16[1,1024,2048]{2,1,0:T(8,128)(2,1)} %all-gather.4.cloned.1.call-done), kind=kOutput, calls=%fused_computation.5 | convolution fusion | flops 2147483648 | bytes 9437184 | tf_op jit(solution)/shard_map/dot_general | solution.py:27
  124.0 49.3 %all-gather.8.cloned.1.call-done = bf16[1,1024,2048]{2,1,0:T(8,128)(2,1)} async-done(((bf16[1,1024,512]{2,1,0:T(8,128)(2,1)}), bf16[1,1024,2048]{2,1,0:T(8,128)(2,1)}) %all-gather.8.cloned.1.call-update) | async-done | bytes 4194320 | tf_op jit(solution)/shard_map/all_gather | solution.py:83
  173.3 10.2 %fusion.11 = bf16[512,1024]{1,0:T(8,128)(2,1)} fusion(bf16[1,1024,2048]{2,1,0:T(8,128)(2,1)} %all-gather.8.cloned.1.call-done, f32[512,2048]{1,0:T(8,128)} %fusion.5, bf16[512,1024]{1,0:T(8,128)(2,1)S(1)} %bitcast.353, bf16[1,1024,2048]{2,1,0:T(8,128)(2,1)} %all-gather.6.cloned.1.call-done), kind=kOutput, calls=%fused_computation.23 | convolution fusion | flops 4301783040 | bytes 14680064 | tf_op jit(solution)/shard_map/dot_general | solution.py:30
  183.5 4.6 %all-to-all-start.1 = ((bf16[8,64,1024]{2,1,0:T(8,128)(2,1)}), bf16[8,64,1024]{2,1,0:T(8,128)(2,1)S(1)}, u32[]{:S(2)}, u32[]{:S(2)}) async-start(bf16[8,64,1024]{2,1,0:T(8,128)(2,1)} %bitcast.354), calls=%async_computation.1 | async-start | bytes 2097152 | tf_op jit(solution)/shard_map/all_to_all | solution.py:86
  188.5 26.2 %all-to-all-done.1 = bf16[8,64,1024]{2,1,0:T(8,128)(2,1)S(1)} async-done(((bf16[8,64,1024]{2,1,0:T(8,128)(2,1)}), bf16[8,64,1024]{2,1,0:T(8,128)(2,1)S(1)}, u32[]{:S(2)}, u32[]{:S(2)}) %all-to-all-start.1) | async-done | bytes 1048608 | tf_op jit(solution)/shard_map/all_to_all | solution.py:86
  214.7 1.3 fusion.20
  (86 shorter events, 11.8 us)
Async XLA Ops:
  6.5 181.6 %copy-start = (bf16[1024,8]{0,1:T(8,128)(2,1)S(1)}, bf16[1024,8]{0,1:T(8,128)(2,1)}, u32[]{:S(2)}) copy-start(bf16[1024,8]{0,1:T(8,128)(2,1)} %param.14) | copy-start | bytes 49156
  6.5 9.4 %copy-start.1 = (bf16[1,256,1024]{2,1,0:T(8,128)(2,1)S(1)}, bf16[1,256,1024]{2,1,0:T(8,128)(2,1)}, u32[]{:S(2)}) copy-start(bf16[1,256,1024]{2,1,0:T(8,128)(2,1)} %param.9) | copy-start | bytes 1572868
  6.5 111.1 %all-gather.4.cloned.1.call-start = ((), (), s32[]{:S(2)}) async-start(), calls=%async_computation.2 | async-start | bytes 5242880 | tf_op jit(solution)/shard_map/all_gather | solution.py:81
  7.3 10.3 %copy-start.3 = (s32[1,256,1]{1,2,0:T(1,128)S(1)}, s32[1,256,1]{1,2,0:T(1,128)}, u32[]{:S(2)}) copy-start(s32[1,256,1]{1,2,0:T(1,128)} %param.10) | copy-start | bytes 3076
  7.3 116.8 %all-gather.6.cloned.1.call-start = ((), (), s32[]{:S(2)}) async-start(), calls=%async_computation.3 | async-start | bytes 5242880 | tf_op jit(solution)/shard_map/all_gather | solution.py:82
  8.0 13.0 %copy-start.7 = (s32[8]{0:T(128)S(1)}, s32[8]{0:T(128)}, u32[]{:S(2)}) copy-start(s32[8]{0:T(128)} %param.11) | copy-start | bytes 100
  8.0 165.3 %all-gather.8.cloned.1.call-start = ((), (), s32[]{:S(2)}) async-start(), calls=%async_computation.4 | async-start | bytes 5242880 | tf_op jit(solution)/shard_map/all_gather | solution.py:83
  9.5 60.2 %collective-permute-start.1 = (bf16[1,15,1024]{2,1,0:T(8,128)(2,1)}, bf16[1,15,1024]{2,1,0:T(8,128)(2,1)}, u32[]{:S(2)}, u32[]{:S(2)}) collective-permute-start(bf16[1,15,1024]{2,1,0:T(8,128)(2,1)} %get-tuple-element.10), channel_id=1, source_target_pairs={{1,0},{2,1},{3,2},{4,3},{5,4},{6,5},{7,6},{9,8},{10,9},{11,10},{12... | collective-permute-start | bytes 92168 | tf_op jit(solution)/shard_map/ppermute | solution.py:21
  10.8 59.7 %collective-permute-start = (bf16[1,15,1024]{2,1,0:T(8,128)(2,1)}, bf16[1,15,1024]{2,1,0:T(8,128)(2,1)}, u32[]{:S(2)}, u32[]{:S(2)}) collective-permute-start(bf16[1,15,1024]{2,1,0:T(8,128)(2,1)} %get-tuple-element.9), channel_id=1, source_target_pairs={{0,1},{1,2},{2,3},{3,4},{4,5},{5,6},{6,7},{8,9},{9,10},{10,11},{11... | collective-permute-start | bytes 92168 | tf_op jit(solution)/shard_map/ppermute | solution.py:18
  64.1 4.1 %copy-start.2 = (f32[256,16,1]{0,2,1:T(1,128)S(1)}, f32[256,16,1]{0,2,1:T(1,128)}, u32[]{:S(2)}) copy-start(f32[256,16,1]{0,2,1:T(1,128)} %get-tuple-element.11) | copy-start | bytes 49156
  65.5 4.2 %copy-start.6 = (bf16[1024]{0:T(1024)(128)(2,1)S(1)}, bf16[1024]{0:T(1024)(128)(2,1)}, u32[]{:S(2)}) copy-start(bf16[1024]{0:T(1024)(128)(2,1)} %param.13) | copy-start | bytes 6148
  70.5 13.9 %copy-start.5 = (s32[256]{0:T(256)S(1)}, s32[256]{0:T(256)}, u32[]{:S(2)}) copy-start(s32[256]{0:T(256)} %compare_select_fusion) | copy-start | bytes 3076
  124.0 64.1 %copy-start.4 = (s32[1,256,1]{1,2,0:T(1,128)S(1)}, s32[1,256,1]{1,2,0:T(1,128)}, u32[]{:S(2)}) copy-start(s32[1,256,1]{1,2,0:T(1,128)} %param.10) | copy-start | bytes 3076
  183.5 31.2 %all-to-all-start.1 = ((bf16[8,64,1024]{2,1,0:T(8,128)(2,1)}), bf16[8,64,1024]{2,1,0:T(8,128)(2,1)S(1)}, u32[]{:S(2)}, u32[]{:S(2)}) async-start(bf16[8,64,1024]{2,1,0:T(8,128)(2,1)} %bitcast.354), calls=%async_computation.1 | async-start | bytes 2097152 | tf_op jit(solution)/shard_map/all_to_all | solution.py:86
Sparse Core Ops, SparseCore 0:
  9.2 55.2 all-gather.3
  66.3 52.5 all-gather.5
  120.7 52.5 all-gather.7
where the time goes:
time: 223 us
  waiting for transfers between devices  77 us (35%)
  local copies, waits for them, and re-layouts  54.1 us (24%)
  blocking collectives  32.6 us (15%)
  matrix products  19.4 us (9%)
  other arithmetic  16.3 us (7%)
  between operations  13.6 us (6%)
  starting transfers between devices  9.6 us (4%)
    all_gather x1, waiting for transfers between devices, on_device(): lax.all_gather(expert_down, 'blk', axis=2, tiled=True)[0]  49.3 us
    reshape x31, local copies, waits for them, and re-layouts, on_device(): weight = jnp.repeat(probs[:, :, k].astype(jnp.float32), head_width, axis=1)  40.3 us
    all_to_all x1, blocking collectives, on_device(): lax.all_to_all(packed, 'seq', split_axis=0, concat_axis=0, tiled=True)  32.6 us
    all_to_all x1, waiting for transfers between devices, on_device(): lax.all_to_all(sent, 'seq', split_axis=0, concat_axis=0, tiled=True)  26.2 us
    reduce_sum x1, other arithmetic, on_device(): scale = lax.rsqrt(jnp.mean(mixed * mixed, axis=-1, keepdims=True) + EPS)  13.9 us
    dot_general x1, matrix products, expert_rows(): lax.dot_general(act, down_piece, (((1,), (1,)), ((), ())), preferred_elem...  10.2 us
    broadcast_in_dim x31, local copies, waits for them, and re-layouts, on_device(): weight = jnp.repeat(probs[:, :, k].astype(jnp.float32), head_width, axis=1)  7.36 us
    dot_general x1, matrix products, expert_rows(): gated = jnp.dot(rows, gate_piece, preferred_element_type=jnp.float32)  6.45 us
  transfers between devices with their start and end apart: 6, of which 2 were waited for; matrix products, arithmetic and copies ran while one was open for 35% of the time, Pallas kernels for 0%

commit v1 on v0

v1 whole, which is shorter than its diff:
```python
import functools

import jax
import jax.numpy as jnp
from jax import lax
from jax.experimental import pallas as pl
from jax.experimental.pallas import tpu as pltpu
from jax.sharding import PartitionSpec as P

HEADS = 16
TAPS = 31
LANES = 32
HALO = 16
FRONT = 96
BLOCK = 128
EPS = 1e-06

VMEM = pl.BlockSpec(memory_space=pltpu.VMEM)
F32 = jnp.float32
BF16 = jnp.bfloat16


def iota(shape, dim):
    return lax.broadcasted_iota(jnp.int32, shape, dim)


def probs_kernel(tokens_ref, weight_ref, probs_ref):
    count = tokens_ref.shape[0]
    columns = weight_ref.shape[1]
    row = iota((columns, HEADS * LANES), 0)
    column = iota((columns, HEADS * LANES), 1)
    tap = column % LANES
    spread = jnp.where((column // LANES * TAPS + tap == row) & (tap < TAPS), 1.0, 0.0).astype(BF16)
    weight = jnp.dot(weight_ref[...], spread, preferred_element_type=F32).astype(BF16)
    logits = jnp.dot(tokens_ref[...], weight, preferred_element_type=F32)
    logits = logits.T.reshape(HEADS, LANES, count)
    used = iota(logits.shape, 1) < TAPS
    logits = jnp.where(used, logits, -3e38)
    top = jnp.max(logits, axis=1, keepdims=True)
    powers = jnp.exp(logits - top)
    probs = powers / jnp.sum(powers, axis=1, keepdims=True)
    probs_ref[...] = probs.reshape(HEADS * LANES, count).T.astype(BF16)


def slots_of(onehot, before, capacity, depth, axis):
    kept = jnp.sum(onehot * (before < capacity).astype(F32), axis=axis, keepdims=True) > 0.5
    expert = iota(onehot.shape, axis).astype(F32)
    slot = jnp.sum(onehot * (expert * depth + before), axis=axis, keepdims=True)
    return jnp.where(kept, slot, -1.0).astype(jnp.int32)


def mix_kernel(
    depth,
    tokens_ref,
    low_ref,
    high_ref,
    probs_ref,
    ids_row_ref,
    ids_ref,
    capacity_ref,
    capacity_row_ref,
    gain_ref,
    router_ref,
    mixed_ref,
    packed_ref,
    gate_ref,
    slot_ref,
    padded_ref,
    normed_ref,
):
    count, width = tokens_ref.shape
    experts = capacity_ref.shape[0]
    padded_ref[pl.ds(0, FRONT), :] = jnp.zeros((FRONT, width), BF16)
    padded_ref[pl.ds(FRONT, HALO), :] = low_ref[...]
    padded_ref[pl.ds(FRONT + HALO, count), :] = tokens_ref[...]
    padded_ref[pl.ds(FRONT + HALO + count, HALO), :] = high_ref[...]
    after = FRONT + 2 * HALO + count
    padded_ref[pl.ds(after, padded_ref.shape[0] - after), :] = jnp.zeros(
        (padded_ref.shape[0] - after, width), BF16
    )
    offset = iota((BLOCK, 2 * BLOCK), 1) - iota((BLOCK, 2 * BLOCK), 0) - 1
    squares = []
    for block in range(count // BLOCK):
        rows = pl.ds(block * BLOCK, BLOCK)
        square = jnp.zeros((BLOCK, 128), F32)
        for group in range(HEADS // 4):
            taps = probs_ref[rows, pl.ds(group * 128, 128)].astype(F32)
            taps = jnp.concatenate([taps, jnp.zeros((BLOCK, BLOCK), F32)], axis=1)
            band = pltpu.roll(taps, 1, 1, stride=1, stride_axis=0)
            for pair in range(2):
                lanes = pl.ds((group * 2 + pair) * 128, 128)
                halves = []
                for head in (2 * pair, 2 * pair + 1):
                    mine = (offset >= head * LANES) & (offset < (head + 1) * LANES)
                    own = jnp.where(mine, band, 0.0).astype(BF16)
                    start = FRONT + block * BLOCK - LANES * head
                    halves.append(
                        jnp.dot(
                            own,
                            padded_ref[pl.ds(start, 2 * BLOCK), lanes],
                            preferred_element_type=F32,
                        )
                    )
                left = iota((BLOCK, 128), 1) < 64
                mixed = tokens_ref[rows, lanes].astype(F32) + jnp.where(left, halves[0], halves[1])
                mixed_ref[rows, lanes] = mixed
                square = square + mixed * mixed
        squares.append(square)
    for block in range(count // BLOCK):
        rows = pl.ds(block * BLOCK, BLOCK)
        mean = jnp.sum(squares[block], axis=1, keepdims=True) / width
        scale = lax.rsqrt(mean + EPS)
        normed_ref[rows, :] = (mixed_ref[rows, :] * scale * gain_ref[...].astype(F32)).astype(BF16)

    normed = normed_ref[...]
    onehot = jnp.where(ids_ref[...] == iota((count, experts), 1), 1.0, 0.0)
    earlier = jnp.where(iota((count, count), 0) > iota((count, count), 1), 1.0, 0.0).astype(BF16)
    before = jnp.dot(earlier, onehot.astype(BF16), preferred_element_type=F32)
    slot_ref[...] = slots_of(onehot, before, capacity_row_ref[...].astype(F32), depth, 1)
    gates = jnp.dot(normed, router_ref[...], preferred_element_type=F32)
    gate_ref[...] = jax.nn.sigmoid(jnp.sum(gates * onehot, axis=1, keepdims=True))

    onehot_row = jnp.where(ids_row_ref[...] == iota((experts, count), 0), 1.0, 0.0)
    later = jnp.where(iota((count, count), 0) < iota((count, count), 1), 1.0, 0.0).astype(BF16)
    before_row = jnp.dot(onehot_row.astype(BF16), later, preferred_element_type=F32)
    slot_row = slots_of(onehot_row, before_row, capacity_ref[...].astype(F32), depth, 0)
    select = jnp.where(iota((experts * depth, count), 0) == slot_row, 1.0, 0.0).astype(BF16)
    packed_ref[...] = jnp.dot(select, normed, preferred_element_type=F32).astype(BF16)


def combine_kernel(mixed_ref, gate_ref, slot_ref, back_ref, out_ref):
    count = mixed_ref.shape[0]
    slots = back_ref.shape[0]
    select = jnp.where(slot_ref[...] == iota((count, slots), 1), 1.0, 0.0).astype(BF16)
    out = jnp.dot(select, back_ref[...], preferred_element_type=F32)
    out_ref[...] = (mixed_ref[...] + gate_ref[...] * out).astype(BF16)


def expert_kernel(pieces, rows_ref, *refs):
    weights, out_ref = refs[: 3 * pieces], refs[3 * pieces]
    rows = rows_ref[...]
    total = None
    for piece in range(pieces):
        gate_ref, up_ref, down_ref = weights[3 * piece : 3 * piece + 3]
        gated = jnp.dot(rows, gate_ref[...], preferred_element_type=F32)
        lifted = jnp.dot(rows, up_ref[...], preferred_element_type=F32)
        act = (gated / (1.0 + jnp.exp(-gated)) * lifted).astype(BF16)
        part = lax.dot_general(
            act, down_ref[...], (((1,), (1,)), ((), ())), preferred_element_type=F32
        )
        total = part if total is None else total + part
    out_ref[...] = total.astype(out_ref.dtype)


def call(kernel, out_shape, scratch=(), flops=0, moved=0):
    return pl.pallas_call(
        kernel,
        out_shape=out_shape,
        scratch_shapes=scratch,
        compiler_params=pltpu.CompilerParams(vmem_limit_bytes=40 * 1024 * 1024),
        cost_estimate=pl.CostEstimate(flops=flops, bytes_accessed=moved, transcendentals=0),
    )


def shape(dims, dtype):
    return jax.ShapeDtypeStruct(dims, dtype)


def on_device(
    tokens,
    expert_ids,
    expert_capacity,
    kernel_weight,
    norm_gain,
    router,
    expert_gate,
    expert_up,
    expert_down,
):
    local = tokens[0]
    count, width = local.shape
    experts = expert_capacity.shape[0]
    depth = max(2, 2 * count // experts)
    slots = experts * depth
    splits = lax.axis_size("blk")
    blocks = lax.axis_size("seq")
    groups = splits // 2
    partner = [(i, i ^ 1) for i in range(splits)]

    def turned(array, step):
        return lax.ppermute(
            array, "blk", [(i, (i + 2 * step) % splits) for i in range(splits)]
        )

    forward = [(i, i + 1) for i in range(blocks - 1)]
    backward = [(target, source) for source, target in forward]
    low = lax.ppermute(local[count - HALO :], "seq", forward)
    high = lax.ppermute(local[:HALO], "seq", backward)
    weights = [expert_gate[0], expert_up[0], expert_down[0]]
    for step in range(1, groups):
        weights += [turned(expert_gate[0], step), turned(expert_up[0], step), turned(expert_down[0], step)]

    probs = call(
        probs_kernel, shape((count, HEADS * LANES), BF16), flops=2 * count * width * 512 * 4, moved=1 << 21
    )(local, kernel_weight)
    ids = expert_ids[0]
    mixed, packed, gate, slot = call(
        functools.partial(mix_kernel, depth),
        (
            shape((count, width), F32),
            shape((slots, width), BF16),
            shape((count, 1), F32),
            shape((count, 1), jnp.int32),
        ),
        scratch=(
            pltpu.VMEM((FRONT + count + BLOCK, width), BF16),
            pltpu.VMEM((count, width), BF16),
        ),
        flops=1 << 31,
        moved=1 << 22,
    )(
        local,
        low,
        high,
        probs,
        ids.reshape(1, count),
        ids,
        expert_capacity[:, None],
        expert_capacity[None, :],
        norm_gain[None, :],
        router,
    )
    arrived = lax.all_to_all(
        packed.reshape(experts, depth, width), "seq", split_axis=0, concat_axis=0, tiled=True
    )
    rows = arrived.reshape(-1, width)
    other = lax.ppermute(rows, "blk", partner)
    total = rows.shape[0]
    flops = 6 * total * width * weights[0].shape[1] * groups
    other_part = call(
        functools.partial(expert_kernel, groups), shape((total, width), BF16), flops=flops, moved=1 << 23
    )(other, *weights)
    back_part = lax.ppermute(other_part, "blk", partner)
    own_part = call(
        functools.partial(expert_kernel, groups), shape((total, width), F32), flops=flops, moved=1 << 23
    )(rows, *weights)
    sent = (own_part + back_part.astype(F32)).astype(BF16).reshape(arrived.shape)
    back = lax.all_to_all(sent, "seq", split_axis=0, concat_axis=0, tiled=True).reshape(slots, width)
    result = call(combine_kernel, shape((count, width), BF16), flops=1 << 28, moved=1 << 22)(
        mixed, gate, slot, back
    )
    return result[None]


def solution(mesh):
    placed = (
        P("blk", "seq", None),
        P("blk", "seq", None),
        P(),
        P(),
        P(),
        P(),
        P("seq", None, "blk"),
        P("seq", None, "blk"),
        P("seq", None, "blk"),
    )
    return jax.shard_map(
        on_device, mesh=mesh, in_specs=placed, out_specs=P("blk", "seq", None), check_vma=False
    )
```

time: 223 us -> 154 us (0.69)
  local copies, waits for them, and re-layouts: 54.1 us -> 5.2 us
  matrix products: 19.4 us -> 0 us
  other arithmetic: 16.3 us -> 0.35 us
  Pallas kernels: 0 us -> 15.9 us
  between operations: 13.6 us -> 0.17 us
  starting transfers between devices: 9.6 us -> 17.5 us
  waiting for transfers between devices: 77 us -> 83.3 us
    ppermute x2 -> x7, waiting for transfers between devices: 0.01 us -> 60.3 us  [the longest x3 42.5 us: turned(): lax.ppermute(array, 'blk', [(i, (i + 2 * step) % splits) for i in range(s...]
    all_gather x3 -> x0, waiting for transfers between devices: 49.3 us -> none  [the longest x1 49.3 us: on_device(): lax.all_gather(expert_down, 'blk', axis=2, tiled=True)[0]]
    reshape x31 -> x0, local copies, waits for them, and re-layouts: 40.3 us -> none  [on_device(): weight = jnp.repeat(probs[:, :, k].astype(jnp.float32), head_width, axis=1)]
    dot_general x5 -> x0, matrix products: 18.8 us -> none  [the longest x1 10.2 us: expert_rows(): lax.dot_general(act, down_piece, (((1,), (1,)), ((), ())), preferred_elem...]
    pallas_call x0 -> x5, Pallas kernels: none -> 15.9 us  [the longest x1 5.41 us: on_device(): call(functools.partial(expert_kernel, groups), shape((total, width), F32)...]
    reduce_sum x2 -> x0, other arithmetic: 14 us -> none  [the longest x1 13.9 us: on_device(): scale = lax.rsqrt(jnp.mean(mixed * mixed, axis=-1, keepdims=True) + EPS)]
    broadcast_in_dim x31 -> x2, local copies, waits for them, and re-layouts: 7.36 us -> 0.09 us  [the longest x1 0.08 us: on_device(): expert_capacity[:, None]]
    ppermute x2 -> x7, starting transfers between devices: 4.91 us -> 11 us  [the longest x3 3.64 us: turned(): lax.ppermute(array, 'blk', [(i, (i + 2 * step) % splits) for i in range(s...]
  transfers between devices with their start and end apart: 6 -> 8, of which waited for: 2 -> 4; matrix products, arithmetic and copies ran while one was open for 35% -> 1% of each run, Pallas kernels for 0% -> 4%
where the time goes in v1:
time: 154 us; the launch traced here: 153 us
  waiting for transfers between devices  83.3 us (54%)
  blocking collectives  30.8 us (20%)
  starting transfers between devices  17.5 us (11%)
  Pallas kernels  15.9 us (10%)
  local copies, waits for them, and re-layouts  5.2 us (3%)
    ppermute x3, waiting for transfers between devices, turned(): lax.ppermute(array, 'blk', [(i, (i + 2 * step) % splits) for i in range(s...  42.5 us
    all_to_all x1, blocking collectives, on_device(): lax.all_to_all(sent, 'seq', split_axis=0, concat_axis=0, tiled=True)  30.8 us
    all_to_all x1, waiting for transfers between devices, on_device(): lax.all_to_all(packed.reshape(experts, depth, width), 'seq', split_axis=0...  23 us
    ppermute x1, waiting for transfers between devices, on_device(): back_part = lax.ppermute(other_part, 'blk', partner)  17.8 us
    all_to_all x1, starting transfers between devices, on_device(): lax.all_to_all(packed.reshape(experts, depth, width), 'seq', split_axis=0...  6.44 us
    pallas_call x1, Pallas kernels, on_device(): call(functools.partial(expert_kernel, groups), shape((total, width), F32)...  5.41 us
    pallas_call x1, Pallas kernels, on_device(): call(functools.partial(expert_kernel, groups), shape((total, width), BF16...  5.4 us
    unnamed x18, local copies, waits for them, and re-layouts  4.14 us
  transfers between devices with their start and end apart: 8, of which 4 were waited for; matrix products, arithmetic and copies ran while one was open for 1% of the time, Pallas kernels for 4%

profile of v1, /device:TPU:0, one launch (start us, length us, event | category | flops | bytes accessed | tf_op | source)
XLA Modules:
  0.0 153.2 jit_solution(5100028676188959873)
XLA Ops:
  0.0 0.0 copy-start
  0.0 0.8 slice_bitcast_fusion
  0.8 1.3 collective-permute-start.1
  2.1 3.0 %collective-permute-start = (bf16[16,1024]{1,0:T(8,128)(2,1)S(1)}, bf16[16,1024]{1,0:T(8,128)(2,1)S(1)}, u32[]{:S(2)}, u32[]{:S(2)}) collective-permute-start(bf16[16,1024]{1,0:T(8,128)(2,1)S(1)} %get-tuple-element.14), channel_id=1, source_target_pairs={{0,1},{1,2},{2,3},{3,4},{4,5},{5,6},{6,7},{8,9},{9,10},{10,11},{11... | collective-permute-start | bytes 98312 | tf_op jit(solution)/shard_map/ppermute | solution.py:197
  5.2 1.5 copy.13.weight_ref
  6.7 0.0 copy-start.7
  6.7 0.0 copy-start.2
  6.7 0.0 copy-start.1
  6.7 0.0 copy-start.6
  6.7 0.0 copy-done
  6.7 1.2 shard_map.91.probs_ref
  8.0 0.0 copy-done.7
  8.0 0.0 copy-done.2
  8.0 0.1 copy.15.capacity_ref
  8.1 0.0 copy-done.1
  8.1 0.1 copy.14.ids_ref
  8.2 0.0 copy-done.6
  8.2 0.2 copy.16.router_ref
  8.4 0.0 collective-permute-done.1.high_ref
  8.4 0.0 collective-permute-done.low_ref
  8.4 2.6 %shard_map.92 = (f32[256,1024]{1,0:T(8,128)S(1)}, bf16[512,1024]{1,0:T(8,128)(2,1)}, f32[256,1]{1,0:T(8,128)S(1)}, s32[256,1]{1,0:T(8,128)S(1)}) custom-call(bf16[256,1024]{1,0:T(8,128)(2,1)S(1)} %bitcast.21, bf16[16,1024]{1,0:T(8,128)(2,1)S(1)} %collective-permute-done.low_ref, bf16[16,1024]{1,0:T(8,128)(2,1)S(1)} %collective-permute-done.1.high_ref, ...), custom_call_target="tpu_custom_call" | custom-call | flops 2147483648 | bytes 4194304 | tf_op jit(solution)/shard_map/pallas_call | solution.py:207
  11.0 0.0 copy-start.3
  11.0 6.4 %all-to-all-start = ((bf16[8,64,1024]{2,1,0:T(8,128)(2,1)}), bf16[8,64,1024]{2,1,0:T(8,128)(2,1)S(1)}, u32[]{:S(2)}, u32[]{:S(2)}) async-start(bf16[8,64,1024]{2,1,0:T(8,128)(2,1)} %bitcast.7), calls=%async_computation | async-start | bytes 2097152 | tf_op jit(solution)/shard_map/all_to_all | solution.py:233
  17.5 0.0 copy-done.3
  17.5 1.6 %collective-permute-start.2 = (bf16[1024,512]{1,0:T(8,128)(2,1)S(1)}, bf16[1024,512]{1,0:T(8,128)(2,1)}, u32[]{:S(2)}, u32[]{:S(2)}) collective-permute-start(bf16[1024,512]{1,0:T(8,128)(2,1)S(1)} %bitcast.26), channel_id=1, source_target_pairs={{0,16},{8,24},{16,0},{24,8},{1,17},{9,25},{17,1},{25,9},{2,18},{10... | collective-permute-start | bytes 3145736 | tf_op jit(solution)/shard_map/ppermute | solution.py:191
  19.1 0.5 collective-permute-start.3
  19.5 1.5 %collective-permute-start.4 = (bf16[1024,512]{1,0:T(8,128)(2,1)}, bf16[1024,512]{1,0:T(8,128)(2,1)}, u32[]{:S(2)}, u32[]{:S(2)}) collective-permute-start(bf16[1024,512]{1,0:T(8,128)(2,1)} %bitcast.32), channel_id=1, source_target_pairs={{0,16},{8,24},{16,0},{24,8},{1,17},{9,25},{17,1},{25,9},{2,18},{10... | collective-permute-start | bytes 3145736 | tf_op jit(solution)/shard_map/ppermute | solution.py:191
  21.1 23.0 %all-to-all-done = bf16[8,64,1024]{2,1,0:T(8,128)(2,1)S(1)} async-done(((bf16[8,64,1024]{2,1,0:T(8,128)(2,1)}), bf16[8,64,1024]{2,1,0:T(8,128)(2,1)S(1)}, u32[]{:S(2)}, u32[]{:S(2)}) %all-to-all-start) | async-done | bytes 1048608 | tf_op jit(solution)/shard_map/all_to_all | solution.py:233
  44.0 1.5 collective-permute-start.5
  45.6 0.0 collective-permute-done.2.refs_3_
  45.6 20.5 %collective-permute-done.3.refs_4_ = bf16[1024,512]{1,0:T(8,128)(2,1)} collective-permute-done((bf16[1024,512]{1,0:T(8,128)(2,1)}, bf16[1024,512]{1,0:T(8,128)(2,1)}, u32[]{:S(2)}, u32[]{:S(2)}) %collective-permute-start.3) | collective-permute-done | bytes 1048608 | tf_op jit(solution)/shard_map/ppermute | solution.py:191
  66.1 22.0 %collective-permute-done.4.refs_5_ = bf16[1024,512]{1,0:T(8,128)(2,1)} collective-permute-done((bf16[1024,512]{1,0:T(8,128)(2,1)}, bf16[1024,512]{1,0:T(8,128)(2,1)}, u32[]{:S(2)}, u32[]{:S(2)}) %collective-permute-start.4) | collective-permute-done | bytes 1048608 | tf_op jit(solution)/shard_map/ppermute | solution.py:191
  88.1 0.0 collective-permute-done.5.rows_ref
  88.1 0.0 copy-start.4
  88.1 1.2 copy-done.4
  89.3 0.0 copy-start.5
  89.3 1.2 copy-done.5
  90.5 5.4 %shard_map.94 = bf16[512,1024]{1,0:T(8,128)(2,1)S(1)} custom-call(bf16[512,1024]{1,0:T(8,128)(2,1)S(1)} %collective-permute-done.5.rows_ref, bf16[1024,512]{1,0:T(8,128)(2,1)S(1)} %bitcast.27, bf16[1024,512]{1,0:T(8,128)(2,1)S(1)} %bitcast.30, bf16[1024,512]{1,0:T(8,128)(2,1)S(1)} %bitcast.33, bf16[1024,512]{1,0:T(8,128)(2,1)} %collective-permute-done.2.refs_3_, ...), custom_call_target="tpu_custom_call" | custom-call | flops 3221225472 | bytes 8388608 | tf_op jit(solution)/shard_map/pallas_call | solution.py:240
  95.9 1.6 %collective-permute-start.6 = (bf16[512,1024]{1,0:T(8,128)(2,1)S(1)}, bf16[512,1024]{1,0:T(8,128)(2,1)S(1)}, u32[]{:S(2)}, u32[]{:S(2)}) collective-permute-start(bf16[512,1024]{1,0:T(8,128)(2,1)S(1)} %shard_map.94), channel_id=1, source_target_pairs={{0,8},{8,0},{16,24},{24,16},{1,9},{9,1},{17,25},{25,17},{2,10},{10... | collective-permute-start | bytes 3145736 | tf_op jit(solution)/shard_map/ppermute | solution.py:243
  97.5 5.4 %shard_map.93 = f32[512,1024]{1,0:T(8,128)S(1)} custom-call(bf16[512,1024]{1,0:T(8,128)(2,1)S(1)} %bitcast.19, bf16[1024,512]{1,0:T(8,128)(2,1)S(1)} %bitcast.28, bf16[1024,512]{1,0:T(8,128)(2,1)S(1)} %bitcast.31, bf16[1024,512]{1,0:T(8,128)(2,1)S(1)} %bitcast.34, bf16[1024,512]{1,0:T(8,128)(2,1)} %collective-permute-done.2.refs_3_, ...), custom_call_target="tpu_custom_call" | custom-call | flops 3221225472 | bytes 8388608 | tf_op jit(solution)/shard_map/pallas_call | solution.py:244
  102.9 17.8 %collective-permute-done.6 = bf16[512,1024]{1,0:T(8,128)(2,1)S(1)} collective-permute-done((bf16[512,1024]{1,0:T(8,128)(2,1)S(1)}, bf16[512,1024]{1,0:T(8,128)(2,1)S(1)}, u32[]{:S(2)}, u32[]{:S(2)}) %collective-permute-start.6) | collective-permute-done | bytes 1048608 | tf_op jit(solution)/shard_map/ppermute | solution.py:243
  120.7 0.3 add_convert_fusion
  121.1 30.8 %all_to_all.10 = bf16[8,64,1024]{2,1,0:T(8,128)(2,1)S(1)} all-to-all(bf16[8,64,1024]{2,1,0:T(8,128)(2,1)S(1)} %bitcast.35), channel_id=1, replica_groups=mesh['blk'=4,'seq'=8] {'seq'}, dimensions={0} | all-to-all | bytes 2097152 | tf_op jit(solution)/shard_map/all_to_all | solution.py:248
  151.9 1.3 shard_map.95
  (1 shorter events, 0.0 us)
Async XLA Ops:
  0.0 6.7 %copy-start = (bf16[1,256,1024]{2,1,0:T(8,128)(2,1)S(1)}, bf16[1,256,1024]{2,1,0:T(8,128)(2,1)}, u32[]{:S(2)}) copy-start(bf16[1,256,1024]{2,1,0:T(8,128)(2,1)} %param.9) | copy-start | bytes 1572868
  0.8 7.6 %collective-permute-start.1 = (bf16[16,1024]{1,0:T(8,128)(2,1)S(1)}, bf16[16,1024]{1,0:T(8,128)(2,1)S(1)}, u32[]{:S(2)}, u32[]{:S(2)}) collective-permute-start(bf16[16,1024]{1,0:T(8,128)(2,1)S(1)} %get-tuple-element.13), channel_id=1, source_target_pairs={{1,0},{2,1},{3,2},{4,3},{5,4},{6,5},{7,6},{9,8},{10,9},{11,10},{12... | collective-permute-start | bytes 98312 | tf_op jit(solution)/shard_map/ppermute | solution.py:198
  2.1 6.3 %collective-permute-start = (bf16[16,1024]{1,0:T(8,128)(2,1)S(1)}, bf16[16,1024]{1,0:T(8,128)(2,1)S(1)}, u32[]{:S(2)}, u32[]{:S(2)}) collective-permute-start(bf16[16,1024]{1,0:T(8,128)(2,1)S(1)} %get-tuple-element.14), channel_id=1, source_target_pairs={{0,1},{1,2},{2,3},{3,4},{4,5},{5,6},{6,7},{8,9},{9,10},{10,11},{11... | collective-permute-start | bytes 98312 | tf_op jit(solution)/shard_map/ppermute | solution.py:197
  6.7 1.3 copy-start.7
  6.7 1.3 copy-start.2
  6.7 1.4 copy-start.1
  6.7 1.5 %copy-start.6 = (bf16[1024,8]{0,1:T(8,128)(2,1)S(1)}, bf16[1024,8]{0,1:T(8,128)(2,1)}, u32[]{:S(2)}) copy-start(bf16[1024,8]{0,1:T(8,128)(2,1)} %param.14) | copy-start | bytes 49156
  11.0 6.4 %copy-start.3 = (bf16[1,1024,512]{2,1,0:T(8,128)(2,1)S(1)}, bf16[1,1024,512]{2,1,0:T(8,128)(2,1)}, u32[]{:S(2)}) copy-start(bf16[1,1024,512]{2,1,0:T(8,128)(2,1)} %param.15) | copy-start | bytes 3145732
  11.0 33.0 %all-to-all-start = ((bf16[8,64,1024]{2,1,0:T(8,128)(2,1)}), bf16[8,64,1024]{2,1,0:T(8,128)(2,1)S(1)}, u32[]{:S(2)}, u32[]{:S(2)}) async-start(bf16[8,64,1024]{2,1,0:T(8,128)(2,1)} %bitcast.7), calls=%async_computation | async-start | bytes 2097152 | tf_op jit(solution)/shard_map/all_to_all | solution.py:233
  17.5 28.1 %collective-permute-start.2 = (bf16[1024,512]{1,0:T(8,128)(2,1)S(1)}, bf16[1024,512]{1,0:T(8,128)(2,1)}, u32[]{:S(2)}, u32[]{:S(2)}) collective-permute-start(bf16[1024,512]{1,0:T(8,128)(2,1)S(1)} %bitcast.26), channel_id=1, source_target_pairs={{0,16},{8,24},{16,0},{24,8},{1,17},{9,25},{17,1},{25,9},{2,18},{10... | collective-permute-start | bytes 3145736 | tf_op jit(solution)/shard_map/ppermute | solution.py:191
  19.1 47.0 %collective-permute-start.3 = (bf16[1024,512]{1,0:T(8,128)(2,1)}, bf16[1024,512]{1,0:T(8,128)(2,1)}, u32[]{:S(2)}, u32[]{:S(2)}) collective-permute-start(bf16[1024,512]{1,0:T(8,128)(2,1)} %bitcast.29), channel_id=1, source_target_pairs={{0,16},{8,24},{16,0},{24,8},{1,17},{9,25},{17,1},{25,9},{2,18},{10... | collective-permute-start | bytes 3145736 | tf_op jit(solution)/shard_map/ppermute | solution.py:191
  19.5 68.5 %collective-permute-start.4 = (bf16[1024,512]{1,0:T(8,128)(2,1)}, bf16[1024,512]{1,0:T(8,128)(2,1)}, u32[]{:S(2)}, u32[]{:S(2)}) collective-permute-start(bf16[1024,512]{1,0:T(8,128)(2,1)} %bitcast.32), channel_id=1, source_target_pairs={{0,16},{8,24},{16,0},{24,8},{1,17},{9,25},{17,1},{25,9},{2,18},{10... | collective-permute-start | bytes 3145736 | tf_op jit(solution)/shard_map/ppermute | solution.py:191
  44.0 44.0 %collective-permute-start.5 = (bf16[512,1024]{1,0:T(8,128)(2,1)S(1)}, bf16[512,1024]{1,0:T(8,128)(2,1)S(1)}, u32[]{:S(2)}, u32[]{:S(2)}) collective-permute-start(bf16[512,1024]{1,0:T(8,128)(2,1)S(1)} %bitcast.18), channel_id=1, source_target_pairs={{0,8},{8,0},{16,24},{24,16},{1,9},{9,1},{17,25},{25,17},{2,10},{10... | collective-permute-start | bytes 3145736 | tf_op jit(solution)/shard_map/ppermute | solution.py:237
  88.1 1.2 copy-start.4
  89.3 1.2 copy-start.5
  95.9 24.8 %collective-permute-start.6 = (bf16[512,1024]{1,0:T(8,128)(2,1)S(1)}, bf16[512,1024]{1,0:T(8,128)(2,1)S(1)}, u32[]{:S(2)}, u32[]{:S(2)}) collective-permute-start(bf16[512,1024]{1,0:T(8,128)(2,1)S(1)} %shard_map.94), channel_id=1, source_target_pairs={{0,8},{8,0},{16,24},{24,16},{1,9},{9,1},{17,25},{25,17},{2,10},{10... | collective-permute-start | bytes 3145736 | tf_op jit(solution)/shard_map/ppermute | solution.py:243

commit v2 on v1

--- a/solution.py
+++ b/solution.py
@@ -42,10 +42,11 @@
     probs_ref[...] = probs.reshape(HEADS * LANES, count).T.astype(BF16)
 
 
-def slots_of(onehot, before, capacity, depth, axis):
+def slots_of(onehot, before, capacity, place, depth, axis):
     kept = jnp.sum(onehot * (before < capacity).astype(F32), axis=axis, keepdims=True) > 0.5
-    expert = iota(onehot.shape, axis).astype(F32)
-    slot = jnp.sum(onehot * (expert * depth + before), axis=axis, keepdims=True)
+    apart = iota(onehot.shape, axis) ^ place
+    first = ((apart >> 1) + (apart & 1) * (onehot.shape[axis] // 2)) * depth
+    slot = jnp.sum(onehot * (first.astype(F32) + before), axis=axis, keepdims=True)
     return jnp.where(kept, slot, -1.0).astype(jnp.int32)
 
 
@@ -59,6 +60,7 @@
     ids_ref,
     capacity_ref,
     capacity_row_ref,
+    place_ref,
     gain_ref,
     router_ref,
     mixed_ref,
@@ -116,30 +118,37 @@
     onehot = jnp.where(ids_ref[...] == iota((count, experts), 1), 1.0, 0.0)
     earlier = jnp.where(iota((count, count), 0) > iota((count, count), 1), 1.0, 0.0).astype(BF16)
     before = jnp.dot(earlier, onehot.astype(BF16), preferred_element_type=F32)
-    slot_ref[...] = slots_of(onehot, before, capacity_row_ref[...].astype(F32), depth, 1)
+    slot_ref[...] = slots_of(onehot, before, capacity_row_ref[...].astype(F32), place_ref[...], depth, 1)
     gates = jnp.dot(normed, router_ref[...], preferred_element_type=F32)
     gate_ref[...] = jax.nn.sigmoid(jnp.sum(gates * onehot, axis=1, keepdims=True))
 
     onehot_row = jnp.where(ids_row_ref[...] == iota((experts, count), 0), 1.0, 0.0)
     later = jnp.where(iota((count, count), 0) < iota((count, count), 1), 1.0, 0.0).astype(BF16)
     before_row = jnp.dot(onehot_row.astype(BF16), later, preferred_element_type=F32)
-    slot_row = slots_of(onehot_row, before_row, capacity_ref[...].astype(F32), depth, 0)
+    slot_row = slots_of(onehot_row, before_row, capacity_ref[...].astype(F32), place_ref[...], depth, 0)
     select = jnp.where(iota((experts * depth, count), 0) == slot_row, 1.0, 0.0).astype(BF16)
-    packed_ref[...] = jnp.dot(select, normed, preferred_element_type=F32).astype(BF16)
-
-
-def combine_kernel(mixed_ref, gate_ref, slot_ref, back_ref, out_ref):
+    packed = jnp.dot(select, normed, preferred_element_type=F32).astype(BF16)
+    packed_ref[...] = packed.reshape(packed_ref.shape)
+
+
+def combine_kernel(mixed_ref, gate_ref, slot_ref, returned_ref, handed_ref, out_ref):
     count = mixed_ref.shape[0]
-    slots = back_ref.shape[0]
-    select = jnp.where(slot_ref[...] == iota((count, slots), 1), 1.0, 0.0).astype(BF16)
-    out = jnp.dot(select, back_ref[...], preferred_element_type=F32)
+    half = returned_ref.shape[0]
+    slot = slot_ref[...]
+    near = jnp.where(slot == iota((count, half), 1), 1.0, 0.0).astype(BF16)
+    cross = jnp.where(slot == iota((count, half), 1) + half, 1.0, 0.0).astype(BF16)
+    out = jnp.dot(near, returned_ref[...], preferred_element_type=F32)
+    out = out + jnp.dot(cross, handed_ref[...], preferred_element_type=F32)
     out_ref[...] = (mixed_ref[...] + gate_ref[...] * out).astype(BF16)
 
 
-def expert_kernel(pieces, rows_ref, *refs):
-    weights, out_ref = refs[: 3 * pieces], refs[3 * pieces]
+def expert_kernel(pieces, own_ref, far_ref, *refs):
+    weights = refs[: 3 * pieces]
+    own_out_ref, far_out_ref, rows_ref, total_ref = refs[3 * pieces :]
+    size = own_ref.shape[0]
+    rows_ref[pl.ds(0, size), :] = own_ref[...]
+    rows_ref[pl.ds(size, size), :] = far_ref[...]
     rows = rows_ref[...]
-    total = None
     for piece in range(pieces):
         gate_ref, up_ref, down_ref = weights[3 * piece : 3 * piece + 3]
         gated = jnp.dot(rows, gate_ref[...], preferred_element_type=F32)
@@ -148,17 +157,18 @@
         part = lax.dot_general(
             act, down_ref[...], (((1,), (1,)), ((), ())), preferred_element_type=F32
         )
-        total = part if total is None else total + part
-    out_ref[...] = total.astype(out_ref.dtype)
-
-
-def call(kernel, out_shape, scratch=(), flops=0, moved=0):
+        total_ref[...] = part if piece == 0 else total_ref[...] + part
+    own_out_ref[...] = total_ref[pl.ds(0, size), :]
+    far_out_ref[...] = total_ref[pl.ds(size, size), :].astype(BF16)
+
+
+def call(kernel, out_shape, scratch=()):
     return pl.pallas_call(
         kernel,
         out_shape=out_shape,
         scratch_shapes=scratch,
         compiler_params=pltpu.CompilerParams(vmem_limit_bytes=40 * 1024 * 1024),
-        cost_estimate=pl.CostEstimate(flops=flops, bytes_accessed=moved, transcendentals=0),
+        cost_estimate=pl.CostEstimate(flops=0, bytes_accessed=0, transcendentals=0),
     )
 
 
@@ -181,34 +191,48 @@
     count, width = local.shape
     experts = expert_capacity.shape[0]
     depth = max(2, 2 * count // experts)
-    slots = experts * depth
     splits = lax.axis_size("blk")
     blocks = lax.axis_size("seq")
-    groups = splits // 2
-    partner = [(i, i ^ 1) for i in range(splits)]
-
-    def turned(array, step):
-        return lax.ppermute(
-            array, "blk", [(i, (i + 2 * step) % splits) for i in range(splits)]
-        )
+    pieces = splits // 2
+    chips = blocks // 2
+
+    def across(array, masks):
+        pairs = [
+            (split * blocks + block, (split ^ masks[block % 2]) * blocks + block)
+            for split in range(splits)
+            for block in range(blocks)
+        ]
+        return lax.ppermute(array, ("blk", "seq"), pairs)
+
+    row_masks = (1, 2)
+    weight_masks = [
+        [mask for mask in range(1, splits) if not mask & row_mask] for row_mask in row_masks
+    ]
+
+    def to_chip(array, apart):
+        return lax.ppermute(array, "seq", [(i, i ^ (2 * apart)) for i in range(blocks)])
+
+    def to_core(array):
+        return lax.ppermute(array, "seq", [(i, i ^ 1) for i in range(blocks)])
 
     forward = [(i, i + 1) for i in range(blocks - 1)]
     backward = [(target, source) for source, target in forward]
+    weights = [expert_gate[0], expert_up[0], expert_down[0]]
+    for masks in zip(*weight_masks, strict=True):
+        gate, up = across(weights[0], masks), across(weights[1], masks)
+        down = lax.optimization_barrier((weights[2], gate))[0]
+        weights += [gate, up, across(down, masks)]
     low = lax.ppermute(local[count - HALO :], "seq", forward)
     high = lax.ppermute(local[:HALO], "seq", backward)
-    weights = [expert_gate[0], expert_up[0], expert_down[0]]
-    for step in range(1, groups):
-        weights += [turned(expert_gate[0], step), turned(expert_up[0], step), turned(expert_down[0], step)]
-
-    probs = call(
-        probs_kernel, shape((count, HEADS * LANES), BF16), flops=2 * count * width * 512 * 4, moved=1 << 21
-    )(local, kernel_weight)
+
+    probs = call(probs_kernel, shape((count, HEADS * LANES), BF16))(local, kernel_weight)
     ids = expert_ids[0]
+    place = lax.axis_index("seq").astype(jnp.int32).reshape(1, 1)
     mixed, packed, gate, slot = call(
         functools.partial(mix_kernel, depth),
         (
             shape((count, width), F32),
-            shape((slots, width), BF16),
+            shape((2, chips, depth, width), BF16),
             shape((count, 1), F32),
             shape((count, 1), jnp.int32),
         ),
@@ -216,8 +240,6 @@
             pltpu.VMEM((FRONT + count + BLOCK, width), BF16),
             pltpu.VMEM((count, width), BF16),
         ),
-        flops=1 << 31,
-        moved=1 << 22,
     )(
         local,
         low,
@@ -227,28 +249,27 @@
         ids,
         expert_capacity[:, None],
         expert_capacity[None, :],
+        place,
         norm_gain[None, :],
         router,
     )
-    arrived = lax.all_to_all(
-        packed.reshape(experts, depth, width), "seq", split_axis=0, concat_axis=0, tiled=True
-    )
-    rows = arrived.reshape(-1, width)
-    other = lax.ppermute(rows, "blk", partner)
-    total = rows.shape[0]
-    flops = 6 * total * width * weights[0].shape[1] * groups
-    other_part = call(
-        functools.partial(expert_kernel, groups), shape((total, width), BF16), flops=flops, moved=1 << 23
-    )(other, *weights)
-    back_part = lax.ppermute(other_part, "blk", partner)
-    own_part = call(
-        functools.partial(expert_kernel, groups), shape((total, width), F32), flops=flops, moved=1 << 23
-    )(rows, *weights)
-    sent = (own_part + back_part.astype(F32)).astype(BF16).reshape(arrived.shape)
-    back = lax.all_to_all(sent, "seq", split_axis=0, concat_axis=0, tiled=True).reshape(slots, width)
-    result = call(combine_kernel, shape((count, width), BF16), flops=1 << 28, moved=1 << 22)(
-        mixed, gate, slot, back
-    )
+    crossed = to_core(packed[1])
+    both = jnp.concatenate([packed[0], crossed], axis=1)
+    size = 2 * depth
+    backs = []
+    for apart in range(chips):
+        rows = to_chip(both[apart], apart) if apart else both[apart]
+        own, other = call(
+            functools.partial(expert_kernel, pieces),
+            (shape((size, width), F32), shape((size, width), BF16)),
+            scratch=(pltpu.VMEM((2 * size, width), BF16), pltpu.VMEM((2 * size, width), F32)),
+        )(rows, across(rows, row_masks), *weights)
+        done = (own + across(other, row_masks).astype(F32)).astype(BF16)
+        backs.append(to_chip(done, apart) if apart else done)
+    back = jnp.stack(backs).reshape(chips, 2, depth, width)
+    returned = back[:, 0].reshape(chips * depth, width)
+    handed = to_core(back[:, 1].reshape(chips * depth, width))
+    result = call(combine_kernel, shape((count, width), BF16))(mixed, gate, slot, returned, handed)
     return result[None]
 
 

time: 154 us -> 90.2 us (0.59)
  waiting for transfers between devices: 83.3 us -> 39.3 us
  blocking collectives: 30.8 us -> 0 us
  starting transfers between devices: 17.5 us -> 32.3 us
  Pallas kernels: 15.9 us -> 11.9 us
    all_to_all x1 -> x0, blocking collectives: 30.8 us -> none  [on_device(): lax.all_to_all(sent, 'seq', split_axis=0, concat_axis=0, tiled=True)]
    all_to_all x1 -> x0, waiting for transfers between devices: 23 us -> none  [on_device(): lax.all_to_all(packed.reshape(experts, depth, width), 'seq', split_axis=0...]
    ppermute x5 -> x19, starting transfers between devices: 6.73 us -> 28 us  [the longest x11 14.3 us: across(): return lax.ppermute(array, ('blk', 'seq'), pairs)]
    ppermute x5 -> x19, waiting for transfers between devices: 60.3 us -> 39.3 us  [the longest x6 35.6 us: to_chip(): lax.ppermute(array, 'seq', [(i, i ^ 2 * apart) for i in range(blocks)])]
    all_to_all x1 -> x0, starting transfers between devices: 6.44 us -> none  [on_device(): lax.all_to_all(packed.reshape(experts, depth, width), 'seq', split_axis=0...]
    pallas_call x4 -> x6, Pallas kernels: 13.3 us -> 10.4 us  [the longest x4 7.83 us: on_device(): call(functools.partial(expert_kernel, pieces), (shape((size, width), F32)...]
  transfers between devices with their start and end apart: 8 -> 21, of which waited for: 4 -> 8; matrix products, arithmetic and copies ran while one was open for 1% -> 3% of each run, Pallas kernels for 4% -> 12%
where the time goes in v2:
time: 90.2 us; the launch traced here: 89.8 us
  waiting for transfers between devices  39.3 us (44%)
  starting transfers between devices  32.3 us (36%)
  Pallas kernels  11.9 us (13%)
  local copies, waits for them, and re-layouts  5.51 us (6%)
    ppermute x6, waiting for transfers between devices, to_chip(): lax.ppermute(array, 'seq', [(i, i ^ 2 * apart) for i in range(blocks)])  35.6 us
    ppermute x11, starting transfers between devices, across(): return lax.ppermute(array, ('blk', 'seq'), pairs)  14.3 us
    ppermute x6, starting transfers between devices, to_chip(): lax.ppermute(array, 'seq', [(i, i ^ 2 * apart) for i in range(blocks)])  12.4 us
    pallas_call x4, Pallas kernels, on_device(): call(functools.partial(expert_kernel, pieces), (shape((size, width), F32)...  7.83 us
    unnamed x18, local copies, waits for them, and re-layouts  4.32 us
    ppermute x1, starting transfers between devices, on_device(): low = lax.ppermute(local[count - HALO:], 'seq', forward)  3.03 us
    ppermute x2, waiting for transfers between devices, to_core(): return lax.ppermute(array, 'seq', [(i, i ^ 1) for i in range(blocks)])  1.9 us
    ppermute x11, waiting for transfers between devices, across(): return lax.ppermute(array, ('blk', 'seq'), pairs)  1.85 us
  transfers between devices with their start and end apart: 21, of which 8 were waited for; matrix products, arithmetic and copies ran while one was open for 3% of the time, Pallas kernels for 12%

profile of v2, /device:TPU:0, one launch (start us, length us, event | category | flops | bytes accessed | tf_op | source)
XLA Modules:
  0.0 89.8 jit_solution(10924836611432853133)
XLA Ops:
  0.0 3.0 %collective-permute-start.4 = (bf16[1024,512]{1,0:T(8,128)(2,1)}, bf16[1024,512]{1,0:T(8,128)(2,1)S(1)}, u32[]{:S(2)}, u32[]{:S(2)}) collective-permute-start(bf16[1024,512]{1,0:T(8,128)(2,1)} %bitcast.40), channel_id=1, source_target_pairs={{0,16},{1,9},{2,18},{3,11},{4,20},{5,13},{6,22},{7,15},{8,24},{9,1... | collective-permute-start | bytes 3145736 | tf_op jit(solution)/shard_map/ppermute | solution.py:205
  3.0 0.8 slice_bitcast_fusion.2
  3.7 1.3 %collective-permute-start.1 = (bf16[16,1024]{1,0:T(8,128)(2,1)S(1)}, bf16[16,1024]{1,0:T(8,128)(2,1)S(1)}, u32[]{:S(2)}, u32[]{:S(2)}) collective-permute-start(bf16[16,1024]{1,0:T(8,128)(2,1)S(1)} %get-tuple-element.39), channel_id=1, source_target_pairs={{1,0},{2,1},{3,2},{4,3},{5,4},{6,5},{7,6},{9,8},{10,9},{11,10},{12... | collective-permute-start | bytes 98312 | tf_op jit(solution)/shard_map/ppermute | solution.py:226
  5.0 3.0 %collective-permute-start = (bf16[16,1024]{1,0:T(8,128)(2,1)S(1)}, bf16[16,1024]{1,0:T(8,128)(2,1)S(1)}, u32[]{:S(2)}, u32[]{:S(2)}) collective-permute-start(bf16[16,1024]{1,0:T(8,128)(2,1)S(1)} %get-tuple-element.40), channel_id=1, source_target_pairs={{0,1},{1,2},{2,3},{3,4},{4,5},{5,6},{6,7},{8,9},{9,10},{10,11},{11... | collective-permute-start | bytes 98312 | tf_op jit(solution)/shard_map/ppermute | solution.py:225
  8.1 0.7 copy-done.7
  8.8 0.7 copy-done.5
  9.4 0.1 copy.19.capacity_ref
  9.5 0.7 copy-done.4
  10.2 0.1 copy.18.ids_ref
  10.3 0.6 copy-done.6
  10.9 0.2 copy.20.router_ref
  11.1 1.5 %copy.17.weight_ref = bf16[1024,496]{1,0:T(8,128)(2,1)S(1)} copy(bf16[1024,496]{0,1:T(8,128)(2,1)} %param.12) | data formatting | bytes 2031616 | tf_op args[3]
  12.7 1.2 %shard_map.91.probs_ref = bf16[256,512]{1,0:T(8,128)(2,1)S(1)} custom-call(bf16[256,1024]{1,0:T(8,128)(2,1)S(1)} %bitcast.55, bf16[1024,496]{1,0:T(8,128)(2,1)S(1)} %copy.17.weight_ref), custom_call_target="tpu_custom_call" | custom-call | tf_op jit(solution)/shard_map/pallas_call | solution.py:228
  13.9 1.6 %shard_map.92 = (f32[256,1024]{1,0:T(8,128)S(1)}, bf16[2,4,64,1024]{3,2,1,0:T(8,128)(2,1)S(1)}, f32[256,1]{1,0:T(8,128)S(1)}, s32[256,1]{1,0:T(8,128)S(1)}) custom-call(bf16[256,1024]{1,0:T(8,128)(2,1)S(1)} %bitcast.56, bf16[16,1024]{1,0:T(8,128)(2,1)S(1)} %collective-permute-done.low_ref, bf16[16,1024]{1,0:T(8,128)(2,1)S(1)} %collective-permute-done.1.high_ref, ...), custom_call_target="tpu_custom_call" | custom-call | tf_op jit(solution)/shard_map/pallas_call | solution.py:231
  15.5 0.1 slice_bitcast_fusion.1
  15.6 1.3 %collective-permute-start.2 = (bf16[4,64,1024]{2,1,0:T(8,128)(2,1)S(1)}, bf16[4,64,1024]{2,1,0:T(8,128)(2,1)S(1)}, u32[]{:S(2)}, u32[]{:S(2)}) collective-permute-start(bf16[4,64,1024]{2,1,0:T(8,128)(2,1)S(1)} %get-tuple-element.38), channel_id=1, source_target_pairs={{0,1},{1,0},{2,3},{3,2},{4,5},{5,4},{6,7},{7,6},{8,9},{9,8},{10,11... | collective-permute-start | bytes 1572872 | tf_op jit(solution)/shard_map/ppermute | solution.py:216
  16.9 1.1 %collective-permute-start.5 = (bf16[1024,512]{1,0:T(8,128)(2,1)S(1)}, bf16[1024,512]{1,0:T(8,128)(2,1)S(1)}, u32[]{:S(2)}, u32[]{:S(2)}) collective-permute-start(bf16[1024,512]{1,0:T(8,128)(2,1)S(1)} %bitcast.45), channel_id=1, source_target_pairs={{0,16},{1,9},{2,18},{3,11},{4,20},{5,13},{6,22},{7,15},{8,24},{9,1... | collective-permute-start | bytes 3145736 | tf_op jit(solution)/shard_map/ppermute | solution.py:205
  18.0 0.9 %collective-permute-start.6 = (bf16[1024,512]{1,0:T(8,128)(2,1)S(1)}, bf16[1024,512]{1,0:T(8,128)(2,1)S(1)}, u32[]{:S(2)}, u32[]{:S(2)}) collective-permute-start(bf16[1024,512]{1,0:T(8,128)(2,1)S(1)} %bitcast.50), channel_id=1, source_target_pairs={{0,16},{1,9},{2,18},{3,11},{4,20},{5,13},{6,22},{7,15},{8,24},{9,1... | collective-permute-start | bytes 3145736 | tf_op jit(solution)/shard_map/ppermute | solution.py:205
  18.9 0.1 fusion.3
  19.1 1.7 %collective-permute-start.8 = (bf16[128,1024]{1,0:T(8,128)(2,1)S(1)}, bf16[128,1024]{1,0:T(8,128)(2,1)S(1)}, u32[]{:S(2)}, u32[]{:S(2)}) collective-permute-start(bf16[128,1024]{1,0:T(8,128)(2,1)S(1)} %get-tuple-element.34), channel_id=1, source_target_pairs={{0,2},{1,3},{2,0},{3,1},{4,6},{5,7},{6,4},{7,5},{8,10},{9,11},{10,... | collective-permute-start | bytes 786440 | tf_op jit(solution)/shard_map/ppermute | solution.py:213
  20.7 2.5 %collective-permute-start.16 = (bf16[128,1024]{1,0:T(8,128)(2,1)S(1)}, bf16[128,1024]{1,0:T(8,128)(2,1)S(1)}, u32[]{:S(2)}, u32[]{:S(2)}) collective-permute-start(bf16[128,1024]{1,0:T(8,128)(2,1)S(1)} %get-tuple-element.35), channel_id=1, source_target_pairs={{0,6},{1,7},{2,4},{3,5},{4,2},{5,3},{6,0},{7,1},{8,14},{9,15},{10,... | collective-permute-start | bytes 786440 | tf_op jit(solution)/shard_map/ppermute | solution.py:213
  23.2 4.7 %collective-permute-done.8.own_ref = bf16[128,1024]{1,0:T(8,128)(2,1)S(1)} collective-permute-done((bf16[128,1024]{1,0:T(8,128)(2,1)S(1)}, bf16[128,1024]{1,0:T(8,128)(2,1)S(1)}, u32[]{:S(2)}, u32[]{:S(2)}) %collective-permute-start.8) | collective-permute-done | bytes 262176 | tf_op jit(solution)/shard_map/ppermute | solution.py:213
  27.9 1.5 %collective-permute-start.9 = (bf16[128,1024]{1,0:T(8,128)(2,1)S(1)}, bf16[128,1024]{1,0:T(8,128)(2,1)S(1)}, u32[]{:S(2)}, u32[]{:S(2)}) collective-permute-start(bf16[128,1024]{1,0:T(8,128)(2,1)S(1)} %collective-permute-done.8.own_ref), channel_id=1, source_target_pairs={{0,8},{1,17},{2,10},{3,19},{4,12},{5,21},{6,14},{7,23},{8,0},{9,25... | collective-permute-start | bytes 786440 | tf_op jit(solution)/shard_map/ppermute | solution.py:205
  29.4 6.5 %collective-permute-done.16.own_ref = bf16[128,1024]{1,0:T(8,128)(2,1)S(1)} collective-permute-done((bf16[128,1024]{1,0:T(8,128)(2,1)S(1)}, bf16[128,1024]{1,0:T(8,128)(2,1)S(1)}, u32[]{:S(2)}, u32[]{:S(2)}) %collective-permute-start.16) | collective-permute-done | bytes 262176 | tf_op jit(solution)/shard_map/ppermute | solution.py:213
  36.0 1.5 %collective-permute-start.17 = (bf16[128,1024]{1,0:T(8,128)(2,1)S(1)}, bf16[128,1024]{1,0:T(8,128)(2,1)S(1)}, u32[]{:S(2)}, u32[]{:S(2)}) collective-permute-start(bf16[128,1024]{1,0:T(8,128)(2,1)S(1)} %collective-permute-done.16.own_ref), channel_id=1, source_target_pairs={{0,8},{1,17},{2,10},{3,19},{4,12},{5,21},{6,14},{7,23},{8,0},{9,25... | collective-permute-start | bytes 786440 | tf_op jit(solution)/shard_map/ppermute | solution.py:205
  37.5 8.4 %collective-permute-done.12.own_ref = bf16[128,1024]{1,0:T(8,128)(2,1)S(1)} collective-permute-done((bf16[128,1024]{1,0:T(8,128)(2,1)S(1)}, bf16[128,1024]{1,0:T(8,128)(2,1)S(1)}, u32[]{:S(2)}, u32[]{:S(2)}) %collective-permute-start.12) | collective-permute-done | bytes 262176 | tf_op jit(solution)/shard_map/ppermute | solution.py:213
  45.9 1.4 %collective-permute-start.13 = (bf16[128,1024]{1,0:T(8,128)(2,1)S(1)}, bf16[128,1024]{1,0:T(8,128)(2,1)S(1)}, u32[]{:S(2)}, u32[]{:S(2)}) collective-permute-start(bf16[128,1024]{1,0:T(8,128)(2,1)S(1)} %collective-permute-done.12.own_ref), channel_id=1, source_target_pairs={{0,8},{1,17},{2,10},{3,19},{4,12},{5,21},{6,14},{7,23},{8,0},{9,25... | collective-permute-start | bytes 786440 | tf_op jit(solution)/shard_map/ppermute | solution.py:205
  47.3 0.6 collective-permute-start.3
  47.9 1.8 %collective-permute-done.6.refs_5_ = bf16[1024,512]{1,0:T(8,128)(2,1)S(1)} collective-permute-done((bf16[1024,512]{1,0:T(8,128)(2,1)S(1)}, bf16[1024,512]{1,0:T(8,128)(2,1)S(1)}, u32[]{:S(2)}, u32[]{:S(2)}) %collective-permute-start.6) | collective-permute-done | bytes 1048608 | tf_op jit(solution)/shard_map/ppermute | solution.py:205
  49.7 2.0 %shard_map.94 = (f32[128,1024]{1,0:T(8,128)S(1)}, bf16[128,1024]{1,0:T(8,128)(2,1)S(1)}) custom-call(bf16[128,1024]{1,0:T(8,128)(2,1)S(1)} %collective-permute-done.8.own_ref, bf16[128,1024]{1,0:T(8,128)(2,1)S(1)} %collective-permute-done.9.far_ref, bf16[1024,512]{1,0:T(8,128)(2,1)S(1)} %bitcast.41, bf16[1024,512]{1,0:T(8,128)(2,1)S(1)} %bitcast.46, ...), custom_call_target="tpu_custom_call" | custom-call | tf_op jit(solution)/shard_map/pallas_call | solution.py:262
  51.7 1.7 %collective-permute-start.10 = (bf16[128,1024]{1,0:T(8,128)(2,1)S(1)}, bf16[128,1024]{1,0:T(8,128)(2,1)S(1)}, u32[]{:S(2)}, u32[]{:S(2)}) collective-permute-start(bf16[128,1024]{1,0:T(8,128)(2,1)S(1)} %get-tuple-element.26), channel_id=1, source_target_pairs={{0,8},{1,17},{2,10},{3,19},{4,12},{5,21},{6,14},{7,23},{8,0},{9,25... | collective-permute-start | bytes 786440 | tf_op jit(solution)/shard_map/ppermute | solution.py:205
  53.4 2.0 %shard_map.96 = (f32[128,1024]{1,0:T(8,128)S(1)}, bf16[128,1024]{1,0:T(8,128)(2,1)S(1)}) custom-call(bf16[128,1024]{1,0:T(8,128)(2,1)S(1)} %collective-permute-done.16.own_ref, bf16[128,1024]{1,0:T(8,128)(2,1)S(1)} %collective-permute-done.17.far_ref, bf16[1024,512]{1,0:T(8,128)(2,1)S(1)} %bitcast.42, bf16[1024,512]{1,0:T(8,128)(2,1)S(1)} %bitcast.47, ...), custom_call_target="tpu_custom_call" | custom-call | tf_op jit(solution)/shard_map/pallas_call | solution.py:262
  55.4 0.5 collective-permute-start.18
  55.8 2.0 %shard_map.95 = (f32[128,1024]{1,0:T(8,128)S(1)}, bf16[128,1024]{1,0:T(8,128)(2,1)S(1)}) custom-call(bf16[128,1024]{1,0:T(8,128)(2,1)S(1)} %collective-permute-done.12.own_ref, bf16[128,1024]{1,0:T(8,128)(2,1)S(1)} %collective-permute-done.13.far_ref, bf16[1024,512]{1,0:T(8,128)(2,1)S(1)} %bitcast.43, bf16[1024,512]{1,0:T(8,128)(2,1)S(1)} %bitcast.48, ...), custom_call_target="tpu_custom_call" | custom-call | tf_op jit(solution)/shard_map/pallas_call | solution.py:262
  57.8 1.7 %collective-permute-start.14 = (bf16[128,1024]{1,0:T(8,128)(2,1)S(1)}, bf16[128,1024]{1,0:T(8,128)(2,1)S(1)}, u32[]{:S(2)}, u32[]{:S(2)}) collective-permute-start(bf16[128,1024]{1,0:T(8,128)(2,1)S(1)} %get-tuple-element.28), channel_id=1, source_target_pairs={{0,8},{1,17},{2,10},{3,19},{4,12},{5,21},{6,14},{7,23},{8,0},{9,25... | collective-permute-start | bytes 786440 | tf_op jit(solution)/shard_map/ppermute | solution.py:205
  59.5 2.0 %shard_map.93 = (f32[128,1024]{1,0:T(8,128)S(1)}, bf16[128,1024]{1,0:T(8,128)(2,1)S(1)}) custom-call(bf16[128,1024]{1,0:T(8,128)(2,1)S(1)} %get-tuple-element.33.own_ref, bf16[128,1024]{1,0:T(8,128)(2,1)S(1)} %collective-permute-done.3.far_ref, bf16[1024,512]{1,0:T(8,128)(2,1)S(1)} %bitcast.44, bf16[1024,512]{1,0:T(8,128)(2,1)S(1)} %bitcast.49, ...), custom_call_target="tpu_custom_call" | custom-call | tf_op jit(solution)/shard_map/pallas_call | solution.py:262
  61.5 0.5 collective-permute-start.7
  62.0 4.2 %collective-permute-start.11 = (bf16[128,1024]{1,0:T(8,128)(2,1)S(1)}, bf16[128,1024]{1,0:T(8,128)(2,1)S(1)}, u32[]{:S(2)}, u32[]{:S(2)}) collective-permute-start(bf16[128,1024]{1,0:T(8,128)(2,1)S(1)} %add_convert_fusion.2), channel_id=1, source_target_pairs={{0,2},{1,3},{2,0},{3,1},{4,6},{5,7},{6,4},{7,5},{8,10},{9,11},{10,... | collective-permute-start | bytes 786440 | tf_op jit(solution)/shard_map/ppermute | solution.py:213
  66.3 3.0 %collective-permute-start.19 = (bf16[128,1024]{1,0:T(8,128)(2,1)S(1)}, bf16[128,1024]{1,0:T(8,128)(2,1)S(1)}, u32[]{:S(2)}, u32[]{:S(2)}) collective-permute-start(bf16[128,1024]{1,0:T(8,128)(2,1)S(1)} %add_convert_fusion), channel_id=1, source_target_pairs={{0,6},{1,7},{2,4},{3,5},{4,2},{5,3},{6,0},{7,1},{8,14},{9,15},{10,... | collective-permute-start | bytes 786440 | tf_op jit(solution)/shard_map/ppermute | solution.py:213
  69.4 1.0 %collective-permute-start.15 = (bf16[128,1024]{1,0:T(8,128)(2,1)S(1)}, bf16[128,1024]{1,0:T(8,128)(2,1)S(1)}, u32[]{:S(2)}, u32[]{:S(2)}) collective-permute-start(bf16[128,1024]{1,0:T(8,128)(2,1)S(1)} %add_convert_fusion.1), channel_id=1, source_target_pairs={{0,4},{1,5},{2,6},{3,7},{4,0},{5,1},{6,2},{7,3},{8,12},{9,13},{10,... | collective-permute-start | bytes 786440 | tf_op jit(solution)/shard_map/ppermute | solution.py:213
  70.4 1.6 %collective-permute-done.11 = bf16[128,1024]{1,0:T(8,128)(2,1)S(1)} collective-permute-done((bf16[128,1024]{1,0:T(8,128)(2,1)S(1)}, bf16[128,1024]{1,0:T(8,128)(2,1)S(1)}, u32[]{:S(2)}, u32[]{:S(2)}) %collective-permute-start.11) | collective-permute-done | bytes 262176 | tf_op jit(solution)/shard_map/ppermute | solution.py:213
  72.0 5.1 %collective-permute-done.19 = bf16[128,1024]{1,0:T(8,128)(2,1)S(1)} collective-permute-done((bf16[128,1024]{1,0:T(8,128)(2,1)S(1)}, bf16[128,1024]{1,0:T(8,128)(2,1)S(1)}, u32[]{:S(2)}, u32[]{:S(2)}) %collective-permute-start.19) | collective-permute-done | bytes 262176 | tf_op jit(solution)/shard_map/ppermute | solution.py:213
  77.1 9.2 %collective-permute-done.15 = bf16[128,1024]{1,0:T(8,128)(2,1)S(1)} collective-permute-done((bf16[128,1024]{1,0:T(8,128)(2,1)S(1)}, bf16[128,1024]{1,0:T(8,128)(2,1)S(1)}, u32[]{:S(2)}, u32[]{:S(2)}) %collective-permute-start.15) | collective-permute-done | bytes 262176 | tf_op jit(solution)/shard_map/ppermute | solution.py:213
  86.3 0.1 pad_maximum_fusion
  86.4 0.1 fusion.7
  86.5 0.1 collective-permute-start.20
  86.6 1.9 %collective-permute-done.20.handed_ref = bf16[256,1024]{1,0:T(8,128)(2,1)S(1)} collective-permute-done((bf16[256,1024]{1,0:T(8,128)(2,1)S(1)}, bf16[256,1024]{1,0:T(8,128)(2,1)S(1)}, u32[]{:S(2)}, u32[]{:S(2)}) %collective-permute-start.20) | collective-permute-done | bytes 524320 | tf_op jit(solution)/shard_map/ppermute | solution.py:216
  88.5 1.3 %shard_map.97 = bf16[256,1024]{1,0:T(8,128)(2,1)} custom-call(f32[256,1024]{1,0:T(8,128)S(1)} %get-tuple-element.18.mixed_ref, f32[256,1]{1,0:T(8,128)S(1)} %get-tuple-element.19.gate_ref, s32[256,1]{1,0:T(8,128)S(1)} %get-tuple-element.20.slot_ref, bf16[256,1024]{1,0:T(8,128)(2,1)S(1)} %bitcast.57, bf16[256,1024]{1,0:T(8,128)(2,1)S(1)} %collective-permute-done.20.handed_ref), custom_call_target="tpu_custom_call" | custom-call | tf_op jit(solution)/shard_map/pallas_call | solution.py:272
  (31 shorter events, 0.3 us)
Async XLA Ops:
  0.0 18.0 %collective-permute-start.4 = (bf16[1024,512]{1,0:T(8,128)(2,1)}, bf16[1024,512]{1,0:T(8,128)(2,1)S(1)}, u32[]{:S(2)}, u32[]{:S(2)}) collective-permute-start(bf16[1024,512]{1,0:T(8,128)(2,1)} %bitcast.40), channel_id=1, source_target_pairs={{0,16},{1,9},{2,18},{3,11},{4,20},{5,13},{6,22},{7,15},{8,24},{9,1... | collective-permute-start | bytes 3145736 | tf_op jit(solution)/shard_map/ppermute | solution.py:205
  3.7 10.2 %collective-permute-start.1 = (bf16[16,1024]{1,0:T(8,128)(2,1)S(1)}, bf16[16,1024]{1,0:T(8,128)(2,1)S(1)}, u32[]{:S(2)}, u32[]{:S(2)}) collective-permute-start(bf16[16,1024]{1,0:T(8,128)(2,1)S(1)} %get-tuple-element.39), channel_id=1, source_target_pairs={{1,0},{2,1},{3,2},{4,3},{5,4},{6,5},{7,6},{9,8},{10,9},{11,10},{12... | collective-permute-start | bytes 98312 | tf_op jit(solution)/shard_map/ppermute | solution.py:226
  5.0 8.9 %collective-permute-start = (bf16[16,1024]{1,0:T(8,128)(2,1)S(1)}, bf16[16,1024]{1,0:T(8,128)(2,1)S(1)}, u32[]{:S(2)}, u32[]{:S(2)}) collective-permute-start(bf16[16,1024]{1,0:T(8,128)(2,1)S(1)} %get-tuple-element.40), channel_id=1, source_target_pairs={{0,1},{1,2},{2,3},{3,4},{4,5},{5,6},{6,7},{8,9},{9,10},{10,11},{11... | collective-permute-start | bytes 98312 | tf_op jit(solution)/shard_map/ppermute | solution.py:225
  8.1 0.7 copy-start.7
  8.8 0.7 copy-start.5
  9.5 0.7 copy-start.4
  10.2 0.7 copy-start.6
  11.1 1.6 %copy-start.3 = (bf16[1,256,1024]{2,1,0:T(8,128)(2,1)S(1)}, bf16[1,256,1024]{2,1,0:T(8,128)(2,1)}, u32[]{:S(2)}) copy-start(bf16[1,256,1024]{2,1,0:T(8,128)(2,1)} %param.9) | copy-start | bytes 1572868
  15.5 1.4 %copy-start.1 = (bf16[1,1024,512]{2,1,0:T(8,128)(2,1)S(1)}, bf16[1,1024,512]{2,1,0:T(8,128)(2,1)}, u32[]{:S(2)}) copy-start(bf16[1,1024,512]{2,1,0:T(8,128)(2,1)} %param.16) | copy-start | bytes 3145732
  15.5 2.5 %copy-start.2 = (bf16[1,1024,512]{2,1,0:T(8,128)(2,1)S(1)}, bf16[1,1024,512]{2,1,0:T(8,128)(2,1)}, u32[]{:S(2)}) copy-start(bf16[1,1024,512]{2,1,0:T(8,128)(2,1)} %param.17) | copy-start | bytes 3145732
  15.6 3.3 %collective-permute-start.2 = (bf16[4,64,1024]{2,1,0:T(8,128)(2,1)S(1)}, bf16[4,64,1024]{2,1,0:T(8,128)(2,1)S(1)}, u32[]{:S(2)}, u32[]{:S(2)}) collective-permute-start(bf16[4,64,1024]{2,1,0:T(8,128)(2,1)S(1)} %get-tuple-element.38), channel_id=1, source_target_pairs={{0,1},{1,0},{2,3},{3,2},{4,5},{5,4},{6,7},{7,6},{8,9},{9,8},{10,11... | collective-permute-start | bytes 1572872 | tf_op jit(solution)/shard_map/ppermute | solution.py:216
  16.9 30.4 %collective-permute-start.5 = (bf16[1024,512]{1,0:T(8,128)(2,1)S(1)}, bf16[1024,512]{1,0:T(8,128)(2,1)S(1)}, u32[]{:S(2)}, u32[]{:S(2)}) collective-permute-start(bf16[1024,512]{1,0:T(8,128)(2,1)S(1)} %bitcast.45), channel_id=1, source_target_pairs={{0,16},{1,9},{2,18},{3,11},{4,20},{5,13},{6,22},{7,15},{8,24},{9,1... | collective-permute-start | bytes 3145736 | tf_op jit(solution)/shard_map/ppermute | solution.py:205
  18.0 31.7 %collective-permute-start.6 = (bf16[1024,512]{1,0:T(8,128)(2,1)S(1)}, bf16[1024,512]{1,0:T(8,128)(2,1)S(1)}, u32[]{:S(2)}, u32[]{:S(2)}) collective-permute-start(bf16[1024,512]{1,0:T(8,128)(2,1)S(1)} %bitcast.50), channel_id=1, source_target_pairs={{0,16},{1,9},{2,18},{3,11},{4,20},{5,13},{6,22},{7,15},{8,24},{9,1... | collective-permute-start | bytes 3145736 | tf_op jit(solution)/shard_map/ppermute | solution.py:205
  18.9 30.8 %copy-start = (bf16[1,1024,512]{2,1,0:T(8,128)(2,1)S(1)}, bf16[1,1024,512]{2,1,0:T(8,128)(2,1)}, u32[]{:S(2)}) copy-start(bf16[1,1024,512]{2,1,0:T(8,128)(2,1)} %param.15) | copy-start | bytes 3145732
  19.1 8.9 %collective-permute-start.8 = (bf16[128,1024]{1,0:T(8,128)(2,1)S(1)}, bf16[128,1024]{1,0:T(8,128)(2,1)S(1)}, u32[]{:S(2)}, u32[]{:S(2)}) collective-permute-start(bf16[128,1024]{1,0:T(8,128)(2,1)S(1)} %get-tuple-element.34), channel_id=1, source_target_pairs={{0,2},{1,3},{2,0},{3,1},{4,6},{5,7},{6,4},{7,5},{8,10},{9,11},{10,... | collective-permute-start | bytes 786440 | tf_op jit(solution)/shard_map/ppermute | solution.py:213
  20.7 15.3 %collective-permute-start.16 = (bf16[128,1024]{1,0:T(8,128)(2,1)S(1)}, bf16[128,1024]{1,0:T(8,128)(2,1)S(1)}, u32[]{:S(2)}, u32[]{:S(2)}) collective-permute-start(bf16[128,1024]{1,0:T(8,128)(2,1)S(1)} %get-tuple-element.35), channel_id=1, source_target_pairs={{0,6},{1,7},{2,4},{3,5},{4,2},{5,3},{6,0},{7,1},{8,14},{9,15},{10,... | collective-permute-start | bytes 786440 | tf_op jit(solution)/shard_map/ppermute | solution.py:213
  23.2 22.7 %collective-permute-start.12 = (bf16[128,1024]{1,0:T(8,128)(2,1)S(1)}, bf16[128,1024]{1,0:T(8,128)(2,1)S(1)}, u32[]{:S(2)}, u32[]{:S(2)}) collective-permute-start(bf16[128,1024]{1,0:T(8,128)(2,1)S(1)} %get-tuple-element.36), channel_id=1, source_target_pairs={{0,4},{1,5},{2,6},{3,7},{4,0},{5,1},{6,2},{7,3},{8,12},{9,13},{10,... | collective-permute-start | bytes 786440 | tf_op jit(solution)/shard_map/ppermute | solution.py:213
  27.9 20.0 %collective-permute-start.9 = (bf16[128,1024]{1,0:T(8,128)(2,1)S(1)}, bf16[128,1024]{1,0:T(8,128)(2,1)S(1)}, u32[]{:S(2)}, u32[]{:S(2)}) collective-permute-start(bf16[128,1024]{1,0:T(8,128)(2,1)S(1)} %collective-permute-done.8.own_ref), channel_id=1, source_target_pairs={{0,8},{1,17},{2,10},{3,19},{4,12},{5,21},{6,14},{7,23},{8,0},{9,25... | collective-permute-start | bytes 786440 | tf_op jit(solution)/shard_map/ppermute | solution.py:205
  36.0 17.4 %collective-permute-start.17 = (bf16[128,1024]{1,0:T(8,128)(2,1)S(1)}, bf16[128,1024]{1,0:T(8,128)(2,1)S(1)}, u32[]{:S(2)}, u32[]{:S(2)}) collective-permute-start(bf16[128,1024]{1,0:T(8,128)(2,1)S(1)} %collective-permute-done.16.own_ref), channel_id=1, source_target_pairs={{0,8},{1,17},{2,10},{3,19},{4,12},{5,21},{6,14},{7,23},{8,0},{9,25... | collective-permute-start | bytes 786440 | tf_op jit(solution)/shard_map/ppermute | solution.py:205
  45.9 10.0 %collective-permute-start.13 = (bf16[128,1024]{1,0:T(8,128)(2,1)S(1)}, bf16[128,1024]{1,0:T(8,128)(2,1)S(1)}, u32[]{:S(2)}, u32[]{:S(2)}) collective-permute-start(bf16[128,1024]{1,0:T(8,128)(2,1)S(1)} %collective-permute-done.12.own_ref), channel_id=1, source_target_pairs={{0,8},{1,17},{2,10},{3,19},{4,12},{5,21},{6,14},{7,23},{8,0},{9,25... | collective-permute-start | bytes 786440 | tf_op jit(solution)/shard_map/ppermute | solution.py:205
  47.3 12.2 %collective-permute-start.3 = (bf16[128,1024]{1,0:T(8,128)(2,1)S(1)}, bf16[128,1024]{1,0:T(8,128)(2,1)S(1)}, u32[]{:S(2)}, u32[]{:S(2)}) collective-permute-start(bf16[128,1024]{1,0:T(8,128)(2,1)S(1)} %get-tuple-element.33.own_ref), channel_id=1, source_target_pairs={{0,8},{1,17},{2,10},{3,19},{4,12},{5,21},{6,14},{7,23},{8,0},{9,25... | collective-permute-start | bytes 786440 | tf_op jit(solution)/shard_map/ppermute | solution.py:205
  51.7 10.2 %collective-permute-start.10 = (bf16[128,1024]{1,0:T(8,128)(2,1)S(1)}, bf16[128,1024]{1,0:T(8,128)(2,1)S(1)}, u32[]{:S(2)}, u32[]{:S(2)}) collective-permute-start(bf16[128,1024]{1,0:T(8,128)(2,1)S(1)} %get-tuple-element.26), channel_id=1, source_target_pairs={{0,8},{1,17},{2,10},{3,19},{4,12},{5,21},{6,14},{7,23},{8,0},{9,25... | collective-permute-start | bytes 786440 | tf_op jit(solution)/shard_map/ppermute | solution.py:205
  55.4 10.9 %collective-permute-start.18 = (bf16[128,1024]{1,0:T(8,128)(2,1)S(1)}, bf16[128,1024]{1,0:T(8,128)(2,1)S(1)}, u32[]{:S(2)}, u32[]{:S(2)}) collective-permute-start(bf16[128,1024]{1,0:T(8,128)(2,1)S(1)} %get-tuple-element.30), channel_id=1, source_target_pairs={{0,8},{1,17},{2,10},{3,19},{4,12},{5,21},{6,14},{7,23},{8,0},{9,25... | collective-permute-start | bytes 786440 | tf_op jit(solution)/shard_map/ppermute | solution.py:205
  57.8 11.5 %collective-permute-start.14 = (bf16[128,1024]{1,0:T(8,128)(2,1)S(1)}, bf16[128,1024]{1,0:T(8,128)(2,1)S(1)}, u32[]{:S(2)}, u32[]{:S(2)}) collective-permute-start(bf16[128,1024]{1,0:T(8,128)(2,1)S(1)} %get-tuple-element.28), channel_id=1, source_target_pairs={{0,8},{1,17},{2,10},{3,19},{4,12},{5,21},{6,14},{7,23},{8,0},{9,25... | collective-permute-start | bytes 786440 | tf_op jit(solution)/shard_map/ppermute | solution.py:205
  61.5 8.9 %collective-permute-start.7 = (bf16[128,1024]{1,0:T(8,128)(2,1)S(1)}, bf16[128,1024]{1,0:T(8,128)(2,1)S(1)}, u32[]{:S(2)}, u32[]{:S(2)}) collective-permute-start(bf16[128,1024]{1,0:T(8,128)(2,1)S(1)} %get-tuple-element.24), channel_id=1, source_target_pairs={{0,8},{1,17},{2,10},{3,19},{4,12},{5,21},{6,14},{7,23},{8,0},{9,25... | collective-permute-start | bytes 786440 | tf_op jit(solution)/shard_map/ppermute | solution.py:205
  62.0 10.1 %collective-permute-start.11 = (bf16[128,1024]{1,0:T(8,128)(2,1)S(1)}, bf16[128,1024]{1,0:T(8,128)(2,1)S(1)}, u32[]{:S(2)}, u32[]{:S(2)}) collective-permute-start(bf16[128,1024]{1,0:T(8,128)(2,1)S(1)} %add_convert_fusion.2), channel_id=1, source_target_pairs={{0,2},{1,3},{2,0},{3,1},{4,6},{5,7},{6,4},{7,5},{8,10},{9,11},{10,... | collective-permute-start | bytes 786440 | tf_op jit(solution)/shard_map/ppermute | solution.py:213
  66.3 10.8 %collective-permute-start.19 = (bf16[128,1024]{1,0:T(8,128)(2,1)S(1)}, bf16[128,1024]{1,0:T(8,128)(2,1)S(1)}, u32[]{:S(2)}, u32[]{:S(2)}) collective-permute-start(bf16[128,1024]{1,0:T(8,128)(2,1)S(1)} %add_convert_fusion), channel_id=1, source_target_pairs={{0,6},{1,7},{2,4},{3,5},{4,2},{5,3},{6,0},{7,1},{8,14},{9,15},{10,... | collective-permute-start | bytes 786440 | tf_op jit(solution)/shard_map/ppermute | solution.py:213
  69.4 17.0 %collective-permute-start.15 = (bf16[128,1024]{1,0:T(8,128)(2,1)S(1)}, bf16[128,1024]{1,0:T(8,128)(2,1)S(1)}, u32[]{:S(2)}, u32[]{:S(2)}) collective-permute-start(bf16[128,1024]{1,0:T(8,128)(2,1)S(1)} %add_convert_fusion.1), channel_id=1, source_target_pairs={{0,4},{1,5},{2,6},{3,7},{4,0},{5,1},{6,2},{7,3},{8,12},{9,13},{10,... | collective-permute-start | bytes 786440 | tf_op jit(solution)/shard_map/ppermute | solution.py:213
  86.5 2.0 %collective-permute-start.20 = (bf16[256,1024]{1,0:T(8,128)(2,1)S(1)}, bf16[256,1024]{1,0:T(8,128)(2,1)S(1)}, u32[]{:S(2)}, u32[]{:S(2)}) collective-permute-start(bf16[256,1024]{1,0:T(8,128)(2,1)S(1)} %bitcast.63), channel_id=1, source_target_pairs={{0,1},{1,0},{2,3},{3,2},{4,5},{5,4},{6,7},{7,6},{8,9},{9,8},{10,11... | collective-permute-start | bytes 1572872 | tf_op jit(solution)/shard_map/ppermute | solution.py:216

commit v3 on v2

v3 whole, which is shorter than its diff:
```python
import functools

import jax
import jax.numpy as jnp
from jax import lax
from jax.experimental import pallas as pl
from jax.experimental.pallas import tpu as pltpu
from jax.sharding import PartitionSpec as P

HEADS = 16
TAPS = 31
LANES = 32
HALO = 16
FRONT = 96
BLOCK = 128
EPS = 1e-06

VMEM = pl.BlockSpec(memory_space=pltpu.VMEM)
HBM = pl.BlockSpec(memory_space=pl.ANY)
F32 = jnp.float32
BF16 = jnp.bfloat16


def iota(shape, dim):
    return lax.broadcasted_iota(jnp.int32, shape, dim)


def probs_kernel(
    depth,
    tokens_ref,
    weight_ref,
    ids_ref,
    place_ref,
    capacity_hbm,
    gain_hbm,
    router_hbm,
    probs_ref,
    onehot_ref,
    slot_ref,
    slot_row_ref,
    gain_ref,
    router_ref,
    capacity_ref,
    sems,
):
    copies = [
        pltpu.make_async_copy(source, target, sems.at[index])
        for index, (source, target) in enumerate(
            ((capacity_hbm, capacity_ref), (gain_hbm, gain_ref), (router_hbm, router_ref))
        )
    ]
    for copy in copies:
        copy.start()
    count = tokens_ref.shape[0]
    columns = weight_ref.shape[0]
    row = iota((HEADS * LANES, columns), 0)
    column = iota((HEADS * LANES, columns), 1)
    tap = row % LANES
    spread = jnp.where((row // LANES * TAPS + tap == column) & (tap < TAPS), 1.0, 0.0).astype(BF16)
    weight = jnp.dot(spread, weight_ref[...], preferred_element_type=F32).astype(BF16)
    logits = lax.dot_general(
        weight, tokens_ref[...], (((1,), (1,)), ((), ())), preferred_element_type=F32
    )
    logits = logits.reshape(HEADS, LANES, count)
    logits = jnp.where(iota(logits.shape, 1) < TAPS, logits, -3e38)
    top = jnp.max(logits, axis=1, keepdims=True)
    powers = jnp.exp(logits - top)
    probs = powers / jnp.sum(powers, axis=1, keepdims=True)
    probs_ref[...] = probs.reshape(HEADS * LANES, count).T.astype(BF16)

    for copy in copies:
        copy.wait()
    experts = router_ref.shape[0]
    expert = iota((experts, count), 0)
    onehot = jnp.where(ids_ref[...] == expert, 1.0, 0.0)
    later = jnp.where(iota((count, count), 0) < iota((count, count), 1), 1.0, 0.0).astype(BF16)
    before = jnp.dot(onehot.astype(BF16), later, preferred_element_type=F32)
    capacity = jnp.zeros((experts, count), jnp.int32)
    for index in range(experts):
        capacity = jnp.where(expert == index, capacity_ref[index], capacity)
    kept = jnp.sum(onehot * (before < capacity.astype(F32)).astype(F32), axis=0, keepdims=True)
    apart = expert ^ place_ref[0]
    first = ((apart >> 1) + (apart & 1) * (experts // 2)) * depth
    slot = jnp.sum(onehot * (first.astype(F32) + before), axis=0, keepdims=True)
    slot = jnp.where(kept > 0.5, slot, -1.0)
    slot_row_ref[...] = slot.astype(jnp.int32)
    slot_ref[...] = jnp.broadcast_to(slot, (8, count)).T.astype(jnp.int32)
    onehot_ref[...] = onehot.T


def mix_kernel(
    tokens_ref,
    low_ref,
    high_ref,
    probs_ref,
    onehot_ref,
    slot_row_ref,
    gain_ref,
    router_ref,
    mixed_ref,
    packed_ref,
    gate_ref,
    padded_ref,
    normed_ref,
):
    count, width = tokens_ref.shape
    padded_ref[pl.ds(0, FRONT), :] = jnp.zeros((FRONT, width), BF16)
    padded_ref[pl.ds(FRONT, HALO), :] = low_ref[...]
    padded_ref[pl.ds(FRONT + HALO, count), :] = tokens_ref[...]
    padded_ref[pl.ds(FRONT + HALO + count, HALO), :] = high_ref[...]
    after = FRONT + 2 * HALO + count
    padded_ref[pl.ds(after, padded_ref.shape[0] - after), :] = jnp.zeros(
        (padded_ref.shape[0] - after, width), BF16
    )
    offset = iota((BLOCK, 2 * BLOCK), 1) - iota((BLOCK, 2 * BLOCK), 0) - 1
    squares = []
    for block in range(count // BLOCK):
        rows = pl.ds(block * BLOCK, BLOCK)
        square = jnp.zeros((BLOCK, 128), F32)
        for group in range(HEADS // 4):
            taps = probs_ref[rows, pl.ds(group * 128, 128)].astype(F32)
            taps = jnp.concatenate([taps, jnp.zeros((BLOCK, BLOCK), F32)], axis=1)
            band = pltpu.roll(taps, 1, 1, stride=1, stride_axis=0)
            for pair in range(2):
                lanes = pl.ds((group * 2 + pair) * 128, 128)
                halves = []
                for head in (2 * pair, 2 * pair + 1):
                    mine = (offset >= head * LANES) & (offset < (head + 1) * LANES)
                    own = jnp.where(mine, band, 0.0).astype(BF16)
                    start = FRONT + block * BLOCK - LANES * head
                    halves.append(
                        jnp.dot(
                            own,
                            padded_ref[pl.ds(start, 2 * BLOCK), lanes],
                            preferred_element_type=F32,
                        )
                    )
                left = iota((BLOCK, 128), 1) < 64
                mixed = tokens_ref[rows, lanes].astype(F32) + jnp.where(left, halves[0], halves[1])
                mixed_ref[rows, lanes] = mixed
                square = square + mixed * mixed
        squares.append(square)
    gain = gain_ref[...].astype(F32)
    for block in range(count // BLOCK):
        rows = pl.ds(block * BLOCK, BLOCK)
        mean = jnp.sum(squares[block], axis=1, keepdims=True) / width
        scale = lax.rsqrt(mean + EPS)
        normed_ref[rows, :] = (mixed_ref[rows, :] * scale * gain).astype(BF16)

    normed = normed_ref[...]
    slots = packed_ref.shape[0] * packed_ref.shape[1] * packed_ref.shape[2]
    select = jnp.where(iota((slots, count), 0) == slot_row_ref[...], 1.0, 0.0).astype(BF16)
    packed = jnp.dot(select, normed, preferred_element_type=F32).astype(BF16)
    packed_ref[...] = packed.reshape(packed_ref.shape)
    gates = lax.dot_general(
        normed, router_ref[...], (((1,), (1,)), ((), ())), preferred_element_type=F32
    )
    gate_ref[...] = jax.nn.sigmoid(jnp.sum(gates * onehot_ref[...], axis=1, keepdims=True))


def combine_kernel(mixed_ref, gate_ref, slot_ref, returned_ref, handed_ref, out_ref):
    count = mixed_ref.shape[0]
    half = returned_ref.shape[0]
    slot = slot_ref[:, :1]
    near = jnp.where(slot == iota((count, half), 1), 1.0, 0.0).astype(BF16)
    cross = jnp.where(slot == iota((count, half), 1) + half, 1.0, 0.0).astype(BF16)
    out = jnp.dot(near, returned_ref[...], preferred_element_type=F32)
    out = out + jnp.dot(cross, handed_ref[...], preferred_element_type=F32)
    out_ref[...] = (mixed_ref[...] + gate_ref[...] * out).astype(BF16)


def act_kernel(pieces, groups, *refs):
    rows_refs, weights = refs[: 2 * groups], refs[2 * groups : 2 * groups + 2 * pieces]
    acts, rows_ref = refs[2 * groups + 2 * pieces : -1], refs[-1]
    size = rows_refs[0].shape[0]
    for index, ref in enumerate(rows_refs):
        rows_ref[pl.ds(index * size, size), :] = ref[...]
    rows = rows_ref[...]
    for piece in range(pieces):
        gate_ref, up_ref = weights[2 * piece : 2 * piece + 2]
        gated = jnp.dot(rows, gate_ref[...], preferred_element_type=F32)
        lifted = jnp.dot(rows, up_ref[...], preferred_element_type=F32)
        acts[piece][...] = (gated / (1.0 + jnp.exp(-gated)) * lifted).astype(BF16)


def down_kernel(pieces, first, *refs):
    acts, downs, (own_ref, far_ref) = refs[:pieces], refs[pieces : 2 * pieces], refs[2 * pieces :]
    size = own_ref.shape[0]
    total = None
    for act_ref, down_ref in zip(acts, downs, strict=True):
        part = lax.dot_general(
            act_ref[pl.ds(first, 2 * size), :],
            down_ref[...],
            (((1,), (1,)), ((), ())),
            preferred_element_type=F32,
        )
        total = part if total is None else total + part
    own_ref[...] = total[:size]
    far_ref[...] = total[size:].astype(BF16)


def add_kernel(own_ref, other_ref, out_ref):
    out_ref[...] = (own_ref[...] + other_ref[...].astype(F32)).astype(BF16)


def split_kernel(back_ref, returned_ref, handed_ref):
    half = returned_ref.shape[0]
    returned_ref[...] = back_ref[pl.ds(0, half), :]
    handed_ref[...] = back_ref[pl.ds(half, half), :]


ADD_COST = 8 << 20
SPLIT_COST = 8 << 20


def call(kernel, out_shape, scratch=(), in_specs=None, cost=0):
    extra = {} if in_specs is None else {"in_specs": in_specs}
    return pl.pallas_call(
        kernel,
        out_shape=out_shape,
        scratch_shapes=scratch,
        **extra,
        compiler_params=pltpu.CompilerParams(vmem_limit_bytes=24 * 1024 * 1024),
        cost_estimate=pl.CostEstimate(flops=0, bytes_accessed=cost, transcendentals=0),
    )


def shape(dims, dtype):
    return jax.ShapeDtypeStruct(dims, dtype)


def on_device(
    tokens,
    expert_ids,
    expert_capacity,
    kernel_weight,
    norm_gain,
    router,
    expert_gate,
    expert_up,
    expert_down,
):
    local = tokens[0]
    count, width = local.shape
    experts = expert_capacity.shape[0]
    depth = max(2, 2 * count // experts)
    splits = lax.axis_size("blk")
    blocks = lax.axis_size("seq")
    pieces = splits // 2
    chips = blocks // 2

    def across(array, masks):
        pairs = [
            (split * blocks + block, (split ^ masks[block % 2]) * blocks + block)
            for split in range(splits)
            for block in range(blocks)
        ]
        return lax.ppermute(array, ("blk", "seq"), pairs)

    def after(array, earlier):
        return lax.optimization_barrier((array, earlier))[0]

    row_masks = (1, 2)
    weight_masks = [
        [mask for mask in range(1, splits) if not mask & row_mask] for row_mask in row_masks
    ]

    def to_chip(array, apart):
        return lax.ppermute(array, "seq", [(i, i ^ (2 * apart)) for i in range(blocks)])

    def to_core(array):
        return lax.ppermute(array, "seq", [(i, i ^ 1) for i in range(blocks)])

    forward = [(i, i + 1) for i in range(blocks - 1)]
    backward = [(target, source) for source, target in forward]
    inner, downs = [expert_gate[0], expert_up[0]], [expert_down[0]]
    for masks in zip(*weight_masks, strict=True):
        inner += [across(array, masks) for array in inner[:2]]
        downs.append(across(after(downs[0], inner[-2]), masks))
    low = lax.ppermute(local[count - HALO :], "seq", forward)
    high = lax.ppermute(local[:HALO], "seq", backward)

    place = lax.axis_index("seq").astype(jnp.int32).reshape(1)
    probs, onehot, slot, slot_row, gain, columns = call(
        functools.partial(probs_kernel, depth),
        (
            shape((count, HEADS * LANES), BF16),
            shape((count, experts), F32),
            shape((count, 8), jnp.int32),
            shape((1, count), jnp.int32),
            shape((1, width), BF16),
            shape((experts, width), BF16),
        ),
        scratch=(pltpu.SMEM((experts,), jnp.int32), pltpu.SemaphoreType.DMA((3,))),
        in_specs=[VMEM, VMEM, VMEM, pl.BlockSpec(memory_space=pltpu.SMEM), HBM, HBM, HBM],
    )(
        local,
        kernel_weight.T,
        expert_ids[0].reshape(1, count),
        place,
        expert_capacity,
        norm_gain[None, :],
        router.T,
    )
    mixed, packed, gate = call(
        mix_kernel,
        (
            shape((count, width), F32),
            shape((2, chips, depth, width), BF16),
            shape((count, 1), F32),
        ),
        scratch=(
            pltpu.VMEM((FRONT + count + BLOCK, width), BF16),
            pltpu.VMEM((count, width), BF16),
        ),
    )(local, low, high, probs, onehot, slot_row, gain, columns)
    crossed = to_core(packed[1])
    both = jnp.concatenate([packed[0], crossed], axis=1)
    size = 2 * depth
    near = list(range(chips // 2))
    order = [apart for apart in reversed(range(chips)) if apart not in near]
    hidden = inner[0].shape[1]
    rows, sums = [None] * chips, [None] * chips

    def arrive(apart, earlier):
        array = both[apart] if earlier is None else after(both[apart], earlier)
        rows[apart] = to_chip(array, apart) if apart else array

    def work(apart, earlier, behind=None):
        if earlier is not None:
            rows[apart] = after(rows[apart], earlier)
        far = across(rows[apart], row_masks)
        own = rows[apart] if behind is None else after(rows[apart], behind)
        acts = call(
            functools.partial(act_kernel, pieces, 1),
            [shape((2 * size, hidden), BF16)] * pieces,
            scratch=(pltpu.VMEM((2 * size, width), BF16),),
        )(own, far, *inner)
        sums[apart] = call(
            functools.partial(down_kernel, pieces, 0),
            (shape((size, width), F32), shape((size, width), BF16)),
        )(*acts, *downs)

    returned, handed = [None] * chips, [None] * chips

    def finish(apart, earlier=None, cost=0):
        own, other = sums[apart]
        done = call(add_kernel, shape((size, width), BF16), cost=cost)(own, across(other, row_masks))
        sent = done if earlier is None else after(done, earlier)
        back = to_chip(sent, apart) if apart else sent
        returned[apart], handed[apart] = call(
            split_kernel, [shape((depth, width), BF16)] * 2, cost=SPLIT_COST
        )(back)
        return done

    for index, apart in enumerate(order):
        arrive(apart, rows[order[index - 1]] if index else None)
        if index == 0:
            work(apart, None)
            first = finish(apart, None, ADD_COST)
        else:
            work(apart, sums[order[index - 1]][1], first)
            finish(apart, returned[order[index - 1]])
    for apart in near:
        arrive(apart, None)
        work(apart, sums[order[0]][1])
        finish(apart)
    returned = jnp.concatenate(returned)
    handed = to_core(jnp.concatenate(handed))
    result = call(combine_kernel, shape((count, width), BF16))(mixed, gate, slot, returned, handed)
    return result[None]


def solution(mesh):
    placed = (
        P("blk", "seq", None),
        P("blk", "seq", None),
        P(),
        P(),
        P(),
        P(),
        P("seq", None, "blk"),
        P("seq", None, "blk"),
        P("seq", None, "blk"),
    )
    return jax.shard_map(
        on_device, mesh=mesh, in_specs=placed, out_specs=P("blk", "seq", None), check_vma=False
    )
```

time: 90.2 us -> 82.5 us (0.915)
  waiting for transfers between devices: 39.3 us -> 26.5 us
  starting transfers between devices: 32.3 us -> 38.8 us
  local copies, waits for them, and re-layouts: 5.51 us -> 3.8 us
    ppermute x6, waiting for transfers between devices: 35.6 us -> 13.4 us  [to_chip(): lax.ppermute(array, 'seq', [(i, i ^ 2 * apart) for i in range(blocks)])]
    ppermute x11, waiting for transfers between devices: 1.85 us -> 11.3 us  [across(): return lax.ppermute(array, ('blk', 'seq'), pairs)]
    ppermute x6, starting transfers between devices: 12.4 us -> 18.5 us  [to_chip(): lax.ppermute(array, 'seq', [(i, i ^ 2 * apart) for i in range(blocks)])]
    ppermute x2, starting transfers between devices: 1.34 us -> 2.93 us  [to_core(): return lax.ppermute(array, 'seq', [(i, i ^ 1) for i in range(blocks)])]
    ppermute x1, starting transfers between devices: 3.03 us -> 1.55 us  [on_device(): low = lax.ppermute(local[count - HALO:], 'seq', forward)]
    unnamed x18, local copies, waits for them, and re-layouts: 4.32 us -> 2.94 us
    pallas_call x6 -> x18, Pallas kernels: 10.6 us -> 11.3 us  [the longest x4 5.03 us: work(): call(functools.partial(act_kernel, pieces, 1), [shape((2 * size, hidden),...]
  transfers between devices with their start and end apart: 21 -> 21, of which waited for: 8 -> 9; matrix products, arithmetic and copies ran while one was open for 3% -> 1% of each run, Pallas kernels for 12% -> 14%
where the time goes in v3:
time: 82.5 us; the launch traced here: 82.2 us
  starting transfers between devices  38.8 us (47%)
  waiting for transfers between devices  26.5 us (32%)
  Pallas kernels  12.6 us (15%)
  local copies, waits for them, and re-layouts  3.8 us (5%)
    ppermute x6, starting transfers between devices, to_chip(): lax.ppermute(array, 'seq', [(i, i ^ 2 * apart) for i in range(blocks)])  18.5 us
    ppermute x11, starting transfers between devices, across(): return lax.ppermute(array, ('blk', 'seq'), pairs)  14.5 us
    ppermute x6, waiting for transfers between devices, to_chip(): lax.ppermute(array, 'seq', [(i, i ^ 2 * apart) for i in range(blocks)])  13.4 us
    ppermute x11, waiting for transfers between devices, across(): return lax.ppermute(array, ('blk', 'seq'), pairs)  11.3 us
    pallas_call x4, Pallas kernels, work(): call(functools.partial(act_kernel, pieces, 1), [shape((2 * size, hidden),...  5.03 us
    pallas_call x4, Pallas kernels, work(): call(functools.partial(down_kernel, pieces, 0), (shape((size, width), F32...  2.95 us
    unnamed x18, local copies, waits for them, and re-layouts  2.94 us
    ppermute x2, starting transfers between devices, to_core(): return lax.ppermute(array, 'seq', [(i, i ^ 1) for i in range(blocks)])  2.93 us
  transfers between devices with their start and end apart: 21, of which 9 were waited for; matrix products, arithmetic and copies ran while one was open for 1% of the time, Pallas kernels for 14%

profile of v3, /device:TPU:0, one launch (start us, length us, event | category | flops | bytes accessed | tf_op | source)
XLA Modules:
  0.0 82.2 jit_solution(176134070831407046)
XLA Ops:
  0.0 3.0 %collective-permute-start.5 = (bf16[1024,512]{1,0:T(8,128)(2,1)}, bf16[1024,512]{1,0:T(8,128)(2,1)S(1)}, u32[]{:S(2)}, u32[]{:S(2)}) collective-permute-start(bf16[1024,512]{1,0:T(8,128)(2,1)} %bitcast.30), channel_id=1, source_target_pairs={{0,16},{1,9},{2,18},{3,11},{4,20},{5,13},{6,22},{7,15},{8,24},{9,1... | collective-permute-start | bytes 3145736 | tf_op jit(solution)/shard_map/ppermute | solution.py:258
  3.0 0.8 slice_bitcast_fusion.2
  3.8 1.6 %collective-permute-start = (bf16[16,1024]{1,0:T(8,128)(2,1)S(1)}, bf16[16,1024]{1,0:T(8,128)(2,1)S(1)}, u32[]{:S(2)}, u32[]{:S(2)}) collective-permute-start(bf16[16,1024]{1,0:T(8,128)(2,1)S(1)} %get-tuple-element.92), channel_id=1, source_target_pairs={{0,1},{1,2},{2,3},{3,4},{4,5},{5,6},{6,7},{8,9},{9,10},{10,11},{11... | collective-permute-start | bytes 98312 | tf_op jit(solution)/shard_map/ppermute | solution.py:280
  5.3 1.3 %collective-permute-start.1 = (bf16[16,1024]{1,0:T(8,128)(2,1)S(1)}, bf16[16,1024]{1,0:T(8,128)(2,1)S(1)}, u32[]{:S(2)}, u32[]{:S(2)}) collective-permute-start(bf16[16,1024]{1,0:T(8,128)(2,1)S(1)} %get-tuple-element.91), channel_id=1, source_target_pairs={{1,0},{2,1},{3,2},{4,3},{5,4},{6,5},{7,6},{9,8},{10,9},{11,10},{12... | collective-permute-start | bytes 98312 | tf_op jit(solution)/shard_map/ppermute | solution.py:281
  6.7 0.6 copy-done.6
  7.3 1.0 %copy-done.3 = bf16[1,256,1024]{2,1,0:T(8,128)(2,1)S(1)} copy-done((bf16[1,256,1024]{2,1,0:T(8,128)(2,1)S(1)}, bf16[1,256,1024]{2,1,0:T(8,128)(2,1)}, u32[]{:S(2)}) %copy-start.3) | copy-done | bytes 524312
  8.4 1.2 %copy-done.4 = bf16[1024,496]{0,1:T(8,128)(2,1)S(1)} copy-done((bf16[1024,496]{0,1:T(8,128)(2,1)S(1)}, bf16[1024,496]{0,1:T(8,128)(2,1)}, u32[]{:S(2)}) %copy-start.4) | copy-done | bytes 1015832
  9.6 1.5 %shard_map.91 = (bf16[256,512]{1,0:T(8,128)(2,1)S(1)}, f32[256,8]{1,0:T(8,128)S(1)}, s32[256,8]{1,0:T(8,128)S(1)}, s32[1,256]{1,0:T(1,128)S(1)}, bf16[1,1024]{1,...) custom-call(bf16[256,1024]{1,0:T(8,128)(2,1)S(1)} %bitcast.40, bf16[496,1024]{1,0:T(8,128)(2,1)S(1)} %bitcast.42, ...), custom_call_target="tpu_custom_call" | custom-call | tf_op jit(solution)/shard_map/pallas_call | solution.py:284
  11.2 1.5 %shard_map.92 = (f32[256,1024]{1,0:T(8,128)S(1)}, bf16[2,4,64,1024]{3,2,1,0:T(8,128)(2,1)S(1)}, f32[256,1]{1,0:T(8,128)S(1)}) custom-call(bf16[256,1024]{1,0:T(8,128)(2,1)S(1)} %bitcast.41, bf16[16,1024]{1,0:T(8,128)(2,1)S(1)} %collective-permute-done.low_ref, bf16[16,1024]{1,0:T(8,128)(2,1)S(1)} %collective-permute-done.1.high_ref, ...), custom_call_target="tpu_custom_call" | custom-call | tf_op jit(solution)/shard_map/pallas_call | solution.py:305
  12.7 0.0 copy-start.2
  12.7 0.0 copy-start
  12.7 0.1 slice_bitcast_fusion
  12.8 2.9 %collective-permute-start.2 = (bf16[4,64,1024]{2,1,0:T(8,128)(2,1)S(1)}, bf16[4,64,1024]{2,1,0:T(8,128)(2,1)S(1)}, u32[]{:S(2)}, u32[]{:S(2)}) collective-permute-start(bf16[4,64,1024]{2,1,0:T(8,128)(2,1)S(1)} %get-tuple-element.89), channel_id=1, source_target_pairs={{0,1},{1,0},{2,3},{3,2},{4,5},{5,4},{6,7},{7,6},{8,9},{9,8},{10,11... | collective-permute-start | bytes 1572872 | tf_op jit(solution)/shard_map/ppermute | solution.py:272
  15.7 0.5 collective-permute-start.6
  16.2 1.8 %collective-permute-start.7 = (bf16[1024,512]{1,0:T(8,128)(2,1)S(1)}, bf16[1024,512]{1,0:T(8,128)(2,1)S(1)}, u32[]{:S(2)}, u32[]{:S(2)}) collective-permute-start(bf16[1024,512]{1,0:T(8,128)(2,1)S(1)} %bitcast.25), channel_id=1, source_target_pairs={{0,16},{1,9},{2,18},{3,11},{4,20},{5,13},{6,22},{7,15},{8,24},{9,1... | collective-permute-start | bytes 3145736 | tf_op jit(solution)/shard_map/ppermute | solution.py:258
  18.0 0.1 fusion.3
  18.1 4.5 %collective-permute-start.3 = (bf16[128,1024]{1,0:T(8,128)(2,1)S(1)}, bf16[128,1024]{1,0:T(8,128)(2,1)S(1)}, u32[]{:S(2)}, u32[]{:S(2)}) collective-permute-start(bf16[128,1024]{1,0:T(8,128)(2,1)S(1)} %get-tuple-element.86), channel_id=1, source_target_pairs={{0,6},{1,7},{2,4},{3,5},{4,2},{5,3},{6,0},{7,1},{8,14},{9,15},{10,... | collective-permute-start | bytes 786440 | tf_op jit(solution)/shard_map/ppermute | solution.py:269
  22.5 6.0 %collective-permute-done.3.refs_0_ = bf16[128,1024]{1,0:T(8,128)(2,1)S(1)} collective-permute-done((bf16[128,1024]{1,0:T(8,128)(2,1)S(1)}, bf16[128,1024]{1,0:T(8,128)(2,1)S(1)}, u32[]{:S(2)}, u32[]{:S(2)}) %collective-permute-start.3) | collective-permute-done | bytes 262176 | tf_op jit(solution)/shard_map/ppermute | solution.py:269
  28.5 1.4 %collective-permute-start.4 = (bf16[128,1024]{1,0:T(8,128)(2,1)S(1)}, bf16[128,1024]{1,0:T(8,128)(2,1)S(1)}, u32[]{:S(2)}, u32[]{:S(2)}) collective-permute-start(bf16[128,1024]{1,0:T(8,128)(2,1)S(1)} %collective-permute-done.3.refs_0_), channel_id=1, source_target_pairs={{0,8},{1,17},{2,10},{3,19},{4,12},{5,21},{6,14},{7,23},{8,0},{9,25... | collective-permute-start | bytes 786440 | tf_op jit(solution)/shard_map/ppermute | solution.py:258
  29.9 6.3 %collective-permute-start.14 = (bf16[128,1024]{1,0:T(8,128)(2,1)S(1)}, bf16[128,1024]{1,0:T(8,128)(2,1)S(1)}, u32[]{:S(2)}, u32[]{:S(2)}) collective-permute-start(bf16[128,1024]{1,0:T(8,128)(2,1)S(1)} %get-tuple-element.70), channel_id=1, source_target_pairs={{0,4},{1,5},{2,6},{3,7},{4,0},{5,1},{6,2},{7,3},{8,12},{9,13},{10,... | collective-permute-start | bytes 786440 | tf_op jit(solution)/shard_map/ppermute | solution.py:269
  36.3 1.5 %collective-permute-done.4.refs_1_ = bf16[128,1024]{1,0:T(8,128)(2,1)S(1)} collective-permute-done((bf16[128,1024]{1,0:T(8,128)(2,1)S(1)}, bf16[128,1024]{1,0:T(8,128)(2,1)S(1)}, u32[]{:S(2)}, u32[]{:S(2)}) %collective-permute-start.4) | collective-permute-done | bytes 262176 | tf_op jit(solution)/shard_map/ppermute | solution.py:258
  37.8 1.3 %shard_map.93 = (bf16[256,512]{1,0:T(8,128)(2,1)S(1)}, bf16[256,512]{1,0:T(8,128)(2,1)S(1)}) custom-call(bf16[128,1024]{1,0:T(8,128)(2,1)S(1)} %collective-permute-done.3.refs_0_, bf16[128,1024]{1,0:T(8,128)(2,1)S(1)} %collective-permute-done.4.refs_1_, bf16[1024,512]{1,0:T(8,128)(2,1)S(1)} %bitcast.31, bf16[1024,512]{1,0:T(8,128)(2,1)S(1)} %bitcast.36, ...), custom_call_target="tpu_custom_call" | custom-call | tf_op jit(solution)/shard_map/pallas_call | solution.py:334
  39.0 5.5 %collective-permute-done.7.refs_3_ = bf16[1024,512]{1,0:T(8,128)(2,1)S(1)} collective-permute-done((bf16[1024,512]{1,0:T(8,128)(2,1)S(1)}, bf16[1024,512]{1,0:T(8,128)(2,1)S(1)}, u32[]{:S(2)}, u32[]{:S(2)}) %collective-permute-start.7) | collective-permute-done | bytes 1048608 | tf_op jit(solution)/shard_map/ppermute | solution.py:258
  44.5 0.7 shard_map.94
  45.3 1.6 %collective-permute-start.15 = (bf16[128,1024]{1,0:T(8,128)(2,1)S(1)}, bf16[128,1024]{1,0:T(8,128)(2,1)S(1)}, u32[]{:S(2)}, u32[]{:S(2)}) collective-permute-start(bf16[128,1024]{1,0:T(8,128)(2,1)S(1)} %get-tuple-element.57), channel_id=1, source_target_pairs={{0,8},{1,17},{2,10},{3,19},{4,12},{5,21},{6,14},{7,23},{8,0},{9,25... | collective-permute-start | bytes 786440 | tf_op jit(solution)/shard_map/ppermute | solution.py:258
  46.8 0.5 collective-permute-start.16
  47.4 1.5 %collective-permute-start.11 = (bf16[128,1024]{1,0:T(8,128)(2,1)S(1)}, bf16[128,1024]{1,0:T(8,128)(2,1)S(1)}, u32[]{:S(2)}, u32[]{:S(2)}) collective-permute-start(bf16[128,1024]{1,0:T(8,128)(2,1)S(1)} %collective-permute-done.10.refs_0_), channel_id=1, source_target_pairs={{0,8},{1,17},{2,10},{3,19},{4,12},{5,21},{6,14},{7,23},{8,0},{9,25... | collective-permute-start | bytes 786440 | tf_op jit(solution)/shard_map/ppermute | solution.py:258
  48.8 0.5 collective-permute-start.8
  49.4 2.3 %collective-permute-done.15.other_ref = bf16[128,1024]{1,0:T(8,128)(2,1)S(1)} collective-permute-done((bf16[128,1024]{1,0:T(8,128)(2,1)S(1)}, bf16[128,1024]{1,0:T(8,128)(2,1)S(1)}, u32[]{:S(2)}, u32[]{:S(2)}) %collective-permute-start.15) | collective-permute-done | bytes 262176 | tf_op jit(solution)/shard_map/ppermute | solution.py:258
  51.7 4.8 %collective-permute-start.18 = (bf16[128,1024]{1,0:T(8,128)(2,1)S(1)}, bf16[128,1024]{1,0:T(8,128)(2,1)S(1)}, u32[]{:S(2)}, u32[]{:S(2)}) collective-permute-start(bf16[128,1024]{1,0:T(8,128)(2,1)S(1)} %shard_map.103), channel_id=1, source_target_pairs={{0,6},{1,7},{2,4},{3,5},{4,2},{5,3},{6,0},{7,1},{8,14},{9,15},{10,... | collective-permute-start | bytes 786440 | tf_op jit(solution)/shard_map/ppermute | solution.py:269
  56.5 1.3 %shard_map.104 = (bf16[256,512]{1,0:T(8,128)(2,1)S(1)}, bf16[256,512]{1,0:T(8,128)(2,1)S(1)}) custom-call(bf16[128,1024]{1,0:T(8,128)(2,1)S(1)} %collective-permute-done.14.refs_0_, bf16[128,1024]{1,0:T(8,128)(2,1)S(1)} %collective-permute-done.16.refs_1_, bf16[1024,512]{1,0:T(8,128)(2,1)S(1)} %bitcast.32, bf16[1024,512]{1,0:T(8,128)(2,1)S(1)} %bitcast.37, ...), custom_call_target="tpu_custom_call" | custom-call | tf_op jit(solution)/shard_map/pallas_call | solution.py:334
  57.8 0.7 shard_map.105
  58.5 1.6 %collective-permute-start.17 = (bf16[128,1024]{1,0:T(8,128)(2,1)S(1)}, bf16[128,1024]{1,0:T(8,128)(2,1)S(1)}, u32[]{:S(2)}, u32[]{:S(2)}) collective-permute-start(bf16[128,1024]{1,0:T(8,128)(2,1)S(1)} %get-tuple-element.77), channel_id=1, source_target_pairs={{0,8},{1,17},{2,10},{3,19},{4,12},{5,21},{6,14},{7,23},{8,0},{9,25... | collective-permute-start | bytes 786440 | tf_op jit(solution)/shard_map/ppermute | solution.py:258
  60.1 1.3 %shard_map.99 = (bf16[256,512]{1,0:T(8,128)(2,1)S(1)}, bf16[256,512]{1,0:T(8,128)(2,1)S(1)}) custom-call(bf16[128,1024]{1,0:T(8,128)(2,1)S(1)} %collective-permute-done.10.refs_0_, bf16[128,1024]{1,0:T(8,128)(2,1)S(1)} %collective-permute-done.11.refs_1_, bf16[1024,512]{1,0:T(8,128)(2,1)S(1)} %bitcast.33, bf16[1024,512]{1,0:T(8,128)(2,1)S(1)} %bitcast.38, ...), custom_call_target="tpu_custom_call" | custom-call | tf_op jit(solution)/shard_map/pallas_call | solution.py:334
  61.4 0.7 shard_map.100
  62.1 0.6 collective-permute-start.12
  62.7 1.3 %shard_map.95 = (bf16[256,512]{1,0:T(8,128)(2,1)S(1)}, bf16[256,512]{1,0:T(8,128)(2,1)S(1)}) custom-call(bf16[128,1024]{1,0:T(8,128)(2,1)S(1)} %get-tuple-element.58.refs_0_, bf16[128,1024]{1,0:T(8,128)(2,1)S(1)} %collective-permute-done.8.refs_1_, bf16[1024,512]{1,0:T(8,128)(2,1)S(1)} %bitcast.34, bf16[1024,512]{1,0:T(8,128)(2,1)S(1)} %bitcast.39, ...), custom_call_target="tpu_custom_call" | custom-call | tf_op jit(solution)/shard_map/pallas_call | solution.py:334
  64.0 0.7 shard_map.96
  64.7 1.6 %collective-permute-start.9 = (bf16[128,1024]{1,0:T(8,128)(2,1)S(1)}, bf16[128,1024]{1,0:T(8,128)(2,1)S(1)}, u32[]{:S(2)}, u32[]{:S(2)}) collective-permute-start(bf16[128,1024]{1,0:T(8,128)(2,1)S(1)} %get-tuple-element.62), channel_id=1, source_target_pairs={{0,8},{1,17},{2,10},{3,19},{4,12},{5,21},{6,14},{7,23},{8,0},{9,25... | collective-permute-start | bytes 786440 | tf_op jit(solution)/shard_map/ppermute | solution.py:258
  66.4 1.7 %collective-permute-start.19 = (bf16[128,1024]{1,0:T(8,128)(2,1)S(1)}, bf16[128,1024]{1,0:T(8,128)(2,1)S(1)}, u32[]{:S(2)}, u32[]{:S(2)}) collective-permute-start(bf16[128,1024]{1,0:T(8,128)(2,1)S(1)} %shard_map.106), channel_id=1, source_target_pairs={{0,4},{1,5},{2,6},{3,7},{4,0},{5,1},{6,2},{7,3},{8,12},{9,13},{10,... | collective-permute-start | bytes 786440 | tf_op jit(solution)/shard_map/ppermute | solution.py:269
  68.1 0.4 collective-permute-done.12.other_ref
  68.6 1.2 %collective-permute-start.13 = (bf16[128,1024]{1,0:T(8,128)(2,1)S(1)}, bf16[128,1024]{1,0:T(8,128)(2,1)S(1)}, u32[]{:S(2)}, u32[]{:S(2)}) collective-permute-start(bf16[128,1024]{1,0:T(8,128)(2,1)S(1)} %shard_map.101), channel_id=1, source_target_pairs={{0,2},{1,3},{2,0},{3,1},{4,6},{5,7},{6,4},{7,5},{8,10},{9,11},{10,... | collective-permute-start | bytes 786440 | tf_op jit(solution)/shard_map/ppermute | solution.py:269
  69.8 1.5 %collective-permute-done.9.other_ref = bf16[128,1024]{1,0:T(8,128)(2,1)S(1)} collective-permute-done((bf16[128,1024]{1,0:T(8,128)(2,1)S(1)}, bf16[128,1024]{1,0:T(8,128)(2,1)S(1)}, u32[]{:S(2)}, u32[]{:S(2)}) %collective-permute-start.9) | collective-permute-done | bytes 262176 | tf_op jit(solution)/shard_map/ppermute | solution.py:258
  71.4 7.0 %collective-permute-done.19.back_ref = bf16[128,1024]{1,0:T(8,128)(2,1)S(1)} collective-permute-done((bf16[128,1024]{1,0:T(8,128)(2,1)S(1)}, bf16[128,1024]{1,0:T(8,128)(2,1)S(1)}, u32[]{:S(2)}, u32[]{:S(2)}) %collective-permute-start.19) | collective-permute-done | bytes 262176 | tf_op jit(solution)/shard_map/ppermute | solution.py:269
  78.5 0.4 collective-permute-done.13.back_ref
  78.9 0.1 collective-permute-start.20
  79.0 1.9 %collective-permute-done.20.handed_ref = bf16[256,1024]{1,0:T(8,128)(2,1)S(1)} collective-permute-done((bf16[256,1024]{1,0:T(8,128)(2,1)S(1)}, bf16[256,1024]{1,0:T(8,128)(2,1)S(1)}, u32[]{:S(2)}, u32[]{:S(2)}) %collective-permute-start.20) | collective-permute-done | bytes 524320 | tf_op jit(solution)/shard_map/ppermute | solution.py:272
  80.9 1.3 %shard_map.109 = bf16[256,1024]{1,0:T(8,128)(2,1)} custom-call(f32[256,1024]{1,0:T(8,128)S(1)} %get-tuple-element.50.mixed_ref, f32[256,1]{1,0:T(8,128)S(1)} %get-tuple-element.51.gate_ref, s32[256,8]{1,0:T(8,128)S(1)} %get-tuple-element.52.slot_ref, bf16[256,1024]{1,0:T(8,128)(2,1)S(1)} %pad_maximum_fusion.returned_ref, ...), custom_call_target="tpu_custom_call" | custom-call | tf_op jit(solution)/shard_map/pallas_call | solution.py:370
  (37 shorter events, 0.4 us)
Async XLA Ops:
  0.0 16.2 %collective-permute-start.5 = (bf16[1024,512]{1,0:T(8,128)(2,1)}, bf16[1024,512]{1,0:T(8,128)(2,1)S(1)}, u32[]{:S(2)}, u32[]{:S(2)}) collective-permute-start(bf16[1024,512]{1,0:T(8,128)(2,1)} %bitcast.30), channel_id=1, source_target_pairs={{0,16},{1,9},{2,18},{3,11},{4,20},{5,13},{6,22},{7,15},{8,24},{9,1... | collective-permute-start | bytes 3145736 | tf_op jit(solution)/shard_map/ppermute | solution.py:258
  3.0 3.7 %copy-start.8 = (bf16[1024]{0:T(1024)(128)(2,1)S(1)}, bf16[1024]{0:T(1024)(128)(2,1)}, u32[]{:S(2)}) copy-start(bf16[1024]{0:T(1024)(128)(2,1)} %param.13) | copy-start | bytes 6148
  3.8 2.9 %copy-start.5 = (bf16[1024,8]{0,1:T(8,128)(2,1)S(1)}, bf16[1024,8]{0,1:T(8,128)(2,1)}, u32[]{:S(2)}) copy-start(bf16[1024,8]{0,1:T(8,128)(2,1)} %param.14) | copy-start | bytes 49156
  3.8 7.4 %collective-permute-start = (bf16[16,1024]{1,0:T(8,128)(2,1)S(1)}, bf16[16,1024]{1,0:T(8,128)(2,1)S(1)}, u32[]{:S(2)}, u32[]{:S(2)}) collective-permute-start(bf16[16,1024]{1,0:T(8,128)(2,1)S(1)} %get-tuple-element.92), channel_id=1, source_target_pairs={{0,1},{1,2},{2,3},{3,4},{4,5},{5,6},{6,7},{8,9},{9,10},{10,11},{11... | collective-permute-start | bytes 98312 | tf_op jit(solution)/shard_map/ppermute | solution.py:280
  5.3 5.8 %collective-permute-start.1 = (bf16[16,1024]{1,0:T(8,128)(2,1)S(1)}, bf16[16,1024]{1,0:T(8,128)(2,1)S(1)}, u32[]{:S(2)}, u32[]{:S(2)}) collective-permute-start(bf16[16,1024]{1,0:T(8,128)(2,1)S(1)} %get-tuple-element.91), channel_id=1, source_target_pairs={{1,0},{2,1},{3,2},{4,3},{5,4},{6,5},{7,6},{9,8},{10,9},{11,10},{12... | collective-permute-start | bytes 98312 | tf_op jit(solution)/shard_map/ppermute | solution.py:281
  6.7 0.7 copy-start.6
  6.7 0.7 copy-start.7
  7.3 1.0 %copy-start.3 = (bf16[1,256,1024]{2,1,0:T(8,128)(2,1)S(1)}, bf16[1,256,1024]{2,1,0:T(8,128)(2,1)}, u32[]{:S(2)}) copy-start(bf16[1,256,1024]{2,1,0:T(8,128)(2,1)} %param.9) | copy-start | bytes 1572868
  8.4 1.2 %copy-start.4 = (bf16[1024,496]{0,1:T(8,128)(2,1)S(1)}, bf16[1024,496]{0,1:T(8,128)(2,1)}, u32[]{:S(2)}) copy-start(bf16[1024,496]{0,1:T(8,128)(2,1)} %param.12) | copy-start | bytes 3047428
  12.7 3.0 %copy-start.2 = (bf16[1,1024,512]{2,1,0:T(8,128)(2,1)S(1)}, bf16[1,1024,512]{2,1,0:T(8,128)(2,1)}, u32[]{:S(2)}) copy-start(bf16[1,1024,512]{2,1,0:T(8,128)(2,1)} %param.16) | copy-start | bytes 3145732
  12.7 3.5 %copy-start = (bf16[1,1024,512]{2,1,0:T(8,128)(2,1)S(1)}, bf16[1,1024,512]{2,1,0:T(8,128)(2,1)}, u32[]{:S(2)}) copy-start(bf16[1,1024,512]{2,1,0:T(8,128)(2,1)} %param.17) | copy-start | bytes 3145732
  12.8 5.2 %collective-permute-start.2 = (bf16[4,64,1024]{2,1,0:T(8,128)(2,1)S(1)}, bf16[4,64,1024]{2,1,0:T(8,128)(2,1)S(1)}, u32[]{:S(2)}, u32[]{:S(2)}) collective-permute-start(bf16[4,64,1024]{2,1,0:T(8,128)(2,1)S(1)} %get-tuple-element.89), channel_id=1, source_target_pairs={{0,1},{1,0},{2,3},{3,2},{4,5},{5,4},{6,7},{7,6},{8,9},{9,8},{10,11... | collective-permute-start | bytes 1572872 | tf_op jit(solution)/shard_map/ppermute | solution.py:272
  15.7 20.6 %collective-permute-start.6 = (bf16[1024,512]{1,0:T(8,128)(2,1)S(1)}, bf16[1024,512]{1,0:T(8,128)(2,1)S(1)}, u32[]{:S(2)}, u32[]{:S(2)}) collective-permute-start(bf16[1024,512]{1,0:T(8,128)(2,1)S(1)} %bitcast.35), channel_id=1, source_target_pairs={{0,16},{1,9},{2,18},{3,11},{4,20},{5,13},{6,22},{7,15},{8,24},{9,1... | collective-permute-start | bytes 3145736 | tf_op jit(solution)/shard_map/ppermute | solution.py:258
  16.2 28.3 %collective-permute-start.7 = (bf16[1024,512]{1,0:T(8,128)(2,1)S(1)}, bf16[1024,512]{1,0:T(8,128)(2,1)S(1)}, u32[]{:S(2)}, u32[]{:S(2)}) collective-permute-start(bf16[1024,512]{1,0:T(8,128)(2,1)S(1)} %bitcast.25), channel_id=1, source_target_pairs={{0,16},{1,9},{2,18},{3,11},{4,20},{5,13},{6,22},{7,15},{8,24},{9,1... | collective-permute-start | bytes 3145736 | tf_op jit(solution)/shard_map/ppermute | solution.py:258
  18.0 19.8 %copy-start.1 = (bf16[1,1024,512]{2,1,0:T(8,128)(2,1)S(1)}, bf16[1,1024,512]{2,1,0:T(8,128)(2,1)}, u32[]{:S(2)}) copy-start(bf16[1,1024,512]{2,1,0:T(8,128)(2,1)} %param.15) | copy-start | bytes 3145732
  18.1 10.4 %collective-permute-start.3 = (bf16[128,1024]{1,0:T(8,128)(2,1)S(1)}, bf16[128,1024]{1,0:T(8,128)(2,1)S(1)}, u32[]{:S(2)}, u32[]{:S(2)}) collective-permute-start(bf16[128,1024]{1,0:T(8,128)(2,1)S(1)} %get-tuple-element.86), channel_id=1, source_target_pairs={{0,6},{1,7},{2,4},{3,5},{4,2},{5,3},{6,0},{7,1},{8,14},{9,15},{10,... | collective-permute-start | bytes 786440 | tf_op jit(solution)/shard_map/ppermute | solution.py:269
  28.5 9.2 %collective-permute-start.4 = (bf16[128,1024]{1,0:T(8,128)(2,1)S(1)}, bf16[128,1024]{1,0:T(8,128)(2,1)S(1)}, u32[]{:S(2)}, u32[]{:S(2)}) collective-permute-start(bf16[128,1024]{1,0:T(8,128)(2,1)S(1)} %collective-permute-done.3.refs_0_), channel_id=1, source_target_pairs={{0,8},{1,17},{2,10},{3,19},{4,12},{5,21},{6,14},{7,23},{8,0},{9,25... | collective-permute-start | bytes 786440 | tf_op jit(solution)/shard_map/ppermute | solution.py:258
  29.9 16.9 %collective-permute-start.14 = (bf16[128,1024]{1,0:T(8,128)(2,1)S(1)}, bf16[128,1024]{1,0:T(8,128)(2,1)S(1)}, u32[]{:S(2)}, u32[]{:S(2)}) collective-permute-start(bf16[128,1024]{1,0:T(8,128)(2,1)S(1)} %get-tuple-element.70), channel_id=1, source_target_pairs={{0,4},{1,5},{2,6},{3,7},{4,0},{5,1},{6,2},{7,3},{8,12},{9,13},{10,... | collective-permute-start | bytes 786440 | tf_op jit(solution)/shard_map/ppermute | solution.py:269
  36.3 11.1 %collective-permute-start.10 = (bf16[128,1024]{1,0:T(8,128)(2,1)S(1)}, bf16[128,1024]{1,0:T(8,128)(2,1)S(1)}, u32[]{:S(2)}, u32[]{:S(2)}) collective-permute-start(bf16[128,1024]{1,0:T(8,128)(2,1)S(1)} %get-tuple-element.88), channel_id=1, source_target_pairs={{0,2},{1,3},{2,0},{3,1},{4,6},{5,7},{6,4},{7,5},{8,10},{9,11},{10,... | collective-permute-start | bytes 786440 | tf_op jit(solution)/shard_map/ppermute | solution.py:269
  45.3 6.4 %collective-permute-start.15 = (bf16[128,1024]{1,0:T(8,128)(2,1)S(1)}, bf16[128,1024]{1,0:T(8,128)(2,1)S(1)}, u32[]{:S(2)}, u32[]{:S(2)}) collective-permute-start(bf16[128,1024]{1,0:T(8,128)(2,1)S(1)} %get-tuple-element.57), channel_id=1, source_target_pairs={{0,8},{1,17},{2,10},{3,19},{4,12},{5,21},{6,14},{7,23},{8,0},{9,25... | collective-permute-start | bytes 786440 | tf_op jit(solution)/shard_map/ppermute | solution.py:258
  46.8 9.7 %collective-permute-start.16 = (bf16[128,1024]{1,0:T(8,128)(2,1)S(1)}, bf16[128,1024]{1,0:T(8,128)(2,1)S(1)}, u32[]{:S(2)}, u32[]{:S(2)}) collective-permute-start(bf16[128,1024]{1,0:T(8,128)(2,1)S(1)} %collective-permute-done.14.refs_0_), channel_id=1, source_target_pairs={{0,8},{1,17},{2,10},{3,19},{4,12},{5,21},{6,14},{7,23},{8,0},{9,25... | collective-permute-start | bytes 786440 | tf_op jit(solution)/shard_map/ppermute | solution.py:258
  47.4 12.7 %collective-permute-start.11 = (bf16[128,1024]{1,0:T(8,128)(2,1)S(1)}, bf16[128,1024]{1,0:T(8,128)(2,1)S(1)}, u32[]{:S(2)}, u32[]{:S(2)}) collective-permute-start(bf16[128,1024]{1,0:T(8,128)(2,1)S(1)} %collective-permute-done.10.refs_0_), channel_id=1, source_target_pairs={{0,8},{1,17},{2,10},{3,19},{4,12},{5,21},{6,14},{7,23},{8,0},{9,25... | collective-permute-start | bytes 786440 | tf_op jit(solution)/shard_map/ppermute | solution.py:258
  48.8 13.9 %collective-permute-start.8 = (bf16[128,1024]{1,0:T(8,128)(2,1)S(1)}, bf16[128,1024]{1,0:T(8,128)(2,1)S(1)}, u32[]{:S(2)}, u32[]{:S(2)}) collective-permute-start(bf16[128,1024]{1,0:T(8,128)(2,1)S(1)} %get-tuple-element.58.refs_0_), channel_id=1, source_target_pairs={{0,8},{1,17},{2,10},{3,19},{4,12},{5,21},{6,14},{7,23},{8,0},{9,25... | collective-permute-start | bytes 786440 | tf_op jit(solution)/shard_map/ppermute | solution.py:258
  51.7 14.5 %collective-permute-start.18 = (bf16[128,1024]{1,0:T(8,128)(2,1)S(1)}, bf16[128,1024]{1,0:T(8,128)(2,1)S(1)}, u32[]{:S(2)}, u32[]{:S(2)}) collective-permute-start(bf16[128,1024]{1,0:T(8,128)(2,1)S(1)} %shard_map.103), channel_id=1, source_target_pairs={{0,6},{1,7},{2,4},{3,5},{4,2},{5,3},{6,0},{7,1},{8,14},{9,15},{10,... | collective-permute-start | bytes 786440 | tf_op jit(solution)/shard_map/ppermute | solution.py:269
  58.5 7.8 %collective-permute-start.17 = (bf16[128,1024]{1,0:T(8,128)(2,1)S(1)}, bf16[128,1024]{1,0:T(8,128)(2,1)S(1)}, u32[]{:S(2)}, u32[]{:S(2)}) collective-permute-start(bf16[128,1024]{1,0:T(8,128)(2,1)S(1)} %get-tuple-element.77), channel_id=1, source_target_pairs={{0,8},{1,17},{2,10},{3,19},{4,12},{5,21},{6,14},{7,23},{8,0},{9,25... | collective-permute-start | bytes 786440 | tf_op jit(solution)/shard_map/ppermute | solution.py:258
  62.1 6.4 %collective-permute-start.12 = (bf16[128,1024]{1,0:T(8,128)(2,1)S(1)}, bf16[128,1024]{1,0:T(8,128)(2,1)S(1)}, u32[]{:S(2)}, u32[]{:S(2)}) collective-permute-start(bf16[128,1024]{1,0:T(8,128)(2,1)S(1)} %get-tuple-element.68), channel_id=1, source_target_pairs={{0,8},{1,17},{2,10},{3,19},{4,12},{5,21},{6,14},{7,23},{8,0},{9,25... | collective-permute-start | bytes 786440 | tf_op jit(solution)/shard_map/ppermute | solution.py:258
  64.7 6.6 %collective-permute-start.9 = (bf16[128,1024]{1,0:T(8,128)(2,1)S(1)}, bf16[128,1024]{1,0:T(8,128)(2,1)S(1)}, u32[]{:S(2)}, u32[]{:S(2)}) collective-permute-start(bf16[128,1024]{1,0:T(8,128)(2,1)S(1)} %get-tuple-element.62), channel_id=1, source_target_pairs={{0,8},{1,17},{2,10},{3,19},{4,12},{5,21},{6,14},{7,23},{8,0},{9,25... | collective-permute-start | bytes 786440 | tf_op jit(solution)/shard_map/ppermute | solution.py:258
  66.4 12.1 %collective-permute-start.19 = (bf16[128,1024]{1,0:T(8,128)(2,1)S(1)}, bf16[128,1024]{1,0:T(8,128)(2,1)S(1)}, u32[]{:S(2)}, u32[]{:S(2)}) collective-permute-start(bf16[128,1024]{1,0:T(8,128)(2,1)S(1)} %shard_map.106), channel_id=1, source_target_pairs={{0,4},{1,5},{2,6},{3,7},{4,0},{5,1},{6,2},{7,3},{8,12},{9,13},{10,... | collective-permute-start | bytes 786440 | tf_op jit(solution)/shard_map/ppermute | solution.py:269
  68.6 10.3 %collective-permute-start.13 = (bf16[128,1024]{1,0:T(8,128)(2,1)S(1)}, bf16[128,1024]{1,0:T(8,128)(2,1)S(1)}, u32[]{:S(2)}, u32[]{:S(2)}) collective-permute-start(bf16[128,1024]{1,0:T(8,128)(2,1)S(1)} %shard_map.101), channel_id=1, source_target_pairs={{0,2},{1,3},{2,0},{3,1},{4,6},{5,7},{6,4},{7,5},{8,10},{9,11},{10,... | collective-permute-start | bytes 786440 | tf_op jit(solution)/shard_map/ppermute | solution.py:269
  78.9 2.0 %collective-permute-start.20 = (bf16[256,1024]{1,0:T(8,128)(2,1)S(1)}, bf16[256,1024]{1,0:T(8,128)(2,1)S(1)}, u32[]{:S(2)}, u32[]{:S(2)}) collective-permute-start(bf16[256,1024]{1,0:T(8,128)(2,1)S(1)} %pad_maximum_fusion.1), channel_id=1, source_target_pairs={{0,1},{1,0},{2,3},{3,2},{4,5},{5,4},{6,7},{7,6},{8,9},{9,8},{10,11... | collective-permute-start | bytes 1572872 | tf_op jit(solution)/shard_map/ppermute | solution.py:272

commit v4 on v3

--- a/solution.py
+++ b/solution.py
@@ -209,11 +209,7 @@
     handed_ref[...] = back_ref[pl.ds(half, half), :]
 
 
-ADD_COST = 8 << 20
-SPLIT_COST = 8 << 20
-
-
-def call(kernel, out_shape, scratch=(), in_specs=None, cost=0):
+def call(kernel, out_shape, scratch=(), in_specs=None):
     extra = {} if in_specs is None else {"in_specs": in_specs}
     return pl.pallas_call(
         kernel,
@@ -221,7 +217,7 @@
         scratch_shapes=scratch,
         **extra,
         compiler_params=pltpu.CompilerParams(vmem_limit_bytes=24 * 1024 * 1024),
-        cost_estimate=pl.CostEstimate(flops=0, bytes_accessed=cost, transcendentals=0),
+        cost_estimate=pl.CostEstimate(flops=0, bytes_accessed=0, transcendentals=0),
     )
 
 
@@ -343,21 +339,21 @@
 
     returned, handed = [None] * chips, [None] * chips
 
-    def finish(apart, earlier=None, cost=0):
+    def finish(apart, earlier=None):
         own, other = sums[apart]
-        done = call(add_kernel, shape((size, width), BF16), cost=cost)(own, across(other, row_masks))
+        done = call(add_kernel, shape((size, width), BF16))(own, across(other, row_masks))
         sent = done if earlier is None else after(done, earlier)
         back = to_chip(sent, apart) if apart else sent
         returned[apart], handed[apart] = call(
-            split_kernel, [shape((depth, width), BF16)] * 2, cost=SPLIT_COST
+            split_kernel, [shape((depth, width), BF16)] * 2
         )(back)
         return done
 
     for index, apart in enumerate(order):
         arrive(apart, rows[order[index - 1]] if index else None)
         if index == 0:
-            work(apart, None)
-            first = finish(apart, None, ADD_COST)
+            work(apart, tuple(inner[3::2]))
+            first = finish(apart)
         else:
             work(apart, sums[order[index - 1]][1], first)
             finish(apart, returned[order[index - 1]])

time: 82.5 us -> 80.3 us (0.973)
  starting transfers between devices: 38.8 us -> 34 us
  waiting for transfers between devices: 26.5 us -> 29.1 us
    ppermute x6, starting transfers between devices: 18.5 us -> 12.6 us  [to_chip(): lax.ppermute(array, 'seq', [(i, i ^ 2 * apart) for i in range(blocks)])]
    ppermute x6, waiting for transfers between devices: 13.4 us -> 17.8 us  [to_chip(): lax.ppermute(array, 'seq', [(i, i ^ 2 * apart) for i in range(blocks)])]
    ppermute x11, waiting for transfers between devices: 11.3 us -> 9.02 us  [across(): return lax.ppermute(array, ('blk', 'seq'), pairs)]
    ppermute x11, starting transfers between devices: 14.5 us -> 15.9 us  [across(): return lax.ppermute(array, ('blk', 'seq'), pairs)]
  transfers between devices with their start and end apart: 21 -> 21, of which waited for: 9 -> 11; matrix products, arithmetic and copies ran while one was open for 1% -> 1% of each run, Pallas kernels for 14% -> 14%
where the time goes in v4:
time: 80.3 us; the launch traced here: 79.9 us
  starting transfers between devices  34 us (42%)
  waiting for transfers between devices  29.1 us (36%)
  Pallas kernels  12.6 us (16%)
  local copies, waits for them, and re-layouts  3.8 us (5%)
    ppermute x6, waiting for transfers between devices, to_chip(): lax.ppermute(array, 'seq', [(i, i ^ 2 * apart) for i in range(blocks)])  17.8 us
    ppermute x11, starting transfers between devices, across(): return lax.ppermute(array, ('blk', 'seq'), pairs)  15.9 us
    ppermute x6, starting transfers between devices, to_chip(): lax.ppermute(array, 'seq', [(i, i ^ 2 * apart) for i in range(blocks)])  12.6 us
    ppermute x11, waiting for transfers between devices, across(): return lax.ppermute(array, ('blk', 'seq'), pairs)  9.02 us
    pallas_call x4, Pallas kernels, work(): call(functools.partial(act_kernel, pieces, 1), [shape((2 * size, hidden),...  5.03 us
    pallas_call x4, Pallas kernels, work(): call(functools.partial(down_kernel, pieces, 0), (shape((size, width), F32...  2.95 us
    unnamed x18, local copies, waits for them, and re-layouts  2.93 us
    ppermute x2, starting transfers between devices, to_core(): return lax.ppermute(array, 'seq', [(i, i ^ 1) for i in range(blocks)])  2.63 us
  transfers between devices with their start and end apart: 21, of which 11 were waited for; matrix products, arithmetic and copies ran while one was open for 1% of the time, Pallas kernels for 14%

profile of v4, /device:TPU:0, one launch (start us, length us, event | category | flops | bytes accessed | tf_op | source)
XLA Modules:
  0.0 79.9 jit_solution(13741630196256887520)
XLA Ops:
  0.0 3.0 %collective-permute-start.6 = (bf16[1024,512]{1,0:T(8,128)(2,1)}, bf16[1024,512]{1,0:T(8,128)(2,1)S(1)}, u32[]{:S(2)}, u32[]{:S(2)}) collective-permute-start(bf16[1024,512]{1,0:T(8,128)(2,1)} %bitcast.30), channel_id=1, source_target_pairs={{0,16},{1,9},{2,18},{3,11},{4,20},{5,13},{6,22},{7,15},{8,24},{9,1... | collective-permute-start | bytes 3145736 | tf_op jit(solution)/shard_map/ppermute | solution.py:254
  3.0 0.8 slice_bitcast_fusion.2
  3.8 1.6 %collective-permute-start = (bf16[16,1024]{1,0:T(8,128)(2,1)S(1)}, bf16[16,1024]{1,0:T(8,128)(2,1)S(1)}, u32[]{:S(2)}, u32[]{:S(2)}) collective-permute-start(bf16[16,1024]{1,0:T(8,128)(2,1)S(1)} %get-tuple-element.94), channel_id=1, source_target_pairs={{0,1},{1,2},{2,3},{3,4},{4,5},{5,6},{6,7},{8,9},{9,10},{10,11},{11... | collective-permute-start | bytes 98312 | tf_op jit(solution)/shard_map/ppermute | solution.py:276
  5.3 1.3 %collective-permute-start.1 = (bf16[16,1024]{1,0:T(8,128)(2,1)S(1)}, bf16[16,1024]{1,0:T(8,128)(2,1)S(1)}, u32[]{:S(2)}, u32[]{:S(2)}) collective-permute-start(bf16[16,1024]{1,0:T(8,128)(2,1)S(1)} %get-tuple-element.93), channel_id=1, source_target_pairs={{1,0},{2,1},{3,2},{4,3},{5,4},{6,5},{7,6},{9,8},{10,9},{11,10},{12... | collective-permute-start | bytes 98312 | tf_op jit(solution)/shard_map/ppermute | solution.py:277
  6.6 1.6 %collective-permute-start.4 = (bf16[1024,512]{1,0:T(8,128)(2,1)}, bf16[1024,512]{1,0:T(8,128)(2,1)S(1)}, u32[]{:S(2)}, u32[]{:S(2)}) collective-permute-start(bf16[1024,512]{1,0:T(8,128)(2,1)} %bitcast.35), channel_id=1, source_target_pairs={{0,16},{1,9},{2,18},{3,11},{4,20},{5,13},{6,22},{7,15},{8,24},{9,1... | collective-permute-start | bytes 3145736 | tf_op jit(solution)/shard_map/ppermute | solution.py:254
  8.2 0.7 copy-done.6
  8.9 1.0 %copy-done.3 = bf16[1,256,1024]{2,1,0:T(8,128)(2,1)S(1)} copy-done((bf16[1,256,1024]{2,1,0:T(8,128)(2,1)S(1)}, bf16[1,256,1024]{2,1,0:T(8,128)(2,1)}, u32[]{:S(2)}) %copy-start.3) | copy-done | bytes 524312
  9.9 1.2 %copy-done.4 = bf16[1024,496]{0,1:T(8,128)(2,1)S(1)} copy-done((bf16[1024,496]{0,1:T(8,128)(2,1)S(1)}, bf16[1024,496]{0,1:T(8,128)(2,1)}, u32[]{:S(2)}) %copy-start.4) | copy-done | bytes 1015832
  11.2 1.5 %shard_map.91 = (bf16[256,512]{1,0:T(8,128)(2,1)S(1)}, f32[256,8]{1,0:T(8,128)S(1)}, s32[256,8]{1,0:T(8,128)S(1)}, s32[1,256]{1,0:T(1,128)S(1)}, bf16[1,1024]{1,...) custom-call(bf16[256,1024]{1,0:T(8,128)(2,1)S(1)} %bitcast.40, bf16[496,1024]{1,0:T(8,128)(2,1)S(1)} %bitcast.42, ...), custom_call_target="tpu_custom_call" | custom-call | tf_op jit(solution)/shard_map/pallas_call | solution.py:280
  12.7 1.5 %shard_map.92 = (f32[256,1024]{1,0:T(8,128)S(1)}, bf16[2,4,64,1024]{3,2,1,0:T(8,128)(2,1)S(1)}, f32[256,1]{1,0:T(8,128)S(1)}) custom-call(bf16[256,1024]{1,0:T(8,128)(2,1)S(1)} %bitcast.41, bf16[16,1024]{1,0:T(8,128)(2,1)S(1)} %collective-permute-done.low_ref, bf16[16,1024]{1,0:T(8,128)(2,1)S(1)} %collective-permute-done.1.high_ref, ...), custom_call_target="tpu_custom_call" | custom-call | tf_op jit(solution)/shard_map/pallas_call | solution.py:301
  14.3 0.1 slice_bitcast_fusion
  14.4 2.6 %collective-permute-start.2 = (bf16[4,64,1024]{2,1,0:T(8,128)(2,1)S(1)}, bf16[4,64,1024]{2,1,0:T(8,128)(2,1)S(1)}, u32[]{:S(2)}, u32[]{:S(2)}) collective-permute-start(bf16[4,64,1024]{2,1,0:T(8,128)(2,1)S(1)} %get-tuple-element.91), channel_id=1, source_target_pairs={{0,1},{1,0},{2,3},{3,2},{4,5},{5,4},{6,7},{7,6},{8,9},{9,8},{10,11... | collective-permute-start | bytes 1572872 | tf_op jit(solution)/shard_map/ppermute | solution.py:268
  16.9 1.1 %collective-permute-start.7 = (bf16[1024,512]{1,0:T(8,128)(2,1)S(1)}, bf16[1024,512]{1,0:T(8,128)(2,1)S(1)}, u32[]{:S(2)}, u32[]{:S(2)}) collective-permute-start(bf16[1024,512]{1,0:T(8,128)(2,1)S(1)} %bitcast.25), channel_id=1, source_target_pairs={{0,16},{1,9},{2,18},{3,11},{4,20},{5,13},{6,22},{7,15},{8,24},{9,1... | collective-permute-start | bytes 3145736 | tf_op jit(solution)/shard_map/ppermute | solution.py:254
  18.0 0.5 collective-permute-done.2
  18.4 0.1 fusion.3
  18.5 4.1 %collective-permute-start.3 = (bf16[128,1024]{1,0:T(8,128)(2,1)S(1)}, bf16[128,1024]{1,0:T(8,128)(2,1)S(1)}, u32[]{:S(2)}, u32[]{:S(2)}) collective-permute-start(bf16[128,1024]{1,0:T(8,128)(2,1)S(1)} %get-tuple-element.88), channel_id=1, source_target_pairs={{0,6},{1,7},{2,4},{3,5},{4,2},{5,3},{6,0},{7,1},{8,14},{9,15},{10,... | collective-permute-start | bytes 786440 | tf_op jit(solution)/shard_map/ppermute | solution.py:265
  22.6 6.5 %collective-permute-done.3.refs_0_ = bf16[128,1024]{1,0:T(8,128)(2,1)S(1)} collective-permute-done((bf16[128,1024]{1,0:T(8,128)(2,1)S(1)}, bf16[128,1024]{1,0:T(8,128)(2,1)S(1)}, u32[]{:S(2)}, u32[]{:S(2)}) %collective-permute-start.3) | collective-permute-done | bytes 262176 | tf_op jit(solution)/shard_map/ppermute | solution.py:265
  29.1 1.0 %collective-permute-start.5 = (bf16[128,1024]{1,0:T(8,128)(2,1)S(1)}, bf16[128,1024]{1,0:T(8,128)(2,1)S(1)}, u32[]{:S(2)}, u32[]{:S(2)}) collective-permute-start(bf16[128,1024]{1,0:T(8,128)(2,1)S(1)} %collective-permute-done.3.refs_0_), channel_id=1, source_target_pairs={{0,8},{1,17},{2,10},{3,19},{4,12},{5,21},{6,14},{7,23},{8,0},{9,25... | collective-permute-start | bytes 786440 | tf_op jit(solution)/shard_map/ppermute | solution.py:254
  30.1 6.2 %collective-permute-start.14 = (bf16[128,1024]{1,0:T(8,128)(2,1)S(1)}, bf16[128,1024]{1,0:T(8,128)(2,1)S(1)}, u32[]{:S(2)}, u32[]{:S(2)}) collective-permute-start(bf16[128,1024]{1,0:T(8,128)(2,1)S(1)} %get-tuple-element.72), channel_id=1, source_target_pairs={{0,4},{1,5},{2,6},{3,7},{4,0},{5,1},{6,2},{7,3},{8,12},{9,13},{10,... | collective-permute-start | bytes 786440 | tf_op jit(solution)/shard_map/ppermute | solution.py:265
  36.4 2.0 %collective-permute-done.5.refs_1_ = bf16[128,1024]{1,0:T(8,128)(2,1)S(1)} collective-permute-done((bf16[128,1024]{1,0:T(8,128)(2,1)S(1)}, bf16[128,1024]{1,0:T(8,128)(2,1)S(1)}, u32[]{:S(2)}, u32[]{:S(2)}) %collective-permute-start.5) | collective-permute-done | bytes 262176 | tf_op jit(solution)/shard_map/ppermute | solution.py:254
  38.3 1.3 %shard_map.93 = (bf16[256,512]{1,0:T(8,128)(2,1)S(1)}, bf16[256,512]{1,0:T(8,128)(2,1)S(1)}) custom-call(bf16[128,1024]{1,0:T(8,128)(2,1)S(1)} %collective-permute-done.3.refs_0_, bf16[128,1024]{1,0:T(8,128)(2,1)S(1)} %collective-permute-done.5.refs_1_, bf16[1024,512]{1,0:T(8,128)(2,1)S(1)} %bitcast.31, bf16[1024,512]{1,0:T(8,128)(2,1)S(1)} %bitcast.36, ...), custom_call_target="tpu_custom_call" | custom-call | tf_op jit(solution)/shard_map/pallas_call | solution.py:330
  39.6 1.6 %collective-permute-done.7.refs_3_ = bf16[1024,512]{1,0:T(8,128)(2,1)S(1)} collective-permute-done((bf16[1024,512]{1,0:T(8,128)(2,1)S(1)}, bf16[1024,512]{1,0:T(8,128)(2,1)S(1)}, u32[]{:S(2)}, u32[]{:S(2)}) %collective-permute-start.7) | collective-permute-done | bytes 1048608 | tf_op jit(solution)/shard_map/ppermute | solution.py:254
  41.2 0.7 shard_map.94
  42.0 2.1 %collective-permute-start.15 = (bf16[128,1024]{1,0:T(8,128)(2,1)S(1)}, bf16[128,1024]{1,0:T(8,128)(2,1)S(1)}, u32[]{:S(2)}, u32[]{:S(2)}) collective-permute-start(bf16[128,1024]{1,0:T(8,128)(2,1)S(1)} %get-tuple-element.59), channel_id=1, source_target_pairs={{0,8},{1,17},{2,10},{3,19},{4,12},{5,21},{6,14},{7,23},{8,0},{9,25... | collective-permute-start | bytes 786440 | tf_op jit(solution)/shard_map/ppermute | solution.py:254
  44.0 3.6 %collective-permute-done.14.refs_0_ = bf16[128,1024]{1,0:T(8,128)(2,1)S(1)} collective-permute-done((bf16[128,1024]{1,0:T(8,128)(2,1)S(1)}, bf16[128,1024]{1,0:T(8,128)(2,1)S(1)}, u32[]{:S(2)}, u32[]{:S(2)}) %collective-permute-start.14) | collective-permute-done | bytes 262176 | tf_op jit(solution)/shard_map/ppermute | solution.py:265
  47.6 1.5 %collective-permute-start.16 = (bf16[128,1024]{1,0:T(8,128)(2,1)S(1)}, bf16[128,1024]{1,0:T(8,128)(2,1)S(1)}, u32[]{:S(2)}, u32[]{:S(2)}) collective-permute-start(bf16[128,1024]{1,0:T(8,128)(2,1)S(1)} %collective-permute-done.14.refs_0_), channel_id=1, source_target_pairs={{0,8},{1,17},{2,10},{3,19},{4,12},{5,21},{6,14},{7,23},{8,0},{9,25... | collective-permute-start | bytes 786440 | tf_op jit(solution)/shard_map/ppermute | solution.py:254
  49.1 0.5 collective-permute-start.11
  49.6 1.5 %collective-permute-start.8 = (bf16[128,1024]{1,0:T(8,128)(2,1)S(1)}, bf16[128,1024]{1,0:T(8,128)(2,1)S(1)}, u32[]{:S(2)}, u32[]{:S(2)}) collective-permute-start(bf16[128,1024]{1,0:T(8,128)(2,1)S(1)} %get-tuple-element.60.refs_0_), channel_id=1, source_target_pairs={{0,8},{1,17},{2,10},{3,19},{4,12},{5,21},{6,14},{7,23},{8,0},{9,25... | collective-permute-start | bytes 786440 | tf_op jit(solution)/shard_map/ppermute | solution.py:254
  51.2 1.5 %collective-permute-start.18 = (bf16[128,1024]{1,0:T(8,128)(2,1)S(1)}, bf16[128,1024]{1,0:T(8,128)(2,1)S(1)}, u32[]{:S(2)}, u32[]{:S(2)}) collective-permute-start(bf16[128,1024]{1,0:T(8,128)(2,1)S(1)} %shard_map.103), channel_id=1, source_target_pairs={{0,6},{1,7},{2,4},{3,5},{4,2},{5,3},{6,0},{7,1},{8,14},{9,15},{10,... | collective-permute-start | bytes 786440 | tf_op jit(solution)/shard_map/ppermute | solution.py:265
  52.6 1.3 %collective-permute-done.16.refs_1_ = bf16[128,1024]{1,0:T(8,128)(2,1)S(1)} collective-permute-done((bf16[128,1024]{1,0:T(8,128)(2,1)S(1)}, bf16[128,1024]{1,0:T(8,128)(2,1)S(1)}, u32[]{:S(2)}, u32[]{:S(2)}) %collective-permute-start.16) | collective-permute-done | bytes 262176 | tf_op jit(solution)/shard_map/ppermute | solution.py:254
  54.0 1.3 %shard_map.104 = (bf16[256,512]{1,0:T(8,128)(2,1)S(1)}, bf16[256,512]{1,0:T(8,128)(2,1)S(1)}) custom-call(bf16[128,1024]{1,0:T(8,128)(2,1)S(1)} %collective-permute-done.14.refs_0_, bf16[128,1024]{1,0:T(8,128)(2,1)S(1)} %collective-permute-done.16.refs_1_, bf16[1024,512]{1,0:T(8,128)(2,1)S(1)} %bitcast.32, bf16[1024,512]{1,0:T(8,128)(2,1)S(1)} %bitcast.37, ...), custom_call_target="tpu_custom_call" | custom-call | tf_op jit(solution)/shard_map/pallas_call | solution.py:330
  55.2 0.7 shard_map.105
  56.0 1.6 %collective-permute-start.17 = (bf16[128,1024]{1,0:T(8,128)(2,1)S(1)}, bf16[128,1024]{1,0:T(8,128)(2,1)S(1)}, u32[]{:S(2)}, u32[]{:S(2)}) collective-permute-start(bf16[128,1024]{1,0:T(8,128)(2,1)S(1)} %get-tuple-element.79), channel_id=1, source_target_pairs={{0,8},{1,17},{2,10},{3,19},{4,12},{5,21},{6,14},{7,23},{8,0},{9,25... | collective-permute-start | bytes 786440 | tf_op jit(solution)/shard_map/ppermute | solution.py:254
  57.5 1.3 %shard_map.99 = (bf16[256,512]{1,0:T(8,128)(2,1)S(1)}, bf16[256,512]{1,0:T(8,128)(2,1)S(1)}) custom-call(bf16[128,1024]{1,0:T(8,128)(2,1)S(1)} %collective-permute-done.10.refs_0_, bf16[128,1024]{1,0:T(8,128)(2,1)S(1)} %collective-permute-done.11.refs_1_, bf16[1024,512]{1,0:T(8,128)(2,1)S(1)} %bitcast.33, bf16[1024,512]{1,0:T(8,128)(2,1)S(1)} %bitcast.38, ...), custom_call_target="tpu_custom_call" | custom-call | tf_op jit(solution)/shard_map/pallas_call | solution.py:330
  58.8 0.7 shard_map.100
  59.6 0.8 collective-permute-start.12
  60.4 1.3 %shard_map.95 = (bf16[256,512]{1,0:T(8,128)(2,1)S(1)}, bf16[256,512]{1,0:T(8,128)(2,1)S(1)}) custom-call(bf16[128,1024]{1,0:T(8,128)(2,1)S(1)} %get-tuple-element.60.refs_0_, bf16[128,1024]{1,0:T(8,128)(2,1)S(1)} %collective-permute-done.8.refs_1_, bf16[1024,512]{1,0:T(8,128)(2,1)S(1)} %bitcast.34, bf16[1024,512]{1,0:T(8,128)(2,1)S(1)} %bitcast.39, ...), custom_call_target="tpu_custom_call" | custom-call | tf_op jit(solution)/shard_map/pallas_call | solution.py:330
  61.6 0.7 shard_map.96
  62.4 1.4 %collective-permute-start.9 = (bf16[128,1024]{1,0:T(8,128)(2,1)S(1)}, bf16[128,1024]{1,0:T(8,128)(2,1)S(1)}, u32[]{:S(2)}, u32[]{:S(2)}) collective-permute-start(bf16[128,1024]{1,0:T(8,128)(2,1)S(1)} %get-tuple-element.64), channel_id=1, source_target_pairs={{0,8},{1,17},{2,10},{3,19},{4,12},{5,21},{6,14},{7,23},{8,0},{9,25... | collective-permute-start | bytes 786440 | tf_op jit(solution)/shard_map/ppermute | solution.py:254
  63.8 0.8 collective-permute-start.19
  64.6 1.4 %collective-permute-done.12.other_ref = bf16[128,1024]{1,0:T(8,128)(2,1)S(1)} collective-permute-done((bf16[128,1024]{1,0:T(8,128)(2,1)S(1)}, bf16[128,1024]{1,0:T(8,128)(2,1)S(1)}, u32[]{:S(2)}, u32[]{:S(2)}) %collective-permute-start.12) | collective-permute-done | bytes 262176 | tf_op jit(solution)/shard_map/ppermute | solution.py:254
  66.0 0.1 collective-permute-start.13
  66.1 2.7 %collective-permute-done.9.other_ref = bf16[128,1024]{1,0:T(8,128)(2,1)S(1)} collective-permute-done((bf16[128,1024]{1,0:T(8,128)(2,1)S(1)}, bf16[128,1024]{1,0:T(8,128)(2,1)S(1)}, u32[]{:S(2)}, u32[]{:S(2)}) %collective-permute-start.9) | collective-permute-done | bytes 262176 | tf_op jit(solution)/shard_map/ppermute | solution.py:254
  68.9 6.8 %collective-permute-done.19.back_ref = bf16[128,1024]{1,0:T(8,128)(2,1)S(1)} collective-permute-done((bf16[128,1024]{1,0:T(8,128)(2,1)S(1)}, bf16[128,1024]{1,0:T(8,128)(2,1)S(1)}, u32[]{:S(2)}, u32[]{:S(2)}) %collective-permute-start.19) | collective-permute-done | bytes 262176 | tf_op jit(solution)/shard_map/ppermute | solution.py:265
  75.7 0.9 %collective-permute-done.13.back_ref = bf16[128,1024]{1,0:T(8,128)(2,1)S(1)} collective-permute-done((bf16[128,1024]{1,0:T(8,128)(2,1)S(1)}, bf16[128,1024]{1,0:T(8,128)(2,1)S(1)}, u32[]{:S(2)}, u32[]{:S(2)}) %collective-permute-start.13) | collective-permute-done | bytes 262176 | tf_op jit(solution)/shard_map/ppermute | solution.py:265
  76.7 0.1 collective-permute-start.20
  76.8 1.9 %collective-permute-done.20.handed_ref = bf16[256,1024]{1,0:T(8,128)(2,1)S(1)} collective-permute-done((bf16[256,1024]{1,0:T(8,128)(2,1)S(1)}, bf16[256,1024]{1,0:T(8,128)(2,1)S(1)}, u32[]{:S(2)}, u32[]{:S(2)}) %collective-permute-start.20) | collective-permute-done | bytes 524320 | tf_op jit(solution)/shard_map/ppermute | solution.py:268
  78.7 1.3 %shard_map.109 = bf16[256,1024]{1,0:T(8,128)(2,1)} custom-call(f32[256,1024]{1,0:T(8,128)S(1)} %get-tuple-element.51.mixed_ref, f32[256,1]{1,0:T(8,128)S(1)} %get-tuple-element.52.gate_ref, s32[256,8]{1,0:T(8,128)S(1)} %get-tuple-element.53.slot_ref, bf16[256,1024]{1,0:T(8,128)(2,1)S(1)} %pad_maximum_fusion.returned_ref, ...), custom_call_target="tpu_custom_call" | custom-call | tf_op jit(solution)/shard_map/pallas_call | solution.py:366
  (37 shorter events, 0.4 us)
Async XLA Ops:
  0.0 16.9 %collective-permute-start.6 = (bf16[1024,512]{1,0:T(8,128)(2,1)}, bf16[1024,512]{1,0:T(8,128)(2,1)S(1)}, u32[]{:S(2)}, u32[]{:S(2)}) collective-permute-start(bf16[1024,512]{1,0:T(8,128)(2,1)} %bitcast.30), channel_id=1, source_target_pairs={{0,16},{1,9},{2,18},{3,11},{4,20},{5,13},{6,22},{7,15},{8,24},{9,1... | collective-permute-start | bytes 3145736 | tf_op jit(solution)/shard_map/ppermute | solution.py:254
  3.0 5.2 %copy-start.8 = (bf16[1024]{0:T(1024)(128)(2,1)S(1)}, bf16[1024]{0:T(1024)(128)(2,1)}, u32[]{:S(2)}) copy-start(bf16[1024]{0:T(1024)(128)(2,1)} %param.13) | copy-start | bytes 6148
  3.8 4.5 %copy-start.5 = (bf16[1024,8]{0,1:T(8,128)(2,1)S(1)}, bf16[1024,8]{0,1:T(8,128)(2,1)}, u32[]{:S(2)}) copy-start(bf16[1024,8]{0,1:T(8,128)(2,1)} %param.14) | copy-start | bytes 49156
  3.8 8.9 %collective-permute-start = (bf16[16,1024]{1,0:T(8,128)(2,1)S(1)}, bf16[16,1024]{1,0:T(8,128)(2,1)S(1)}, u32[]{:S(2)}, u32[]{:S(2)}) collective-permute-start(bf16[16,1024]{1,0:T(8,128)(2,1)S(1)} %get-tuple-element.94), channel_id=1, source_target_pairs={{0,1},{1,2},{2,3},{3,4},{4,5},{5,6},{6,7},{8,9},{9,10},{10,11},{11... | collective-permute-start | bytes 98312 | tf_op jit(solution)/shard_map/ppermute | solution.py:276
  5.3 7.4 %collective-permute-start.1 = (bf16[16,1024]{1,0:T(8,128)(2,1)S(1)}, bf16[16,1024]{1,0:T(8,128)(2,1)S(1)}, u32[]{:S(2)}, u32[]{:S(2)}) collective-permute-start(bf16[16,1024]{1,0:T(8,128)(2,1)S(1)} %get-tuple-element.93), channel_id=1, source_target_pairs={{1,0},{2,1},{3,2},{4,3},{5,4},{6,5},{7,6},{9,8},{10,9},{11,10},{12... | collective-permute-start | bytes 98312 | tf_op jit(solution)/shard_map/ppermute | solution.py:277
  6.6 22.5 %collective-permute-start.4 = (bf16[1024,512]{1,0:T(8,128)(2,1)}, bf16[1024,512]{1,0:T(8,128)(2,1)S(1)}, u32[]{:S(2)}, u32[]{:S(2)}) collective-permute-start(bf16[1024,512]{1,0:T(8,128)(2,1)} %bitcast.35), channel_id=1, source_target_pairs={{0,16},{1,9},{2,18},{3,11},{4,20},{5,13},{6,22},{7,15},{8,24},{9,1... | collective-permute-start | bytes 3145736 | tf_op jit(solution)/shard_map/ppermute | solution.py:254
  8.2 0.7 copy-start.6
  8.2 0.7 copy-start.7
  8.9 1.0 %copy-start.3 = (bf16[1,256,1024]{2,1,0:T(8,128)(2,1)S(1)}, bf16[1,256,1024]{2,1,0:T(8,128)(2,1)}, u32[]{:S(2)}) copy-start(bf16[1,256,1024]{2,1,0:T(8,128)(2,1)} %param.9) | copy-start | bytes 1572868
  9.9 1.2 %copy-start.4 = (bf16[1024,496]{0,1:T(8,128)(2,1)S(1)}, bf16[1024,496]{0,1:T(8,128)(2,1)}, u32[]{:S(2)}) copy-start(bf16[1024,496]{0,1:T(8,128)(2,1)} %param.12) | copy-start | bytes 3047428
  14.3 2.7 %copy-start = (bf16[1,1024,512]{2,1,0:T(8,128)(2,1)S(1)}, bf16[1,1024,512]{2,1,0:T(8,128)(2,1)}, u32[]{:S(2)}) copy-start(bf16[1,1024,512]{2,1,0:T(8,128)(2,1)} %param.17) | copy-start | bytes 3145732
  14.4 4.1 %collective-permute-start.2 = (bf16[4,64,1024]{2,1,0:T(8,128)(2,1)S(1)}, bf16[4,64,1024]{2,1,0:T(8,128)(2,1)S(1)}, u32[]{:S(2)}, u32[]{:S(2)}) collective-permute-start(bf16[4,64,1024]{2,1,0:T(8,128)(2,1)S(1)} %get-tuple-element.91), channel_id=1, source_target_pairs={{0,1},{1,0},{2,3},{3,2},{4,5},{5,4},{6,7},{7,6},{8,9},{9,8},{10,11... | collective-permute-start | bytes 1572872 | tf_op jit(solution)/shard_map/ppermute | solution.py:268
  16.9 24.3 %collective-permute-start.7 = (bf16[1024,512]{1,0:T(8,128)(2,1)S(1)}, bf16[1024,512]{1,0:T(8,128)(2,1)S(1)}, u32[]{:S(2)}, u32[]{:S(2)}) collective-permute-start(bf16[1024,512]{1,0:T(8,128)(2,1)S(1)} %bitcast.25), channel_id=1, source_target_pairs={{0,16},{1,9},{2,18},{3,11},{4,20},{5,13},{6,22},{7,15},{8,24},{9,1... | collective-permute-start | bytes 3145736 | tf_op jit(solution)/shard_map/ppermute | solution.py:254
  18.4 19.9 %copy-start.1 = (bf16[1,1024,512]{2,1,0:T(8,128)(2,1)S(1)}, bf16[1,1024,512]{2,1,0:T(8,128)(2,1)}, u32[]{:S(2)}) copy-start(bf16[1,1024,512]{2,1,0:T(8,128)(2,1)} %param.15) | copy-start | bytes 3145732
  18.4 19.9 %copy-start.2 = (bf16[1,1024,512]{2,1,0:T(8,128)(2,1)S(1)}, bf16[1,1024,512]{2,1,0:T(8,128)(2,1)}, u32[]{:S(2)}) copy-start(bf16[1,1024,512]{2,1,0:T(8,128)(2,1)} %param.16) | copy-start | bytes 3145732
  18.5 10.6 %collective-permute-start.3 = (bf16[128,1024]{1,0:T(8,128)(2,1)S(1)}, bf16[128,1024]{1,0:T(8,128)(2,1)S(1)}, u32[]{:S(2)}, u32[]{:S(2)}) collective-permute-start(bf16[128,1024]{1,0:T(8,128)(2,1)S(1)} %get-tuple-element.88), channel_id=1, source_target_pairs={{0,6},{1,7},{2,4},{3,5},{4,2},{5,3},{6,0},{7,1},{8,14},{9,15},{10,... | collective-permute-start | bytes 786440 | tf_op jit(solution)/shard_map/ppermute | solution.py:265
  29.1 9.2 %collective-permute-start.5 = (bf16[128,1024]{1,0:T(8,128)(2,1)S(1)}, bf16[128,1024]{1,0:T(8,128)(2,1)S(1)}, u32[]{:S(2)}, u32[]{:S(2)}) collective-permute-start(bf16[128,1024]{1,0:T(8,128)(2,1)S(1)} %collective-permute-done.3.refs_0_), channel_id=1, source_target_pairs={{0,8},{1,17},{2,10},{3,19},{4,12},{5,21},{6,14},{7,23},{8,0},{9,25... | collective-permute-start | bytes 786440 | tf_op jit(solution)/shard_map/ppermute | solution.py:254
  30.1 17.5 %collective-permute-start.14 = (bf16[128,1024]{1,0:T(8,128)(2,1)S(1)}, bf16[128,1024]{1,0:T(8,128)(2,1)S(1)}, u32[]{:S(2)}, u32[]{:S(2)}) collective-permute-start(bf16[128,1024]{1,0:T(8,128)(2,1)S(1)} %get-tuple-element.72), channel_id=1, source_target_pairs={{0,4},{1,5},{2,6},{3,7},{4,0},{5,1},{6,2},{7,3},{8,12},{9,13},{10,... | collective-permute-start | bytes 786440 | tf_op jit(solution)/shard_map/ppermute | solution.py:265
  36.3 12.7 %collective-permute-start.10 = (bf16[128,1024]{1,0:T(8,128)(2,1)S(1)}, bf16[128,1024]{1,0:T(8,128)(2,1)S(1)}, u32[]{:S(2)}, u32[]{:S(2)}) collective-permute-start(bf16[128,1024]{1,0:T(8,128)(2,1)S(1)} %get-tuple-element.90), channel_id=1, source_target_pairs={{0,2},{1,3},{2,0},{3,1},{4,6},{5,7},{6,4},{7,5},{8,10},{9,11},{10,... | collective-permute-start | bytes 786440 | tf_op jit(solution)/shard_map/ppermute | solution.py:265
  42.0 9.1 %collective-permute-start.15 = (bf16[128,1024]{1,0:T(8,128)(2,1)S(1)}, bf16[128,1024]{1,0:T(8,128)(2,1)S(1)}, u32[]{:S(2)}, u32[]{:S(2)}) collective-permute-start(bf16[128,1024]{1,0:T(8,128)(2,1)S(1)} %get-tuple-element.59), channel_id=1, source_target_pairs={{0,8},{1,17},{2,10},{3,19},{4,12},{5,21},{6,14},{7,23},{8,0},{9,25... | collective-permute-start | bytes 786440 | tf_op jit(solution)/shard_map/ppermute | solution.py:254
  47.6 6.4 %collective-permute-start.16 = (bf16[128,1024]{1,0:T(8,128)(2,1)S(1)}, bf16[128,1024]{1,0:T(8,128)(2,1)S(1)}, u32[]{:S(2)}, u32[]{:S(2)}) collective-permute-start(bf16[128,1024]{1,0:T(8,128)(2,1)S(1)} %collective-permute-done.14.refs_0_), channel_id=1, source_target_pairs={{0,8},{1,17},{2,10},{3,19},{4,12},{5,21},{6,14},{7,23},{8,0},{9,25... | collective-permute-start | bytes 786440 | tf_op jit(solution)/shard_map/ppermute | solution.py:254
  49.1 8.4 %collective-permute-start.11 = (bf16[128,1024]{1,0:T(8,128)(2,1)S(1)}, bf16[128,1024]{1,0:T(8,128)(2,1)S(1)}, u32[]{:S(2)}, u32[]{:S(2)}) collective-permute-start(bf16[128,1024]{1,0:T(8,128)(2,1)S(1)} %collective-permute-done.10.refs_0_), channel_id=1, source_target_pairs={{0,8},{1,17},{2,10},{3,19},{4,12},{5,21},{6,14},{7,23},{8,0},{9,25... | collective-permute-start | bytes 786440 | tf_op jit(solution)/shard_map/ppermute | solution.py:254
  49.6 10.7 %collective-permute-start.8 = (bf16[128,1024]{1,0:T(8,128)(2,1)S(1)}, bf16[128,1024]{1,0:T(8,128)(2,1)S(1)}, u32[]{:S(2)}, u32[]{:S(2)}) collective-permute-start(bf16[128,1024]{1,0:T(8,128)(2,1)S(1)} %get-tuple-element.60.refs_0_), channel_id=1, source_target_pairs={{0,8},{1,17},{2,10},{3,19},{4,12},{5,21},{6,14},{7,23},{8,0},{9,25... | collective-permute-start | bytes 786440 | tf_op jit(solution)/shard_map/ppermute | solution.py:254
  51.2 12.6 %collective-permute-start.18 = (bf16[128,1024]{1,0:T(8,128)(2,1)S(1)}, bf16[128,1024]{1,0:T(8,128)(2,1)S(1)}, u32[]{:S(2)}, u32[]{:S(2)}) collective-permute-start(bf16[128,1024]{1,0:T(8,128)(2,1)S(1)} %shard_map.103), channel_id=1, source_target_pairs={{0,6},{1,7},{2,4},{3,5},{4,2},{5,3},{6,0},{7,1},{8,14},{9,15},{10,... | collective-permute-start | bytes 786440 | tf_op jit(solution)/shard_map/ppermute | solution.py:265
  56.0 7.8 %collective-permute-start.17 = (bf16[128,1024]{1,0:T(8,128)(2,1)S(1)}, bf16[128,1024]{1,0:T(8,128)(2,1)S(1)}, u32[]{:S(2)}, u32[]{:S(2)}) collective-permute-start(bf16[128,1024]{1,0:T(8,128)(2,1)S(1)} %get-tuple-element.79), channel_id=1, source_target_pairs={{0,8},{1,17},{2,10},{3,19},{4,12},{5,21},{6,14},{7,23},{8,0},{9,25... | collective-permute-start | bytes 786440 | tf_op jit(solution)/shard_map/ppermute | solution.py:254
  59.6 6.4 %collective-permute-start.12 = (bf16[128,1024]{1,0:T(8,128)(2,1)S(1)}, bf16[128,1024]{1,0:T(8,128)(2,1)S(1)}, u32[]{:S(2)}, u32[]{:S(2)}) collective-permute-start(bf16[128,1024]{1,0:T(8,128)(2,1)S(1)} %get-tuple-element.70), channel_id=1, source_target_pairs={{0,8},{1,17},{2,10},{3,19},{4,12},{5,21},{6,14},{7,23},{8,0},{9,25... | collective-permute-start | bytes 786440 | tf_op jit(solution)/shard_map/ppermute | solution.py:254
  62.4 6.4 %collective-permute-start.9 = (bf16[128,1024]{1,0:T(8,128)(2,1)S(1)}, bf16[128,1024]{1,0:T(8,128)(2,1)S(1)}, u32[]{:S(2)}, u32[]{:S(2)}) collective-permute-start(bf16[128,1024]{1,0:T(8,128)(2,1)S(1)} %get-tuple-element.64), channel_id=1, source_target_pairs={{0,8},{1,17},{2,10},{3,19},{4,12},{5,21},{6,14},{7,23},{8,0},{9,25... | collective-permute-start | bytes 786440 | tf_op jit(solution)/shard_map/ppermute | solution.py:254
  63.8 11.9 %collective-permute-start.19 = (bf16[128,1024]{1,0:T(8,128)(2,1)S(1)}, bf16[128,1024]{1,0:T(8,128)(2,1)S(1)}, u32[]{:S(2)}, u32[]{:S(2)}) collective-permute-start(bf16[128,1024]{1,0:T(8,128)(2,1)S(1)} %shard_map.106), channel_id=1, source_target_pairs={{0,4},{1,5},{2,6},{3,7},{4,0},{5,1},{6,2},{7,3},{8,12},{9,13},{10,... | collective-permute-start | bytes 786440 | tf_op jit(solution)/shard_map/ppermute | solution.py:265
  66.0 10.6 %collective-permute-start.13 = (bf16[128,1024]{1,0:T(8,128)(2,1)S(1)}, bf16[128,1024]{1,0:T(8,128)(2,1)S(1)}, u32[]{:S(2)}, u32[]{:S(2)}) collective-permute-start(bf16[128,1024]{1,0:T(8,128)(2,1)S(1)} %shard_map.101), channel_id=1, source_target_pairs={{0,2},{1,3},{2,0},{3,1},{4,6},{5,7},{6,4},{7,5},{8,10},{9,11},{10,... | collective-permute-start | bytes 786440 | tf_op jit(solution)/shard_map/ppermute | solution.py:265
  76.7 2.0 %collective-permute-start.20 = (bf16[256,1024]{1,0:T(8,128)(2,1)S(1)}, bf16[256,1024]{1,0:T(8,128)(2,1)S(1)}, u32[]{:S(2)}, u32[]{:S(2)}) collective-permute-start(bf16[256,1024]{1,0:T(8,128)(2,1)S(1)} %pad_maximum_fusion.1), channel_id=1, source_target_pairs={{0,1},{1,0},{2,3},{3,2},{4,5},{5,4},{6,7},{7,6},{8,9},{9,8},{10,11... | collective-permute-start | bytes 1572872 | tf_op jit(solution)/shard_map/ppermute | solution.py:268

commit v5 on v4

--- a/solution.py
+++ b/solution.py
@@ -16,13 +16,36 @@
 EPS = 1e-06
 
 VMEM = pl.BlockSpec(memory_space=pltpu.VMEM)
-HBM = pl.BlockSpec(memory_space=pl.ANY)
+HBM = pl.BlockSpec(memory_space=pltpu.HBM)
+SMEM = pl.BlockSpec(memory_space=pltpu.SMEM)
 F32 = jnp.float32
 BF16 = jnp.bfloat16
 
 
 def iota(shape, dim):
     return lax.broadcasted_iota(jnp.int32, shape, dim)
+
+
+def fetch_kernel(place_ref, *refs):
+    count = len(refs) // 2 - 2
+    sources, targets, (near_ref, cross_ref, sems) = refs[:count], refs[count:-3], refs[-3:]
+    half = sources[-1].shape[0] // 2
+    sources = [*sources[:-1], *[sources[-1].at[pl.ds(first, half), :] for first in (0, half)]]
+    copies = [
+        pltpu.make_async_copy(source, target, sems.at[index])
+        for index, (source, target) in enumerate(zip(sources, targets, strict=True))
+    ]
+    for copy in copies:
+        copy.start()
+    copies[0].wait()
+    tokens_ref = targets[0]
+    head = tokens_ref[pl.ds(0, HALO), :]
+    tail = tokens_ref[pl.ds(tokens_ref.shape[0] - HALO, HALO), :]
+    low_core = place_ref[0] % 2 == 0
+    near_ref[...] = jnp.where(low_core, tail, head)
+    cross_ref[...] = jnp.where(low_core, head, tail)
+    for copy in copies[1:]:
+        copy.wait()
 
 
 def probs_kernel(
@@ -30,27 +53,13 @@
     tokens_ref,
     weight_ref,
     ids_ref,
+    capacity_ref,
     place_ref,
-    capacity_hbm,
-    gain_hbm,
-    router_hbm,
     probs_ref,
     onehot_ref,
     slot_ref,
     slot_row_ref,
-    gain_ref,
-    router_ref,
-    capacity_ref,
-    sems,
 ):
-    copies = [
-        pltpu.make_async_copy(source, target, sems.at[index])
-        for index, (source, target) in enumerate(
-            ((capacity_hbm, capacity_ref), (gain_hbm, gain_ref), (router_hbm, router_ref))
-        )
-    ]
-    for copy in copies:
-        copy.start()
     count = tokens_ref.shape[0]
     columns = weight_ref.shape[0]
     row = iota((HEADS * LANES, columns), 0)
@@ -68,30 +77,28 @@
     probs = powers / jnp.sum(powers, axis=1, keepdims=True)
     probs_ref[...] = probs.reshape(HEADS * LANES, count).T.astype(BF16)
 
-    for copy in copies:
-        copy.wait()
-    experts = router_ref.shape[0]
+    experts = capacity_ref.shape[1]
     expert = iota((experts, count), 0)
     onehot = jnp.where(ids_ref[...] == expert, 1.0, 0.0)
+    chosen = onehot.astype(BF16)
     later = jnp.where(iota((count, count), 0) < iota((count, count), 1), 1.0, 0.0).astype(BF16)
-    before = jnp.dot(onehot.astype(BF16), later, preferred_element_type=F32)
-    capacity = jnp.zeros((experts, count), jnp.int32)
-    for index in range(experts):
-        capacity = jnp.where(expert == index, capacity_ref[index], capacity)
-    kept = jnp.sum(onehot * (before < capacity.astype(F32)).astype(F32), axis=0, keepdims=True)
+    before = jnp.dot(chosen, later, preferred_element_type=F32)
+    rank = jnp.sum(onehot * before, axis=0, keepdims=True)
+    limit = jnp.dot(capacity_ref[...].astype(F32).astype(BF16), chosen, preferred_element_type=F32)
     apart = expert ^ place_ref[0]
     first = ((apart >> 1) + (apart & 1) * (experts // 2)) * depth
-    slot = jnp.sum(onehot * (first.astype(F32) + before), axis=0, keepdims=True)
-    slot = jnp.where(kept > 0.5, slot, -1.0)
+    slot = jnp.sum(onehot * first.astype(F32), axis=0, keepdims=True) + rank
+    slot = jnp.where(rank < limit, slot, -1.0)
     slot_row_ref[...] = slot.astype(jnp.int32)
     slot_ref[...] = jnp.broadcast_to(slot, (8, count)).T.astype(jnp.int32)
     onehot_ref[...] = onehot.T
 
 
 def mix_kernel(
+    place_ref,
     tokens_ref,
-    low_ref,
-    high_ref,
+    near_ref,
+    cross_ref,
     probs_ref,
     onehot_ref,
     slot_row_ref,
@@ -105,9 +112,11 @@
 ):
     count, width = tokens_ref.shape
     padded_ref[pl.ds(0, FRONT), :] = jnp.zeros((FRONT, width), BF16)
-    padded_ref[pl.ds(FRONT, HALO), :] = low_ref[...]
+    low_core = place_ref[0] % 2 == 0
+    near, cross = near_ref[...], cross_ref[...]
+    padded_ref[pl.ds(FRONT, HALO), :] = jnp.where(low_core, cross, near)
     padded_ref[pl.ds(FRONT + HALO, count), :] = tokens_ref[...]
-    padded_ref[pl.ds(FRONT + HALO + count, HALO), :] = high_ref[...]
+    padded_ref[pl.ds(FRONT + HALO + count, HALO), :] = jnp.where(low_core, near, cross)
     after = FRONT + 2 * HALO + count
     padded_ref[pl.ds(after, padded_ref.shape[0] - after), :] = jnp.zeros(
         (padded_ref.shape[0] - after, width), BF16
@@ -140,7 +149,7 @@
                 mixed_ref[rows, lanes] = mixed
                 square = square + mixed * mixed
         squares.append(square)
-    gain = gain_ref[...].astype(F32)
+    gain = gain_ref[...].astype(F32).reshape(1, width)
     for block in range(count // BLOCK):
         rows = pl.ds(block * BLOCK, BLOCK)
         mean = jnp.sum(squares[block], axis=1, keepdims=True) / width
@@ -183,20 +192,19 @@
         acts[piece][...] = (gated / (1.0 + jnp.exp(-gated)) * lifted).astype(BF16)
 
 
-def down_kernel(pieces, first, *refs):
-    acts, downs, (own_ref, far_ref) = refs[:pieces], refs[pieces : 2 * pieces], refs[2 * pieces :]
-    size = own_ref.shape[0]
-    total = None
-    for act_ref, down_ref in zip(acts, downs, strict=True):
-        part = lax.dot_general(
-            act_ref[pl.ds(first, 2 * size), :],
-            down_ref[...],
-            (((1,), (1,)), ((), ())),
-            preferred_element_type=F32,
-        )
-        total = part if total is None else total + part
-    own_ref[...] = total[:size]
-    far_ref[...] = total[size:].astype(BF16)
+def down_kernel(pieces, *refs):
+    acts, downs, (own_ref, far_ref) = refs[:pieces], refs[pieces : 3 * pieces], refs[3 * pieces :]
+    size, width = own_ref.shape
+    for half in range(2):
+        columns = pl.ds(half * (width // 2), width // 2)
+        total = None
+        for act_ref, down_ref in zip(acts, downs[half::2], strict=True):
+            part = lax.dot_general(
+                act_ref[...], down_ref[...], (((1,), (1,)), ((), ())), preferred_element_type=F32
+            )
+            total = part if total is None else total + part
+        own_ref[:, columns] = total[:size]
+        far_ref[:, columns] = total[size:].astype(BF16)
 
 
 def add_kernel(own_ref, other_ref, out_ref):
@@ -267,37 +275,44 @@
     def to_core(array):
         return lax.ppermute(array, "seq", [(i, i ^ 1) for i in range(blocks)])
 
-    forward = [(i, i + 1) for i in range(blocks - 1)]
-    backward = [(target, source) for source, target in forward]
-    inner, downs = [expert_gate[0], expert_up[0]], [expert_down[0]]
+    place = lax.axis_index("seq").astype(jnp.int32).reshape(1)
+    sources = [
+        local,
+        kernel_weight.T,
+        expert_ids[0].reshape(1, count),
+        expert_capacity[None, :],
+        norm_gain,
+        router.T,
+        expert_down[0],
+    ]
+    half = (width // 2, expert_down.shape[2])
+    hidden = expert_gate.shape[2]
+    local, kernel_rows, ids, capacity, gain, columns, *down, near_edge, cross_edge = call(
+        fetch_kernel,
+        [pltpu.VMEM(array.shape, array.dtype) for array in sources[:-1]]
+        + [pltpu.VMEM(half, BF16)] * 2
+        + [pltpu.VMEM((HALO, width), BF16)] * 2,
+        scratch=(pltpu.SemaphoreType.DMA((len(sources) + 1,)),),
+        in_specs=[SMEM] + [HBM] * len(sources),
+    )(place, *[pltpu.with_memory_space_constraint(array, pltpu.HBM) for array in sources])
+    inner, downs = [expert_gate[0], expert_up[0]], list(down)
     for masks in zip(*weight_masks, strict=True):
         inner += [across(array, masks) for array in inner[:2]]
-        downs.append(across(after(downs[0], inner[-2]), masks))
-    low = lax.ppermute(local[count - HALO :], "seq", forward)
-    high = lax.ppermute(local[:HALO], "seq", backward)
-
-    place = lax.axis_index("seq").astype(jnp.int32).reshape(1)
-    probs, onehot, slot, slot_row, gain, columns = call(
+        downs += [across(after(array, inner[-2]), masks) for array in down]
+    near_edge = to_core(near_edge)
+    between = [(i, i + 1) for i in range(1, blocks - 1, 2)]
+    between += [(target, source) for source, target in between]
+    cross_edge = lax.ppermute(cross_edge, "seq", between)
+    probs, onehot, slot, slot_row = call(
         functools.partial(probs_kernel, depth),
         (
             shape((count, HEADS * LANES), BF16),
             shape((count, experts), F32),
             shape((count, 8), jnp.int32),
             shape((1, count), jnp.int32),
-            shape((1, width), BF16),
-            shape((experts, width), BF16),
         ),
-        scratch=(pltpu.SMEM((experts,), jnp.int32), pltpu.SemaphoreType.DMA((3,))),
-        in_specs=[VMEM, VMEM, VMEM, pl.BlockSpec(memory_space=pltpu.SMEM), HBM, HBM, HBM],
-    )(
-        local,
-        kernel_weight.T,
-        expert_ids[0].reshape(1, count),
-        place,
-        expert_capacity,
-        norm_gain[None, :],
-        router.T,
-    )
+        in_specs=[VMEM, VMEM, VMEM, VMEM, SMEM],
+    )(local, kernel_rows, ids, capacity, place)
     mixed, packed, gate = call(
         mix_kernel,
         (
@@ -309,13 +324,13 @@
             pltpu.VMEM((FRONT + count + BLOCK, width), BF16),
             pltpu.VMEM((count, width), BF16),
         ),
-    )(local, low, high, probs, onehot, slot_row, gain, columns)
+        in_specs=[SMEM] + [VMEM] * 8,
+    )(place, local, near_edge, cross_edge, probs, onehot, slot_row, gain, columns)
     crossed = to_core(packed[1])
     both = jnp.concatenate([packed[0], crossed], axis=1)
     size = 2 * depth
     near = list(range(chips // 2))
     order = [apart for apart in reversed(range(chips)) if apart not in near]
-    hidden = inner[0].shape[1]
     rows, sums = [None] * chips, [None] * chips
 
     def arrive(apart, earlier):
@@ -333,7 +348,7 @@
             scratch=(pltpu.VMEM((2 * size, width), BF16),),
         )(own, far, *inner)
         sums[apart] = call(
-            functools.partial(down_kernel, pieces, 0),
+            functools.partial(down_kernel, pieces),
             (shape((size, width), F32), shape((size, width), BF16)),
         )(*acts, *downs)
 

time: 80.3 us -> 78.4 us (0.976)
  local copies, waits for them, and re-layouts: 3.8 us -> 0.08 us
  Pallas kernels: 12.6 us -> 14.2 us
    ppermute x6, waiting for transfers between devices: 17.8 us -> 12.7 us  [to_chip(): lax.ppermute(array, 'seq', [(i, i ^ 2 * apart) for i in range(blocks)])]
    ppermute x11 -> x12, waiting for transfers between devices: 9.02 us -> 12.6 us  [across(): return lax.ppermute(array, ('blk', 'seq'), pairs)]
    unnamed x18 -> x4, local copies, waits for them, and re-layouts: 2.93 us -> 0.01 us
    ppermute x2 -> x1, starting transfers between devices: 2.84 us -> 0.66 us  [on_device(): cross_edge = lax.ppermute(cross_edge, 'seq', between)]
    pallas_call x4 -> x5, Pallas kernels: 2.95 us -> 4.84 us  [the longest x4 2.96 us: work(): call(functools.partial(down_kernel, pieces), (shape((size, width), F32),...]
    ppermute x6, starting transfers between devices: 12.6 us -> 14.4 us  [to_chip(): lax.ppermute(array, 'seq', [(i, i ^ 2 * apart) for i in range(blocks)])]
    ppermute x2 -> x3, waiting for transfers between devices: 2.32 us -> 3.39 us  [to_core(): return lax.ppermute(array, 'seq', [(i, i ^ 1) for i in range(blocks)])]
    ppermute x2 -> x3, starting transfers between devices: 2.63 us -> 3.34 us  [to_core(): return lax.ppermute(array, 'seq', [(i, i ^ 1) for i in range(blocks)])]
  transfers between devices with their start and end apart: 21 -> 22, of which waited for: 11 -> 11; matrix products, arithmetic and copies ran while one was open for 1% -> 0% of each run, Pallas kernels for 14% -> 16%
where the time goes in v5:
time: 78.4 us; the launch traced here: 78.2 us
  starting transfers between devices  34.8 us (44%)
  waiting for transfers between devices  28.8 us (37%)
  Pallas kernels  14.2 us (18%)
    ppermute x12, starting transfers between devices, across(): return lax.ppermute(array, ('blk', 'seq'), pairs)  16.4 us
    ppermute x6, starting transfers between devices, to_chip(): lax.ppermute(array, 'seq', [(i, i ^ 2 * apart) for i in range(blocks)])  14.4 us
    ppermute x6, waiting for transfers between devices, to_chip(): lax.ppermute(array, 'seq', [(i, i ^ 2 * apart) for i in range(blocks)])  12.7 us
    ppermute x12, waiting for transfers between devices, across(): return lax.ppermute(array, ('blk', 'seq'), pairs)  12.6 us
    pallas_call x4, Pallas kernels, work(): call(functools.partial(act_kernel, pieces, 1), [shape((2 * size, hidden),...  5.03 us
    ppermute x3, waiting for transfers between devices, to_core(): return lax.ppermute(array, 'seq', [(i, i ^ 1) for i in range(blocks)])  3.39 us
    ppermute x3, starting transfers between devices, to_core(): return lax.ppermute(array, 'seq', [(i, i ^ 1) for i in range(blocks)])  3.34 us
    pallas_call x4, Pallas kernels, work(): call(functools.partial(down_kernel, pieces), (shape((size, width), F32),...  2.96 us
  transfers between devices with their start and end apart: 22, of which 11 were waited for; matrix products, arithmetic and copies ran while one was open for 0% of the time, Pallas kernels for 16%

profile of v5, /device:TPU:0, one launch (start us, length us, event | category | flops | bytes accessed | tf_op | source)
XLA Modules:
  0.0 78.2 jit_solution(379464527171719689)
XLA Ops:
  0.0 3.0 %collective-permute-start.6 = (bf16[1024,512]{1,0:T(8,128)(2,1)}, bf16[1024,512]{1,0:T(8,128)(2,1)S(1)}, u32[]{:S(2)}, u32[]{:S(2)}) collective-permute-start(bf16[1024,512]{1,0:T(8,128)(2,1)} %bitcast.22), channel_id=1, source_target_pairs={{0,16},{1,9},{2,18},{3,11},{4,20},{5,13},{6,22},{7,15},{8,24},{9,1... | collective-permute-start | bytes 3145736 | tf_op jit(solution)/shard_map/ppermute | solution.py:262
  3.0 1.9 %shard_map.91 = (bf16[256,1024]{1,0:T(8,128)(2,1)S(1)}, bf16[496,1024]{1,0:T(8,128)(2,1)S(1)}, s32[1,256]{1,0:T(1,128)S(1)}, s32[1,8]{1,0:T(1,128)S(1)}, bf16[10...) custom-call(s32[1]{0:T(128)} %bitcast.place_ref, ...), custom_call_target="tpu_custom_call" | custom-call | tf_op jit(solution)/shard_map/pallas_call | solution.py:290
  4.9 0.1 collective-permute-start
  4.9 0.7 collective-permute-start.1
  5.6 1.1 %collective-permute-start.4 = (bf16[1024,512]{1,0:T(8,128)(2,1)S(1)}, bf16[1024,512]{1,0:T(8,128)(2,1)S(1)}, u32[]{:S(2)}, u32[]{:S(2)}) collective-permute-start(bf16[1024,512]{1,0:T(8,128)(2,1)S(1)} %bitcast.27), channel_id=1, source_target_pairs={{0,16},{1,9},{2,18},{3,11},{4,20},{5,13},{6,22},{7,15},{8,24},{9,1... | collective-permute-start | bytes 3145736 | tf_op jit(solution)/shard_map/ppermute | solution.py:262
  6.7 1.2 %shard_map.92 = (bf16[256,512]{1,0:T(8,128)(2,1)S(1)}, f32[256,8]{1,0:T(8,128)S(1)}, s32[256,8]{1,0:T(8,128)S(1)}, s32[1,256]{1,0:T(1,128)S(1)}) custom-call(bf16[256,1024]{1,0:T(8,128)(2,1)S(1)} %get-tuple-element.55.tokens_ref, bf16[496,1024]{1,0:T(8,128)(2,1)S(1)} %get-tuple-element.58.weight_ref, s32[1,256]{1,0:T(1,128)S(1)} %get-tuple-element.59.ids_ref, ...), custom_call_target="tpu_custom_call" | custom-call | tf_op jit(solution)/shard_map/pallas_call | solution.py:306
  7.9 0.0 collective-permute-done.near_ref
  8.0 1.5 %shard_map.93 = (f32[256,1024]{1,0:T(8,128)S(1)}, bf16[2,4,64,1024]{3,2,1,0:T(8,128)(2,1)S(1)}, f32[256,1]{1,0:T(8,128)S(1)}) custom-call(s32[1]{0:T(128)} %bitcast.place_ref, bf16[256,1024]{1,0:T(8,128)(2,1)S(1)} %get-tuple-element.55.tokens_ref, bf16[16,1024]{1,0:T(8,128)(2,1)S(1)} %collective-permute-done.near_ref, ...), custom_call_target="tpu_custom_call" | custom-call | tf_op jit(solution)/shard_map/pallas_call | solution.py:316
  9.5 0.1 slice_bitcast_fusion
  9.6 3.2 %collective-permute-start.2 = (bf16[4,64,1024]{2,1,0:T(8,128)(2,1)S(1)}, bf16[4,64,1024]{2,1,0:T(8,128)(2,1)S(1)}, u32[]{:S(2)}, u32[]{:S(2)}) collective-permute-start(bf16[4,64,1024]{2,1,0:T(8,128)(2,1)S(1)} %get-tuple-element.109), channel_id=1, source_target_pairs={{0,1},{1,0},{2,3},{3,2},{4,5},{5,4},{6,7},{7,6},{8,9},{9,8},{10,11... | collective-permute-start | bytes 1572872 | tf_op jit(solution)/shard_map/ppermute | solution.py:276
  12.8 1.5 %collective-permute-done.2 = bf16[4,64,1024]{2,1,0:T(8,128)(2,1)S(1)} collective-permute-done((bf16[4,64,1024]{2,1,0:T(8,128)(2,1)S(1)}, bf16[4,64,1024]{2,1,0:T(8,128)(2,1)S(1)}, u32[]{:S(2)}, u32[]{:S(2)}) %collective-permute-start.2) | collective-permute-done | bytes 524320 | tf_op jit(solution)/shard_map/ppermute | solution.py:276
  14.3 0.1 fusion.3
  14.4 3.1 %collective-permute-start.3 = (bf16[128,1024]{1,0:T(8,128)(2,1)S(1)}, bf16[128,1024]{1,0:T(8,128)(2,1)S(1)}, u32[]{:S(2)}, u32[]{:S(2)}) collective-permute-start(bf16[128,1024]{1,0:T(8,128)(2,1)S(1)} %get-tuple-element.106), channel_id=1, source_target_pairs={{0,6},{1,7},{2,4},{3,5},{4,2},{5,3},{6,0},{7,1},{8,14},{9,15},{10,... | collective-permute-start | bytes 786440 | tf_op jit(solution)/shard_map/ppermute | solution.py:273
  17.5 1.0 %collective-permute-start.7 = (bf16[512,512]{1,0:T(8,128)(2,1)S(1)}, bf16[512,512]{1,0:T(8,128)(2,1)S(1)}, u32[]{:S(2)}, u32[]{:S(2)}) collective-permute-start(bf16[512,512]{1,0:T(8,128)(2,1)S(1)} %get-tuple-element.75.refs_2_), channel_id=1, source_target_pairs={{0,16},{1,9},{2,18},{3,11},{4,20},{5,13},{6,22},{7,15},{8,24},{9,1... | collective-permute-start | bytes 1572872 | tf_op jit(solution)/shard_map/ppermute | solution.py:262
  18.5 1.0 %collective-permute-start.8 = (bf16[512,512]{1,0:T(8,128)(2,1)S(1)}, bf16[512,512]{1,0:T(8,128)(2,1)S(1)}, u32[]{:S(2)}, u32[]{:S(2)}) collective-permute-start(bf16[512,512]{1,0:T(8,128)(2,1)S(1)} %get-tuple-element.76.refs_3_), channel_id=1, source_target_pairs={{0,16},{1,9},{2,18},{3,11},{4,20},{5,13},{6,22},{7,15},{8,24},{9,1... | collective-permute-start | bytes 1572872 | tf_op jit(solution)/shard_map/ppermute | solution.py:262
  19.5 5.4 %collective-permute-done.3.refs_0_ = bf16[128,1024]{1,0:T(8,128)(2,1)S(1)} collective-permute-done((bf16[128,1024]{1,0:T(8,128)(2,1)S(1)}, bf16[128,1024]{1,0:T(8,128)(2,1)S(1)}, u32[]{:S(2)}, u32[]{:S(2)}) %collective-permute-start.3) | collective-permute-done | bytes 262176 | tf_op jit(solution)/shard_map/ppermute | solution.py:273
  25.0 2.2 %collective-permute-done.4.refs_5_ = bf16[1024,512]{1,0:T(8,128)(2,1)S(1)} collective-permute-done((bf16[1024,512]{1,0:T(8,128)(2,1)S(1)}, bf16[1024,512]{1,0:T(8,128)(2,1)S(1)}, u32[]{:S(2)}, u32[]{:S(2)}) %collective-permute-start.4) | collective-permute-done | bytes 1048608 | tf_op jit(solution)/shard_map/ppermute | solution.py:262
  27.2 2.0 %collective-permute-start.5 = (bf16[128,1024]{1,0:T(8,128)(2,1)S(1)}, bf16[128,1024]{1,0:T(8,128)(2,1)S(1)}, u32[]{:S(2)}, u32[]{:S(2)}) collective-permute-start(bf16[128,1024]{1,0:T(8,128)(2,1)S(1)} %collective-permute-done.3.refs_0_), channel_id=1, source_target_pairs={{0,8},{1,17},{2,10},{3,19},{4,12},{5,21},{6,14},{7,23},{8,0},{9,25... | collective-permute-start | bytes 786440 | tf_op jit(solution)/shard_map/ppermute | solution.py:262
  29.2 3.4 %collective-permute-start.15 = (bf16[128,1024]{1,0:T(8,128)(2,1)S(1)}, bf16[128,1024]{1,0:T(8,128)(2,1)S(1)}, u32[]{:S(2)}, u32[]{:S(2)}) collective-permute-start(bf16[128,1024]{1,0:T(8,128)(2,1)S(1)} %get-tuple-element.90), channel_id=1, source_target_pairs={{0,4},{1,5},{2,6},{3,7},{4,0},{5,1},{6,2},{7,3},{8,12},{9,13},{10,... | collective-permute-start | bytes 786440 | tf_op jit(solution)/shard_map/ppermute | solution.py:273
  32.6 0.7 collective-permute-start.11
  33.4 3.1 %collective-permute-done.5.refs_1_ = bf16[128,1024]{1,0:T(8,128)(2,1)S(1)} collective-permute-done((bf16[128,1024]{1,0:T(8,128)(2,1)S(1)}, bf16[128,1024]{1,0:T(8,128)(2,1)S(1)}, u32[]{:S(2)}, u32[]{:S(2)}) %collective-permute-start.5) | collective-permute-done | bytes 262176 | tf_op jit(solution)/shard_map/ppermute | solution.py:262
  36.4 1.3 %shard_map.94 = (bf16[256,512]{1,0:T(8,128)(2,1)S(1)}, bf16[256,512]{1,0:T(8,128)(2,1)S(1)}) custom-call(bf16[128,1024]{1,0:T(8,128)(2,1)S(1)} %collective-permute-done.3.refs_0_, bf16[128,1024]{1,0:T(8,128)(2,1)S(1)} %collective-permute-done.5.refs_1_, bf16[1024,512]{1,0:T(8,128)(2,1)S(1)} %bitcast.23, bf16[1024,512]{1,0:T(8,128)(2,1)S(1)} %bitcast.28, ...), custom_call_target="tpu_custom_call" | custom-call | tf_op jit(solution)/shard_map/pallas_call | solution.py:345
  37.7 3.5 %collective-permute-done.8.refs_5_ = bf16[512,512]{1,0:T(8,128)(2,1)S(1)} collective-permute-done((bf16[512,512]{1,0:T(8,128)(2,1)S(1)}, bf16[512,512]{1,0:T(8,128)(2,1)S(1)}, u32[]{:S(2)}, u32[]{:S(2)}) %collective-permute-start.8) | collective-permute-done | bytes 524320 | tf_op jit(solution)/shard_map/ppermute | solution.py:262
  41.2 0.7 shard_map.95
  42.0 2.1 %collective-permute-start.16 = (bf16[128,1024]{1,0:T(8,128)(2,1)S(1)}, bf16[128,1024]{1,0:T(8,128)(2,1)S(1)}, u32[]{:S(2)}, u32[]{:S(2)}) collective-permute-start(bf16[128,1024]{1,0:T(8,128)(2,1)S(1)} %get-tuple-element.77), channel_id=1, source_target_pairs={{0,8},{1,17},{2,10},{3,19},{4,12},{5,21},{6,14},{7,23},{8,0},{9,25... | collective-permute-start | bytes 786440 | tf_op jit(solution)/shard_map/ppermute | solution.py:262
  44.0 0.5 collective-permute-start.17
  44.6 1.5 %collective-permute-start.12 = (bf16[128,1024]{1,0:T(8,128)(2,1)S(1)}, bf16[128,1024]{1,0:T(8,128)(2,1)S(1)}, u32[]{:S(2)}, u32[]{:S(2)}) collective-permute-start(bf16[128,1024]{1,0:T(8,128)(2,1)S(1)} %collective-permute-done.11.refs_0_), channel_id=1, source_target_pairs={{0,8},{1,17},{2,10},{3,19},{4,12},{5,21},{6,14},{7,23},{8,0},{9,25... | collective-permute-start | bytes 786440 | tf_op jit(solution)/shard_map/ppermute | solution.py:262
  46.1 0.5 collective-permute-start.9
  46.6 1.8 %collective-permute-done.16.other_ref = bf16[128,1024]{1,0:T(8,128)(2,1)S(1)} collective-permute-done((bf16[128,1024]{1,0:T(8,128)(2,1)S(1)}, bf16[128,1024]{1,0:T(8,128)(2,1)S(1)}, u32[]{:S(2)}, u32[]{:S(2)}) %collective-permute-start.16) | collective-permute-done | bytes 262176 | tf_op jit(solution)/shard_map/ppermute | solution.py:262
  48.5 4.2 %collective-permute-start.19 = (bf16[128,1024]{1,0:T(8,128)(2,1)S(1)}, bf16[128,1024]{1,0:T(8,128)(2,1)S(1)}, u32[]{:S(2)}, u32[]{:S(2)}) collective-permute-start(bf16[128,1024]{1,0:T(8,128)(2,1)S(1)} %shard_map.104), channel_id=1, source_target_pairs={{0,6},{1,7},{2,4},{3,5},{4,2},{5,3},{6,0},{7,1},{8,14},{9,15},{10,... | collective-permute-start | bytes 786440 | tf_op jit(solution)/shard_map/ppermute | solution.py:273
  52.6 1.3 %shard_map.105 = (bf16[256,512]{1,0:T(8,128)(2,1)S(1)}, bf16[256,512]{1,0:T(8,128)(2,1)S(1)}) custom-call(bf16[128,1024]{1,0:T(8,128)(2,1)S(1)} %collective-permute-done.15.refs_0_, bf16[128,1024]{1,0:T(8,128)(2,1)S(1)} %collective-permute-done.17.refs_1_, bf16[1024,512]{1,0:T(8,128)(2,1)S(1)} %bitcast.24, bf16[1024,512]{1,0:T(8,128)(2,1)S(1)} %bitcast.29, ...), custom_call_target="tpu_custom_call" | custom-call | tf_op jit(solution)/shard_map/pallas_call | solution.py:345
  53.9 0.7 shard_map.106
  54.7 1.6 %collective-permute-start.18 = (bf16[128,1024]{1,0:T(8,128)(2,1)S(1)}, bf16[128,1024]{1,0:T(8,128)(2,1)S(1)}, u32[]{:S(2)}, u32[]{:S(2)}) collective-permute-start(bf16[128,1024]{1,0:T(8,128)(2,1)S(1)} %get-tuple-element.97), channel_id=1, source_target_pairs={{0,8},{1,17},{2,10},{3,19},{4,12},{5,21},{6,14},{7,23},{8,0},{9,25... | collective-permute-start | bytes 786440 | tf_op jit(solution)/shard_map/ppermute | solution.py:262
  56.2 1.3 %shard_map.100 = (bf16[256,512]{1,0:T(8,128)(2,1)S(1)}, bf16[256,512]{1,0:T(8,128)(2,1)S(1)}) custom-call(bf16[128,1024]{1,0:T(8,128)(2,1)S(1)} %collective-permute-done.11.refs_0_, bf16[128,1024]{1,0:T(8,128)(2,1)S(1)} %collective-permute-done.12.refs_1_, bf16[1024,512]{1,0:T(8,128)(2,1)S(1)} %bitcast.25, bf16[1024,512]{1,0:T(8,128)(2,1)S(1)} %bitcast.30, ...), custom_call_target="tpu_custom_call" | custom-call | tf_op jit(solution)/shard_map/pallas_call | solution.py:345
  57.5 0.7 shard_map.101
  58.2 0.6 collective-permute-start.13
  58.8 1.3 %shard_map.96 = (bf16[256,512]{1,0:T(8,128)(2,1)S(1)}, bf16[256,512]{1,0:T(8,128)(2,1)S(1)}) custom-call(bf16[128,1024]{1,0:T(8,128)(2,1)S(1)} %get-tuple-element.78.refs_0_, bf16[128,1024]{1,0:T(8,128)(2,1)S(1)} %collective-permute-done.9.refs_1_, bf16[1024,512]{1,0:T(8,128)(2,1)S(1)} %bitcast.26, bf16[1024,512]{1,0:T(8,128)(2,1)S(1)} %bitcast.31, ...), custom_call_target="tpu_custom_call" | custom-call | tf_op jit(solution)/shard_map/pallas_call | solution.py:345
  60.1 0.7 shard_map.97
  60.8 1.6 %collective-permute-start.10 = (bf16[128,1024]{1,0:T(8,128)(2,1)S(1)}, bf16[128,1024]{1,0:T(8,128)(2,1)S(1)}, u32[]{:S(2)}, u32[]{:S(2)}) collective-permute-start(bf16[128,1024]{1,0:T(8,128)(2,1)S(1)} %get-tuple-element.82), channel_id=1, source_target_pairs={{0,8},{1,17},{2,10},{3,19},{4,12},{5,21},{6,14},{7,23},{8,0},{9,25... | collective-permute-start | bytes 786440 | tf_op jit(solution)/shard_map/ppermute | solution.py:262
  62.5 1.7 %collective-permute-start.20 = (bf16[128,1024]{1,0:T(8,128)(2,1)S(1)}, bf16[128,1024]{1,0:T(8,128)(2,1)S(1)}, u32[]{:S(2)}, u32[]{:S(2)}) collective-permute-start(bf16[128,1024]{1,0:T(8,128)(2,1)S(1)} %shard_map.107), channel_id=1, source_target_pairs={{0,4},{1,5},{2,6},{3,7},{4,0},{5,1},{6,2},{7,3},{8,12},{9,13},{10,... | collective-permute-start | bytes 786440 | tf_op jit(solution)/shard_map/ppermute | solution.py:273
  64.2 0.4 collective-permute-done.13.other_ref
  64.7 1.2 %collective-permute-start.14 = (bf16[128,1024]{1,0:T(8,128)(2,1)S(1)}, bf16[128,1024]{1,0:T(8,128)(2,1)S(1)}, u32[]{:S(2)}, u32[]{:S(2)}) collective-permute-start(bf16[128,1024]{1,0:T(8,128)(2,1)S(1)} %shard_map.102), channel_id=1, source_target_pairs={{0,2},{1,3},{2,0},{3,1},{4,6},{5,7},{6,4},{7,5},{8,10},{9,11},{10,... | collective-permute-start | bytes 786440 | tf_op jit(solution)/shard_map/ppermute | solution.py:273
  65.9 1.5 %collective-permute-done.10.other_ref = bf16[128,1024]{1,0:T(8,128)(2,1)S(1)} collective-permute-done((bf16[128,1024]{1,0:T(8,128)(2,1)S(1)}, bf16[128,1024]{1,0:T(8,128)(2,1)S(1)}, u32[]{:S(2)}, u32[]{:S(2)}) %collective-permute-start.10) | collective-permute-done | bytes 262176 | tf_op jit(solution)/shard_map/ppermute | solution.py:262
  67.5 6.9 %collective-permute-done.20.back_ref = bf16[128,1024]{1,0:T(8,128)(2,1)S(1)} collective-permute-done((bf16[128,1024]{1,0:T(8,128)(2,1)S(1)}, bf16[128,1024]{1,0:T(8,128)(2,1)S(1)}, u32[]{:S(2)}, u32[]{:S(2)}) %collective-permute-start.20) | collective-permute-done | bytes 262176 | tf_op jit(solution)/shard_map/ppermute | solution.py:273
  74.4 0.4 collective-permute-done.14.back_ref
  75.0 0.1 collective-permute-start.21
  75.1 1.9 %collective-permute-done.21.handed_ref = bf16[256,1024]{1,0:T(8,128)(2,1)S(1)} collective-permute-done((bf16[256,1024]{1,0:T(8,128)(2,1)S(1)}, bf16[256,1024]{1,0:T(8,128)(2,1)S(1)}, u32[]{:S(2)}, u32[]{:S(2)}) %collective-permute-start.21) | collective-permute-done | bytes 524320 | tf_op jit(solution)/shard_map/ppermute | solution.py:276
  76.9 1.3 %shard_map.110 = bf16[256,1024]{1,0:T(8,128)(2,1)} custom-call(f32[256,1024]{1,0:T(8,128)S(1)} %get-tuple-element.66.mixed_ref, f32[256,1]{1,0:T(8,128)S(1)} %get-tuple-element.67.gate_ref, s32[256,8]{1,0:T(8,128)S(1)} %get-tuple-element.68.slot_ref, bf16[256,1024]{1,0:T(8,128)(2,1)S(1)} %pad_maximum_fusion.returned_ref, ...), custom_call_target="tpu_custom_call" | custom-call | tf_op jit(solution)/shard_map/pallas_call | solution.py:381
  (24 shorter events, 0.4 us)
Async XLA Ops:
  0.0 17.5 %collective-permute-start.6 = (bf16[1024,512]{1,0:T(8,128)(2,1)}, bf16[1024,512]{1,0:T(8,128)(2,1)S(1)}, u32[]{:S(2)}, u32[]{:S(2)}) collective-permute-start(bf16[1024,512]{1,0:T(8,128)(2,1)} %bitcast.22), channel_id=1, source_target_pairs={{0,16},{1,9},{2,18},{3,11},{4,20},{5,13},{6,22},{7,15},{8,24},{9,1... | collective-permute-start | bytes 3145736 | tf_op jit(solution)/shard_map/ppermute | solution.py:262
  3.0 2.6 %copy-start.1 = (bf16[1,1024,512]{2,1,0:T(8,128)(2,1)S(1)}, bf16[1,1024,512]{2,1,0:T(8,128)(2,1)}, u32[]{:S(2)}) copy-start(bf16[1,1024,512]{2,1,0:T(8,128)(2,1)} %param.16) | copy-start | bytes 3145732
  4.9 3.1 %collective-permute-start = (bf16[16,1024]{1,0:T(8,128)(2,1)S(1)}, bf16[16,1024]{1,0:T(8,128)(2,1)S(1)}, u32[]{:S(2)}, u32[]{:S(2)}) collective-permute-start(bf16[16,1024]{1,0:T(8,128)(2,1)S(1)} %get-tuple-element.56), channel_id=1, source_target_pairs={{0,1},{1,0},{2,3},{3,2},{4,5},{5,4},{6,7},{7,6},{8,9},{9,8},{10,11... | collective-permute-start | bytes 98312 | tf_op jit(solution)/shard_map/ppermute | solution.py:276
  4.9 3.0 %collective-permute-start.1 = (bf16[16,1024]{1,0:T(8,128)(2,1)S(1)}, bf16[16,1024]{1,0:T(8,128)(2,1)S(1)}, u32[]{:S(2)}, u32[]{:S(2)}) collective-permute-start(bf16[16,1024]{1,0:T(8,128)(2,1)S(1)} %get-tuple-element.57), channel_id=1, source_target_pairs={{1,2},{3,4},{5,6},{2,1},{4,3},{6,5},{9,10},{11,12},{13,14},{10,9},... | collective-permute-start | bytes 98312 | tf_op jit(solution)/shard_map/ppermute | solution.py:305
  5.6 21.6 %collective-permute-start.4 = (bf16[1024,512]{1,0:T(8,128)(2,1)S(1)}, bf16[1024,512]{1,0:T(8,128)(2,1)S(1)}, u32[]{:S(2)}, u32[]{:S(2)}) collective-permute-start(bf16[1024,512]{1,0:T(8,128)(2,1)S(1)} %bitcast.27), channel_id=1, source_target_pairs={{0,16},{1,9},{2,18},{3,11},{4,20},{5,13},{6,22},{7,15},{8,24},{9,1... | collective-permute-start | bytes 3145736 | tf_op jit(solution)/shard_map/ppermute | solution.py:262
  9.6 4.7 %collective-permute-start.2 = (bf16[4,64,1024]{2,1,0:T(8,128)(2,1)S(1)}, bf16[4,64,1024]{2,1,0:T(8,128)(2,1)S(1)}, u32[]{:S(2)}, u32[]{:S(2)}) collective-permute-start(bf16[4,64,1024]{2,1,0:T(8,128)(2,1)S(1)} %get-tuple-element.109), channel_id=1, source_target_pairs={{0,1},{1,0},{2,3},{3,2},{4,5},{5,4},{6,7},{7,6},{8,9},{9,8},{10,11... | collective-permute-start | bytes 1572872 | tf_op jit(solution)/shard_map/ppermute | solution.py:276
  14.3 22.1 %copy-start = (bf16[1,1024,512]{2,1,0:T(8,128)(2,1)S(1)}, bf16[1,1024,512]{2,1,0:T(8,128)(2,1)}, u32[]{:S(2)}) copy-start(bf16[1,1024,512]{2,1,0:T(8,128)(2,1)} %param.15) | copy-start | bytes 3145732
  14.4 10.6 %collective-permute-start.3 = (bf16[128,1024]{1,0:T(8,128)(2,1)S(1)}, bf16[128,1024]{1,0:T(8,128)(2,1)S(1)}, u32[]{:S(2)}, u32[]{:S(2)}) collective-permute-start(bf16[128,1024]{1,0:T(8,128)(2,1)S(1)} %get-tuple-element.106), channel_id=1, source_target_pairs={{0,6},{1,7},{2,4},{3,5},{4,2},{5,3},{6,0},{7,1},{8,14},{9,15},{10,... | collective-permute-start | bytes 786440 | tf_op jit(solution)/shard_map/ppermute | solution.py:273
  17.5 20.2 %collective-permute-start.7 = (bf16[512,512]{1,0:T(8,128)(2,1)S(1)}, bf16[512,512]{1,0:T(8,128)(2,1)S(1)}, u32[]{:S(2)}, u32[]{:S(2)}) collective-permute-start(bf16[512,512]{1,0:T(8,128)(2,1)S(1)} %get-tuple-element.75.refs_2_), channel_id=1, source_target_pairs={{0,16},{1,9},{2,18},{3,11},{4,20},{5,13},{6,22},{7,15},{8,24},{9,1... | collective-permute-start | bytes 1572872 | tf_op jit(solution)/shard_map/ppermute | solution.py:262
  18.5 22.7 %collective-permute-start.8 = (bf16[512,512]{1,0:T(8,128)(2,1)S(1)}, bf16[512,512]{1,0:T(8,128)(2,1)S(1)}, u32[]{:S(2)}, u32[]{:S(2)}) collective-permute-start(bf16[512,512]{1,0:T(8,128)(2,1)S(1)} %get-tuple-element.76.refs_3_), channel_id=1, source_target_pairs={{0,16},{1,9},{2,18},{3,11},{4,20},{5,13},{6,22},{7,15},{8,24},{9,1... | collective-permute-start | bytes 1572872 | tf_op jit(solution)/shard_map/ppermute | solution.py:262
  27.2 9.2 %collective-permute-start.5 = (bf16[128,1024]{1,0:T(8,128)(2,1)S(1)}, bf16[128,1024]{1,0:T(8,128)(2,1)S(1)}, u32[]{:S(2)}, u32[]{:S(2)}) collective-permute-start(bf16[128,1024]{1,0:T(8,128)(2,1)S(1)} %collective-permute-done.3.refs_0_), channel_id=1, source_target_pairs={{0,8},{1,17},{2,10},{3,19},{4,12},{5,21},{6,14},{7,23},{8,0},{9,25... | collective-permute-start | bytes 786440 | tf_op jit(solution)/shard_map/ppermute | solution.py:262
  29.2 14.9 %collective-permute-start.15 = (bf16[128,1024]{1,0:T(8,128)(2,1)S(1)}, bf16[128,1024]{1,0:T(8,128)(2,1)S(1)}, u32[]{:S(2)}, u32[]{:S(2)}) collective-permute-start(bf16[128,1024]{1,0:T(8,128)(2,1)S(1)} %get-tuple-element.90), channel_id=1, source_target_pairs={{0,4},{1,5},{2,6},{3,7},{4,0},{5,1},{6,2},{7,3},{8,12},{9,13},{10,... | collective-permute-start | bytes 786440 | tf_op jit(solution)/shard_map/ppermute | solution.py:273
  32.6 12.0 %collective-permute-start.11 = (bf16[128,1024]{1,0:T(8,128)(2,1)S(1)}, bf16[128,1024]{1,0:T(8,128)(2,1)S(1)}, u32[]{:S(2)}, u32[]{:S(2)}) collective-permute-start(bf16[128,1024]{1,0:T(8,128)(2,1)S(1)} %get-tuple-element.108), channel_id=1, source_target_pairs={{0,2},{1,3},{2,0},{3,1},{4,6},{5,7},{6,4},{7,5},{8,10},{9,11},{10,... | collective-permute-start | bytes 786440 | tf_op jit(solution)/shard_map/ppermute | solution.py:273
  42.0 6.4 %collective-permute-start.16 = (bf16[128,1024]{1,0:T(8,128)(2,1)S(1)}, bf16[128,1024]{1,0:T(8,128)(2,1)S(1)}, u32[]{:S(2)}, u32[]{:S(2)}) collective-permute-start(bf16[128,1024]{1,0:T(8,128)(2,1)S(1)} %get-tuple-element.77), channel_id=1, source_target_pairs={{0,8},{1,17},{2,10},{3,19},{4,12},{5,21},{6,14},{7,23},{8,0},{9,25... | collective-permute-start | bytes 786440 | tf_op jit(solution)/shard_map/ppermute | solution.py:262
  44.0 8.6 %collective-permute-start.17 = (bf16[128,1024]{1,0:T(8,128)(2,1)S(1)}, bf16[128,1024]{1,0:T(8,128)(2,1)S(1)}, u32[]{:S(2)}, u32[]{:S(2)}) collective-permute-start(bf16[128,1024]{1,0:T(8,128)(2,1)S(1)} %collective-permute-done.15.refs_0_), channel_id=1, source_target_pairs={{0,8},{1,17},{2,10},{3,19},{4,12},{5,21},{6,14},{7,23},{8,0},{9,25... | collective-permute-start | bytes 786440 | tf_op jit(solution)/shard_map/ppermute | solution.py:262
  44.6 11.6 %collective-permute-start.12 = (bf16[128,1024]{1,0:T(8,128)(2,1)S(1)}, bf16[128,1024]{1,0:T(8,128)(2,1)S(1)}, u32[]{:S(2)}, u32[]{:S(2)}) collective-permute-start(bf16[128,1024]{1,0:T(8,128)(2,1)S(1)} %collective-permute-done.11.refs_0_), channel_id=1, source_target_pairs={{0,8},{1,17},{2,10},{3,19},{4,12},{5,21},{6,14},{7,23},{8,0},{9,25... | collective-permute-start | bytes 786440 | tf_op jit(solution)/shard_map/ppermute | solution.py:262
  46.1 12.8 %collective-permute-start.9 = (bf16[128,1024]{1,0:T(8,128)(2,1)S(1)}, bf16[128,1024]{1,0:T(8,128)(2,1)S(1)}, u32[]{:S(2)}, u32[]{:S(2)}) collective-permute-start(bf16[128,1024]{1,0:T(8,128)(2,1)S(1)} %get-tuple-element.78.refs_0_), channel_id=1, source_target_pairs={{0,8},{1,17},{2,10},{3,19},{4,12},{5,21},{6,14},{7,23},{8,0},{9,25... | collective-permute-start | bytes 786440 | tf_op jit(solution)/shard_map/ppermute | solution.py:262
  48.5 13.9 %collective-permute-start.19 = (bf16[128,1024]{1,0:T(8,128)(2,1)S(1)}, bf16[128,1024]{1,0:T(8,128)(2,1)S(1)}, u32[]{:S(2)}, u32[]{:S(2)}) collective-permute-start(bf16[128,1024]{1,0:T(8,128)(2,1)S(1)} %shard_map.104), channel_id=1, source_target_pairs={{0,6},{1,7},{2,4},{3,5},{4,2},{5,3},{6,0},{7,1},{8,14},{9,15},{10,... | collective-permute-start | bytes 786440 | tf_op jit(solution)/shard_map/ppermute | solution.py:273
  54.7 7.8 %collective-permute-start.18 = (bf16[128,1024]{1,0:T(8,128)(2,1)S(1)}, bf16[128,1024]{1,0:T(8,128)(2,1)S(1)}, u32[]{:S(2)}, u32[]{:S(2)}) collective-permute-start(bf16[128,1024]{1,0:T(8,128)(2,1)S(1)} %get-tuple-element.97), channel_id=1, source_target_pairs={{0,8},{1,17},{2,10},{3,19},{4,12},{5,21},{6,14},{7,23},{8,0},{9,25... | collective-permute-start | bytes 786440 | tf_op jit(solution)/shard_map/ppermute | solution.py:262
  58.2 6.4 %collective-permute-start.13 = (bf16[128,1024]{1,0:T(8,128)(2,1)S(1)}, bf16[128,1024]{1,0:T(8,128)(2,1)S(1)}, u32[]{:S(2)}, u32[]{:S(2)}) collective-permute-start(bf16[128,1024]{1,0:T(8,128)(2,1)S(1)} %get-tuple-element.88), channel_id=1, source_target_pairs={{0,8},{1,17},{2,10},{3,19},{4,12},{5,21},{6,14},{7,23},{8,0},{9,25... | collective-permute-start | bytes 786440 | tf_op jit(solution)/shard_map/ppermute | solution.py:262
  60.8 6.6 %collective-permute-start.10 = (bf16[128,1024]{1,0:T(8,128)(2,1)S(1)}, bf16[128,1024]{1,0:T(8,128)(2,1)S(1)}, u32[]{:S(2)}, u32[]{:S(2)}) collective-permute-start(bf16[128,1024]{1,0:T(8,128)(2,1)S(1)} %get-tuple-element.82), channel_id=1, source_target_pairs={{0,8},{1,17},{2,10},{3,19},{4,12},{5,21},{6,14},{7,23},{8,0},{9,25... | collective-permute-start | bytes 786440 | tf_op jit(solution)/shard_map/ppermute | solution.py:262
  62.5 11.9 %collective-permute-start.20 = (bf16[128,1024]{1,0:T(8,128)(2,1)S(1)}, bf16[128,1024]{1,0:T(8,128)(2,1)S(1)}, u32[]{:S(2)}, u32[]{:S(2)}) collective-permute-start(bf16[128,1024]{1,0:T(8,128)(2,1)S(1)} %shard_map.107), channel_id=1, source_target_pairs={{0,4},{1,5},{2,6},{3,7},{4,0},{5,1},{6,2},{7,3},{8,12},{9,13},{10,... | collective-permute-start | bytes 786440 | tf_op jit(solution)/shard_map/ppermute | solution.py:273
  64.7 10.2 %collective-permute-start.14 = (bf16[128,1024]{1,0:T(8,128)(2,1)S(1)}, bf16[128,1024]{1,0:T(8,128)(2,1)S(1)}, u32[]{:S(2)}, u32[]{:S(2)}) collective-permute-start(bf16[128,1024]{1,0:T(8,128)(2,1)S(1)} %shard_map.102), channel_id=1, source_target_pairs={{0,2},{1,3},{2,0},{3,1},{4,6},{5,7},{6,4},{7,5},{8,10},{9,11},{10,... | collective-permute-start | bytes 786440 | tf_op jit(solution)/shard_map/ppermute | solution.py:273
  75.0 2.0 %collective-permute-start.21 = (bf16[256,1024]{1,0:T(8,128)(2,1)S(1)}, bf16[256,1024]{1,0:T(8,128)(2,1)S(1)}, u32[]{:S(2)}, u32[]{:S(2)}) collective-permute-start(bf16[256,1024]{1,0:T(8,128)(2,1)S(1)} %pad_maximum_fusion.1), channel_id=1, source_target_pairs={{0,1},{1,0},{2,3},{3,2},{4,5},{5,4},{6,7},{7,6},{8,9},{9,8},{10,11... | collective-permute-start | bytes 1572872 | tf_op jit(solution)/shard_map/ppermute | solution.py:276

commit v6 on v5

--- a/solution.py
+++ b/solution.py
@@ -167,15 +167,22 @@
     gate_ref[...] = jax.nn.sigmoid(jnp.sum(gates * onehot_ref[...], axis=1, keepdims=True))
 
 
-def combine_kernel(mixed_ref, gate_ref, slot_ref, returned_ref, handed_ref, out_ref):
-    count = mixed_ref.shape[0]
-    half = returned_ref.shape[0]
-    slot = slot_ref[:, :1]
-    near = jnp.where(slot == iota((count, half), 1), 1.0, 0.0).astype(BF16)
-    cross = jnp.where(slot == iota((count, half), 1) + half, 1.0, 0.0).astype(BF16)
-    out = jnp.dot(near, returned_ref[...], preferred_element_type=F32)
-    out = out + jnp.dot(cross, handed_ref[...], preferred_element_type=F32)
-    out_ref[...] = (mixed_ref[...] + gate_ref[...] * out).astype(BF16)
+def combine_kernel(places, total_ref, gate_ref, slot_ref, *refs):
+    pieces, (out_ref, held_ref) = refs[:-2], refs[-2:]
+    count = total_ref.shape[0]
+    held = held_ref.shape[0]
+    depth = held // len(places)
+    first = 0
+    for piece_ref in pieces:
+        held_ref[pl.ds(first, piece_ref.shape[0]), :] = piece_ref[...]
+        first += piece_ref.shape[0]
+    place = iota((count, held), 1)
+    row = place % depth
+    for index, group in enumerate(places):
+        row = row + jnp.where(place // depth == index, group * depth, 0)
+    select = jnp.where(slot_ref[:, :1] == row, 1.0, 0.0).astype(BF16)
+    out = jnp.dot(select, held_ref[...], preferred_element_type=F32)
+    out_ref[...] = (total_ref[...] + gate_ref[...] * out).astype(out_ref.dtype)
 
 
 def act_kernel(pieces, groups, *refs):
@@ -205,6 +212,40 @@
             total = part if total is None else total + part
         own_ref[:, columns] = total[:size]
         far_ref[:, columns] = total[size:].astype(BF16)
+
+
+def early_kernel(pieces, *refs):
+    acts, own_downs, first_halves, total_ref = (
+        refs[:pieces],
+        refs[pieces : pieces + 2],
+        refs[pieces + 2 : -1],
+        refs[-1],
+    )
+    width = total_ref.shape[1]
+    for half in range(2):
+        downs = [own_downs[half], *(first_halves if half == 0 else ())]
+        total = None
+        for act_ref, down_ref in zip(acts, downs, strict=False):
+            part = lax.dot_general(
+                act_ref[...], down_ref[...], (((1,), (1,)), ((), ())), preferred_element_type=F32
+            )
+            total = part if total is None else total + part
+        total_ref[:, pl.ds(half * (width // 2), width // 2)] = total
+
+
+def late_kernel(pieces, *refs):
+    total_ref, acts, downs, (own_ref, far_ref) = refs[0], refs[1:pieces], refs[pieces : 2 * pieces - 1], refs[-2:]
+    size, width = own_ref.shape
+    first, second = pl.ds(0, width // 2), pl.ds(width // 2, width // 2)
+    total = total_ref[:, second]
+    for act_ref, down_ref in zip(acts, downs, strict=True):
+        total = total + lax.dot_general(
+            act_ref[...], down_ref[...], (((1,), (1,)), ((), ())), preferred_element_type=F32
+        )
+    far_ref[:, first] = total_ref[pl.ds(size, size), first].astype(BF16)
+    far_ref[:, second] = total[size:].astype(BF16)
+    own_ref[:, first] = total_ref[pl.ds(0, size), first]
+    own_ref[:, second] = total[:size]
 
 
 def add_kernel(own_ref, other_ref, out_ref):
@@ -376,10 +417,20 @@
         arrive(apart, None)
         work(apart, sums[order[0]][1])
         finish(apart)
-    returned = jnp.concatenate(returned)
-    handed = to_core(jnp.concatenate(handed))
-    result = call(combine_kernel, shape((count, width), BF16))(mixed, gate, slot, returned, handed)
-    return result[None]
+    def combine(total, places, arrays, dtype):
+        return call(
+            functools.partial(combine_kernel, tuple(places)),
+            shape((count, width), dtype),
+            scratch=(pltpu.VMEM((len(places) * depth, width), BF16),),
+        )(total, gate, slot, *arrays)
+
+    late = [apart for apart in range(chips) if apart in order[1:] or apart == near[-1]]
+    early = [apart for apart in range(chips) if apart not in late]
+    soon = to_core(jnp.concatenate([handed[apart] for apart in early]))
+    last = to_core(jnp.concatenate([handed[apart] for apart in late]))
+    places = list(range(chips)) + [chips + apart for apart in early]
+    total = combine(mixed, places, [*returned, soon], F32)
+    return combine(total, [chips + apart for apart in late], [last], BF16)[None]
 
 
 def solution(mesh):

time: 78.4 us -> 77.8 us (level)
  waiting for transfers between devices: 28.8 us -> 27.8 us
    ppermute x3 -> x4, waiting for transfers between devices: 3.39 us -> 2.57 us  [to_core(): return lax.ppermute(array, 'seq', [(i, i ^ 1) for i in range(blocks)])]
    pallas_call x1 -> x2, Pallas kernels: 1.28 us -> 1.61 us  [combine(): call(functools.partial(combine_kernel, tuple(places)), shape((count, widt...]
    ppermute x3 -> x4, starting transfers between devices: 3.34 us -> 3.41 us  [to_core(): return lax.ppermute(array, 'seq', [(i, i ^ 1) for i in range(blocks)])]
  transfers between devices with their start and end apart: 22 -> 23, of which waited for: 11 -> 11; matrix products, arithmetic and copies ran while one was open for 0% -> 0% of each run, Pallas kernels for 16% -> 17%
where the time goes in v6:
time: 77.8 us; the launch traced here: 77.7 us
  starting transfers between devices  34.9 us (45%)
  waiting for transfers between devices  27.8 us (36%)
  Pallas kernels  14.5 us (19%)
    ppermute x12, starting transfers between devices, across(): return lax.ppermute(array, ('blk', 'seq'), pairs)  16.4 us
    ppermute x6, starting transfers between devices, to_chip(): lax.ppermute(array, 'seq', [(i, i ^ 2 * apart) for i in range(blocks)])  14.4 us
    ppermute x12, waiting for transfers between devices, across(): return lax.ppermute(array, ('blk', 'seq'), pairs)  12.6 us
    ppermute x6, waiting for transfers between devices, to_chip(): lax.ppermute(array, 'seq', [(i, i ^ 2 * apart) for i in range(blocks)])  12.6 us
    pallas_call x4, Pallas kernels, work(): call(functools.partial(act_kernel, pieces, 1), [shape((2 * size, hidden),...  5.03 us
    ppermute x4, starting transfers between devices, to_core(): return lax.ppermute(array, 'seq', [(i, i ^ 1) for i in range(blocks)])  3.41 us
    pallas_call x4, Pallas kernels, work(): call(functools.partial(down_kernel, pieces), (shape((size, width), F32),...  2.96 us
    ppermute x4, waiting for transfers between devices, to_core(): return lax.ppermute(array, 'seq', [(i, i ^ 1) for i in range(blocks)])  2.57 us
  transfers between devices with their start and end apart: 23, of which 11 were waited for; matrix products, arithmetic and copies ran while one was open for 0% of the time, Pallas kernels for 17%

profile of v6, /device:TPU:0, one launch (start us, length us, event | category | flops | bytes accessed | tf_op | source)
XLA Modules:
  0.0 77.7 jit_solution(14457375730549557315)
XLA Ops:
  0.0 3.0 %collective-permute-start.6 = (bf16[1024,512]{1,0:T(8,128)(2,1)}, bf16[1024,512]{1,0:T(8,128)(2,1)S(1)}, u32[]{:S(2)}, u32[]{:S(2)}) collective-permute-start(bf16[1024,512]{1,0:T(8,128)(2,1)} %bitcast.22), channel_id=1, source_target_pairs={{0,16},{1,9},{2,18},{3,11},{4,20},{5,13},{6,22},{7,15},{8,24},{9,1... | collective-permute-start | bytes 3145736 | tf_op jit(solution)/shard_map/ppermute | solution.py:303
  3.0 1.9 %shard_map.91 = (bf16[256,1024]{1,0:T(8,128)(2,1)S(1)}, bf16[496,1024]{1,0:T(8,128)(2,1)S(1)}, s32[1,256]{1,0:T(1,128)S(1)}, s32[1,8]{1,0:T(1,128)S(1)}, bf16[10...) custom-call(s32[1]{0:T(128)} %bitcast.place_ref, ...), custom_call_target="tpu_custom_call" | custom-call | tf_op jit(solution)/shard_map/pallas_call | solution.py:331
  4.9 0.1 collective-permute-start
  4.9 0.7 collective-permute-start.1
  5.6 1.1 %collective-permute-start.4 = (bf16[1024,512]{1,0:T(8,128)(2,1)S(1)}, bf16[1024,512]{1,0:T(8,128)(2,1)S(1)}, u32[]{:S(2)}, u32[]{:S(2)}) collective-permute-start(bf16[1024,512]{1,0:T(8,128)(2,1)S(1)} %bitcast.27), channel_id=1, source_target_pairs={{0,16},{1,9},{2,18},{3,11},{4,20},{5,13},{6,22},{7,15},{8,24},{9,1... | collective-permute-start | bytes 3145736 | tf_op jit(solution)/shard_map/ppermute | solution.py:303
  6.7 1.2 %shard_map.92 = (bf16[256,512]{1,0:T(8,128)(2,1)S(1)}, f32[256,8]{1,0:T(8,128)S(1)}, s32[256,8]{1,0:T(8,128)S(1)}, s32[1,256]{1,0:T(1,128)S(1)}) custom-call(bf16[256,1024]{1,0:T(8,128)(2,1)S(1)} %get-tuple-element.55.tokens_ref, bf16[496,1024]{1,0:T(8,128)(2,1)S(1)} %get-tuple-element.58.weight_ref, s32[1,256]{1,0:T(1,128)S(1)} %get-tuple-element.59.ids_ref, ...), custom_call_target="tpu_custom_call" | custom-call | tf_op jit(solution)/shard_map/pallas_call | solution.py:347
  8.0 1.5 %shard_map.93 = (f32[256,1024]{1,0:T(8,128)S(1)}, bf16[2,4,64,1024]{3,2,1,0:T(8,128)(2,1)S(1)}, f32[256,1]{1,0:T(8,128)S(1)}) custom-call(s32[1]{0:T(128)} %bitcast.place_ref, bf16[256,1024]{1,0:T(8,128)(2,1)S(1)} %get-tuple-element.55.tokens_ref, bf16[16,1024]{1,0:T(8,128)(2,1)S(1)} %collective-permute-done.near_ref, ...), custom_call_target="tpu_custom_call" | custom-call | tf_op jit(solution)/shard_map/pallas_call | solution.py:357
  9.5 0.1 slice_bitcast_fusion
  9.6 3.2 %collective-permute-start.2 = (bf16[4,64,1024]{2,1,0:T(8,128)(2,1)S(1)}, bf16[4,64,1024]{2,1,0:T(8,128)(2,1)S(1)}, u32[]{:S(2)}, u32[]{:S(2)}) collective-permute-start(bf16[4,64,1024]{2,1,0:T(8,128)(2,1)S(1)} %get-tuple-element.109), channel_id=1, source_target_pairs={{0,1},{1,0},{2,3},{3,2},{4,5},{5,4},{6,7},{7,6},{8,9},{9,8},{10,11... | collective-permute-start | bytes 1572872 | tf_op jit(solution)/shard_map/ppermute | solution.py:317
  12.8 1.5 %collective-permute-done.2 = bf16[4,64,1024]{2,1,0:T(8,128)(2,1)S(1)} collective-permute-done((bf16[4,64,1024]{2,1,0:T(8,128)(2,1)S(1)}, bf16[4,64,1024]{2,1,0:T(8,128)(2,1)S(1)}, u32[]{:S(2)}, u32[]{:S(2)}) %collective-permute-start.2) | collective-permute-done | bytes 524320 | tf_op jit(solution)/shard_map/ppermute | solution.py:317
  14.4 3.1 %collective-permute-start.3 = (bf16[128,1024]{1,0:T(8,128)(2,1)S(1)}, bf16[128,1024]{1,0:T(8,128)(2,1)S(1)}, u32[]{:S(2)}, u32[]{:S(2)}) collective-permute-start(bf16[128,1024]{1,0:T(8,128)(2,1)S(1)} %get-tuple-element.107), channel_id=1, source_target_pairs={{0,6},{1,7},{2,4},{3,5},{4,2},{5,3},{6,0},{7,1},{8,14},{9,15},{10,... | collective-permute-start | bytes 786440 | tf_op jit(solution)/shard_map/ppermute | solution.py:314
  17.5 1.0 %collective-permute-start.7 = (bf16[512,512]{1,0:T(8,128)(2,1)S(1)}, bf16[512,512]{1,0:T(8,128)(2,1)S(1)}, u32[]{:S(2)}, u32[]{:S(2)}) collective-permute-start(bf16[512,512]{1,0:T(8,128)(2,1)S(1)} %get-tuple-element.75.refs_2_), channel_id=1, source_target_pairs={{0,16},{1,9},{2,18},{3,11},{4,20},{5,13},{6,22},{7,15},{8,24},{9,1... | collective-permute-start | bytes 1572872 | tf_op jit(solution)/shard_map/ppermute | solution.py:303
  18.5 1.0 %collective-permute-start.8 = (bf16[512,512]{1,0:T(8,128)(2,1)S(1)}, bf16[512,512]{1,0:T(8,128)(2,1)S(1)}, u32[]{:S(2)}, u32[]{:S(2)}) collective-permute-start(bf16[512,512]{1,0:T(8,128)(2,1)S(1)} %get-tuple-element.76.refs_3_), channel_id=1, source_target_pairs={{0,16},{1,9},{2,18},{3,11},{4,20},{5,13},{6,22},{7,15},{8,24},{9,1... | collective-permute-start | bytes 1572872 | tf_op jit(solution)/shard_map/ppermute | solution.py:303
  19.5 5.4 %collective-permute-done.3.refs_0_ = bf16[128,1024]{1,0:T(8,128)(2,1)S(1)} collective-permute-done((bf16[128,1024]{1,0:T(8,128)(2,1)S(1)}, bf16[128,1024]{1,0:T(8,128)(2,1)S(1)}, u32[]{:S(2)}, u32[]{:S(2)}) %collective-permute-start.3) | collective-permute-done | bytes 262176 | tf_op jit(solution)/shard_map/ppermute | solution.py:314
  25.0 2.2 %collective-permute-done.4.refs_5_ = bf16[1024,512]{1,0:T(8,128)(2,1)S(1)} collective-permute-done((bf16[1024,512]{1,0:T(8,128)(2,1)S(1)}, bf16[1024,512]{1,0:T(8,128)(2,1)S(1)}, u32[]{:S(2)}, u32[]{:S(2)}) %collective-permute-start.4) | collective-permute-done | bytes 1048608 | tf_op jit(solution)/shard_map/ppermute | solution.py:303
  27.2 2.0 %collective-permute-start.5 = (bf16[128,1024]{1,0:T(8,128)(2,1)S(1)}, bf16[128,1024]{1,0:T(8,128)(2,1)S(1)}, u32[]{:S(2)}, u32[]{:S(2)}) collective-permute-start(bf16[128,1024]{1,0:T(8,128)(2,1)S(1)} %collective-permute-done.3.refs_0_), channel_id=1, source_target_pairs={{0,8},{1,17},{2,10},{3,19},{4,12},{5,21},{6,14},{7,23},{8,0},{9,25... | collective-permute-start | bytes 786440 | tf_op jit(solution)/shard_map/ppermute | solution.py:303
  29.2 3.4 %collective-permute-start.15 = (bf16[128,1024]{1,0:T(8,128)(2,1)S(1)}, bf16[128,1024]{1,0:T(8,128)(2,1)S(1)}, u32[]{:S(2)}, u32[]{:S(2)}) collective-permute-start(bf16[128,1024]{1,0:T(8,128)(2,1)S(1)} %get-tuple-element.90), channel_id=1, source_target_pairs={{0,4},{1,5},{2,6},{3,7},{4,0},{5,1},{6,2},{7,3},{8,12},{9,13},{10,... | collective-permute-start | bytes 786440 | tf_op jit(solution)/shard_map/ppermute | solution.py:314
  32.6 0.7 collective-permute-start.11
  33.4 3.1 %collective-permute-done.5.refs_1_ = bf16[128,1024]{1,0:T(8,128)(2,1)S(1)} collective-permute-done((bf16[128,1024]{1,0:T(8,128)(2,1)S(1)}, bf16[128,1024]{1,0:T(8,128)(2,1)S(1)}, u32[]{:S(2)}, u32[]{:S(2)}) %collective-permute-start.5) | collective-permute-done | bytes 262176 | tf_op jit(solution)/shard_map/ppermute | solution.py:303
  36.4 1.3 %shard_map.94 = (bf16[256,512]{1,0:T(8,128)(2,1)S(1)}, bf16[256,512]{1,0:T(8,128)(2,1)S(1)}) custom-call(bf16[128,1024]{1,0:T(8,128)(2,1)S(1)} %collective-permute-done.3.refs_0_, bf16[128,1024]{1,0:T(8,128)(2,1)S(1)} %collective-permute-done.5.refs_1_, bf16[1024,512]{1,0:T(8,128)(2,1)S(1)} %bitcast.23, bf16[1024,512]{1,0:T(8,128)(2,1)S(1)} %bitcast.28, ...), custom_call_target="tpu_custom_call" | custom-call | tf_op jit(solution)/shard_map/pallas_call | solution.py:386
  37.7 3.5 %collective-permute-done.8.refs_5_ = bf16[512,512]{1,0:T(8,128)(2,1)S(1)} collective-permute-done((bf16[512,512]{1,0:T(8,128)(2,1)S(1)}, bf16[512,512]{1,0:T(8,128)(2,1)S(1)}, u32[]{:S(2)}, u32[]{:S(2)}) %collective-permute-start.8) | collective-permute-done | bytes 524320 | tf_op jit(solution)/shard_map/ppermute | solution.py:303
  41.2 0.7 shard_map.95
  42.0 2.1 %collective-permute-start.16 = (bf16[128,1024]{1,0:T(8,128)(2,1)S(1)}, bf16[128,1024]{1,0:T(8,128)(2,1)S(1)}, u32[]{:S(2)}, u32[]{:S(2)}) collective-permute-start(bf16[128,1024]{1,0:T(8,128)(2,1)S(1)} %get-tuple-element.77), channel_id=1, source_target_pairs={{0,8},{1,17},{2,10},{3,19},{4,12},{5,21},{6,14},{7,23},{8,0},{9,25... | collective-permute-start | bytes 786440 | tf_op jit(solution)/shard_map/ppermute | solution.py:303
  44.0 0.5 collective-permute-start.17
  44.6 1.5 %collective-permute-start.12 = (bf16[128,1024]{1,0:T(8,128)(2,1)S(1)}, bf16[128,1024]{1,0:T(8,128)(2,1)S(1)}, u32[]{:S(2)}, u32[]{:S(2)}) collective-permute-start(bf16[128,1024]{1,0:T(8,128)(2,1)S(1)} %collective-permute-done.11.refs_0_), channel_id=1, source_target_pairs={{0,8},{1,17},{2,10},{3,19},{4,12},{5,21},{6,14},{7,23},{8,0},{9,25... | collective-permute-start | bytes 786440 | tf_op jit(solution)/shard_map/ppermute | solution.py:303
  46.1 0.5 collective-permute-start.9
  46.6 1.8 %collective-permute-done.16.other_ref = bf16[128,1024]{1,0:T(8,128)(2,1)S(1)} collective-permute-done((bf16[128,1024]{1,0:T(8,128)(2,1)S(1)}, bf16[128,1024]{1,0:T(8,128)(2,1)S(1)}, u32[]{:S(2)}, u32[]{:S(2)}) %collective-permute-start.16) | collective-permute-done | bytes 262176 | tf_op jit(solution)/shard_map/ppermute | solution.py:303
  48.5 4.2 %collective-permute-start.19 = (bf16[128,1024]{1,0:T(8,128)(2,1)S(1)}, bf16[128,1024]{1,0:T(8,128)(2,1)S(1)}, u32[]{:S(2)}, u32[]{:S(2)}) collective-permute-start(bf16[128,1024]{1,0:T(8,128)(2,1)S(1)} %shard_map.104), channel_id=1, source_target_pairs={{0,6},{1,7},{2,4},{3,5},{4,2},{5,3},{6,0},{7,1},{8,14},{9,15},{10,... | collective-permute-start | bytes 786440 | tf_op jit(solution)/shard_map/ppermute | solution.py:314
  52.6 1.3 %shard_map.105 = (bf16[256,512]{1,0:T(8,128)(2,1)S(1)}, bf16[256,512]{1,0:T(8,128)(2,1)S(1)}) custom-call(bf16[128,1024]{1,0:T(8,128)(2,1)S(1)} %collective-permute-done.15.refs_0_, bf16[128,1024]{1,0:T(8,128)(2,1)S(1)} %collective-permute-done.17.refs_1_, bf16[1024,512]{1,0:T(8,128)(2,1)S(1)} %bitcast.24, bf16[1024,512]{1,0:T(8,128)(2,1)S(1)} %bitcast.29, ...), custom_call_target="tpu_custom_call" | custom-call | tf_op jit(solution)/shard_map/pallas_call | solution.py:386
  53.9 0.7 shard_map.106
  54.7 1.6 %collective-permute-start.18 = (bf16[128,1024]{1,0:T(8,128)(2,1)S(1)}, bf16[128,1024]{1,0:T(8,128)(2,1)S(1)}, u32[]{:S(2)}, u32[]{:S(2)}) collective-permute-start(bf16[128,1024]{1,0:T(8,128)(2,1)S(1)} %get-tuple-element.97), channel_id=1, source_target_pairs={{0,8},{1,17},{2,10},{3,19},{4,12},{5,21},{6,14},{7,23},{8,0},{9,25... | collective-permute-start | bytes 786440 | tf_op jit(solution)/shard_map/ppermute | solution.py:303
  56.2 1.3 %shard_map.100 = (bf16[256,512]{1,0:T(8,128)(2,1)S(1)}, bf16[256,512]{1,0:T(8,128)(2,1)S(1)}) custom-call(bf16[128,1024]{1,0:T(8,128)(2,1)S(1)} %collective-permute-done.11.refs_0_, bf16[128,1024]{1,0:T(8,128)(2,1)S(1)} %collective-permute-done.12.refs_1_, bf16[1024,512]{1,0:T(8,128)(2,1)S(1)} %bitcast.25, bf16[1024,512]{1,0:T(8,128)(2,1)S(1)} %bitcast.30, ...), custom_call_target="tpu_custom_call" | custom-call | tf_op jit(solution)/shard_map/pallas_call | solution.py:386
  57.5 0.7 shard_map.101
  58.2 0.6 collective-permute-start.13
  58.8 1.3 %shard_map.96 = (bf16[256,512]{1,0:T(8,128)(2,1)S(1)}, bf16[256,512]{1,0:T(8,128)(2,1)S(1)}) custom-call(bf16[128,1024]{1,0:T(8,128)(2,1)S(1)} %get-tuple-element.78.refs_0_, bf16[128,1024]{1,0:T(8,128)(2,1)S(1)} %collective-permute-done.9.refs_1_, bf16[1024,512]{1,0:T(8,128)(2,1)S(1)} %bitcast.26, bf16[1024,512]{1,0:T(8,128)(2,1)S(1)} %bitcast.31, ...), custom_call_target="tpu_custom_call" | custom-call | tf_op jit(solution)/shard_map/pallas_call | solution.py:386
  60.1 0.7 shard_map.97
  60.8 1.6 %collective-permute-start.10 = (bf16[128,1024]{1,0:T(8,128)(2,1)S(1)}, bf16[128,1024]{1,0:T(8,128)(2,1)S(1)}, u32[]{:S(2)}, u32[]{:S(2)}) collective-permute-start(bf16[128,1024]{1,0:T(8,128)(2,1)S(1)} %get-tuple-element.82), channel_id=1, source_target_pairs={{0,8},{1,17},{2,10},{3,19},{4,12},{5,21},{6,14},{7,23},{8,0},{9,25... | collective-permute-start | bytes 786440 | tf_op jit(solution)/shard_map/ppermute | solution.py:303
  62.5 1.7 %collective-permute-start.20 = (bf16[128,1024]{1,0:T(8,128)(2,1)S(1)}, bf16[128,1024]{1,0:T(8,128)(2,1)S(1)}, u32[]{:S(2)}, u32[]{:S(2)}) collective-permute-start(bf16[128,1024]{1,0:T(8,128)(2,1)S(1)} %shard_map.107), channel_id=1, source_target_pairs={{0,4},{1,5},{2,6},{3,7},{4,0},{5,1},{6,2},{7,3},{8,12},{9,13},{10,... | collective-permute-start | bytes 786440 | tf_op jit(solution)/shard_map/ppermute | solution.py:314
  64.2 0.4 collective-permute-done.13.other_ref
  64.7 1.2 %collective-permute-start.14 = (bf16[128,1024]{1,0:T(8,128)(2,1)S(1)}, bf16[128,1024]{1,0:T(8,128)(2,1)S(1)}, u32[]{:S(2)}, u32[]{:S(2)}) collective-permute-start(bf16[128,1024]{1,0:T(8,128)(2,1)S(1)} %shard_map.102), channel_id=1, source_target_pairs={{0,2},{1,3},{2,0},{3,1},{4,6},{5,7},{6,4},{7,5},{8,10},{9,11},{10,... | collective-permute-start | bytes 786440 | tf_op jit(solution)/shard_map/ppermute | solution.py:314
  65.9 1.5 %collective-permute-done.10.other_ref = bf16[128,1024]{1,0:T(8,128)(2,1)S(1)} collective-permute-done((bf16[128,1024]{1,0:T(8,128)(2,1)S(1)}, bf16[128,1024]{1,0:T(8,128)(2,1)S(1)}, u32[]{:S(2)}, u32[]{:S(2)}) %collective-permute-start.10) | collective-permute-done | bytes 262176 | tf_op jit(solution)/shard_map/ppermute | solution.py:303
  67.6 0.1 collective-permute-start.21
  67.7 6.8 %collective-permute-done.20.back_ref = bf16[128,1024]{1,0:T(8,128)(2,1)S(1)} collective-permute-done((bf16[128,1024]{1,0:T(8,128)(2,1)S(1)}, bf16[128,1024]{1,0:T(8,128)(2,1)S(1)}, u32[]{:S(2)}, u32[]{:S(2)}) %collective-permute-start.20) | collective-permute-done | bytes 262176 | tf_op jit(solution)/shard_map/ppermute | solution.py:314
  74.4 0.4 collective-permute-done.14.back_ref
  74.9 0.1 collective-permute-start.22
  75.0 0.5 shard_map.110.total_ref
  75.5 1.0 %collective-permute-done.22.refs_0_ = bf16[128,1024]{1,0:T(8,128)(2,1)S(1)} collective-permute-done((bf16[128,1024]{1,0:T(8,128)(2,1)S(1)}, bf16[128,1024]{1,0:T(8,128)(2,1)S(1)}, u32[]{:S(2)}, u32[]{:S(2)}) %collective-permute-start.22) | collective-permute-done | bytes 262176 | tf_op jit(solution)/shard_map/ppermute | solution.py:317
  76.5 1.1 %shard_map.111 = bf16[256,1024]{1,0:T(8,128)(2,1)} custom-call(f32[256,1024]{1,0:T(8,128)S(1)} %shard_map.110.total_ref, f32[256,1]{1,0:T(8,128)S(1)} %get-tuple-element.67.gate_ref, s32[256,8]{1,0:T(8,128)S(1)} %get-tuple-element.68.slot_ref, bf16[128,1024]{1,0:T(8,128)(2,1)S(1)} %collective-permute-done.22.refs_0_), custom_call_target="tpu_custom_call" | custom-call | tf_op jit(solution)/shard_map/pallas_call | solution.py:421
  (27 shorter events, 0.4 us)
Async XLA Ops:
  0.0 17.5 %collective-permute-start.6 = (bf16[1024,512]{1,0:T(8,128)(2,1)}, bf16[1024,512]{1,0:T(8,128)(2,1)S(1)}, u32[]{:S(2)}, u32[]{:S(2)}) collective-permute-start(bf16[1024,512]{1,0:T(8,128)(2,1)} %bitcast.22), channel_id=1, source_target_pairs={{0,16},{1,9},{2,18},{3,11},{4,20},{5,13},{6,22},{7,15},{8,24},{9,1... | collective-permute-start | bytes 3145736 | tf_op jit(solution)/shard_map/ppermute | solution.py:303
  3.0 2.6 %copy-start.1 = (bf16[1,1024,512]{2,1,0:T(8,128)(2,1)S(1)}, bf16[1,1024,512]{2,1,0:T(8,128)(2,1)}, u32[]{:S(2)}) copy-start(bf16[1,1024,512]{2,1,0:T(8,128)(2,1)} %param.16) | copy-start | bytes 3145732
  4.9 3.1 %collective-permute-start = (bf16[16,1024]{1,0:T(8,128)(2,1)S(1)}, bf16[16,1024]{1,0:T(8,128)(2,1)S(1)}, u32[]{:S(2)}, u32[]{:S(2)}) collective-permute-start(bf16[16,1024]{1,0:T(8,128)(2,1)S(1)} %get-tuple-element.56), channel_id=1, source_target_pairs={{0,1},{1,0},{2,3},{3,2},{4,5},{5,4},{6,7},{7,6},{8,9},{9,8},{10,11... | collective-permute-start | bytes 98312 | tf_op jit(solution)/shard_map/ppermute | solution.py:317
  4.9 3.0 %collective-permute-start.1 = (bf16[16,1024]{1,0:T(8,128)(2,1)S(1)}, bf16[16,1024]{1,0:T(8,128)(2,1)S(1)}, u32[]{:S(2)}, u32[]{:S(2)}) collective-permute-start(bf16[16,1024]{1,0:T(8,128)(2,1)S(1)} %get-tuple-element.57), channel_id=1, source_target_pairs={{1,2},{3,4},{5,6},{2,1},{4,3},{6,5},{9,10},{11,12},{13,14},{10,9},... | collective-permute-start | bytes 98312 | tf_op jit(solution)/shard_map/ppermute | solution.py:346
  5.6 21.6 %collective-permute-start.4 = (bf16[1024,512]{1,0:T(8,128)(2,1)S(1)}, bf16[1024,512]{1,0:T(8,128)(2,1)S(1)}, u32[]{:S(2)}, u32[]{:S(2)}) collective-permute-start(bf16[1024,512]{1,0:T(8,128)(2,1)S(1)} %bitcast.27), channel_id=1, source_target_pairs={{0,16},{1,9},{2,18},{3,11},{4,20},{5,13},{6,22},{7,15},{8,24},{9,1... | collective-permute-start | bytes 3145736 | tf_op jit(solution)/shard_map/ppermute | solution.py:303
  9.6 4.7 %collective-permute-start.2 = (bf16[4,64,1024]{2,1,0:T(8,128)(2,1)S(1)}, bf16[4,64,1024]{2,1,0:T(8,128)(2,1)S(1)}, u32[]{:S(2)}, u32[]{:S(2)}) collective-permute-start(bf16[4,64,1024]{2,1,0:T(8,128)(2,1)S(1)} %get-tuple-element.109), channel_id=1, source_target_pairs={{0,1},{1,0},{2,3},{3,2},{4,5},{5,4},{6,7},{7,6},{8,9},{9,8},{10,11... | collective-permute-start | bytes 1572872 | tf_op jit(solution)/shard_map/ppermute | solution.py:317
  14.3 22.1 %copy-start = (bf16[1,1024,512]{2,1,0:T(8,128)(2,1)S(1)}, bf16[1,1024,512]{2,1,0:T(8,128)(2,1)}, u32[]{:S(2)}) copy-start(bf16[1,1024,512]{2,1,0:T(8,128)(2,1)} %param.15) | copy-start | bytes 3145732
  14.4 10.6 %collective-permute-start.3 = (bf16[128,1024]{1,0:T(8,128)(2,1)S(1)}, bf16[128,1024]{1,0:T(8,128)(2,1)S(1)}, u32[]{:S(2)}, u32[]{:S(2)}) collective-permute-start(bf16[128,1024]{1,0:T(8,128)(2,1)S(1)} %get-tuple-element.107), channel_id=1, source_target_pairs={{0,6},{1,7},{2,4},{3,5},{4,2},{5,3},{6,0},{7,1},{8,14},{9,15},{10,... | collective-permute-start | bytes 786440 | tf_op jit(solution)/shard_map/ppermute | solution.py:314
  17.5 20.2 %collective-permute-start.7 = (bf16[512,512]{1,0:T(8,128)(2,1)S(1)}, bf16[512,512]{1,0:T(8,128)(2,1)S(1)}, u32[]{:S(2)}, u32[]{:S(2)}) collective-permute-start(bf16[512,512]{1,0:T(8,128)(2,1)S(1)} %get-tuple-element.75.refs_2_), channel_id=1, source_target_pairs={{0,16},{1,9},{2,18},{3,11},{4,20},{5,13},{6,22},{7,15},{8,24},{9,1... | collective-permute-start | bytes 1572872 | tf_op jit(solution)/shard_map/ppermute | solution.py:303
  18.5 22.7 %collective-permute-start.8 = (bf16[512,512]{1,0:T(8,128)(2,1)S(1)}, bf16[512,512]{1,0:T(8,128)(2,1)S(1)}, u32[]{:S(2)}, u32[]{:S(2)}) collective-permute-start(bf16[512,512]{1,0:T(8,128)(2,1)S(1)} %get-tuple-element.76.refs_3_), channel_id=1, source_target_pairs={{0,16},{1,9},{2,18},{3,11},{4,20},{5,13},{6,22},{7,15},{8,24},{9,1... | collective-permute-start | bytes 1572872 | tf_op jit(solution)/shard_map/ppermute | solution.py:303
  27.2 9.2 %collective-permute-start.5 = (bf16[128,1024]{1,0:T(8,128)(2,1)S(1)}, bf16[128,1024]{1,0:T(8,128)(2,1)S(1)}, u32[]{:S(2)}, u32[]{:S(2)}) collective-permute-start(bf16[128,1024]{1,0:T(8,128)(2,1)S(1)} %collective-permute-done.3.refs_0_), channel_id=1, source_target_pairs={{0,8},{1,17},{2,10},{3,19},{4,12},{5,21},{6,14},{7,23},{8,0},{9,25... | collective-permute-start | bytes 786440 | tf_op jit(solution)/shard_map/ppermute | solution.py:303
  29.2 14.9 %collective-permute-start.15 = (bf16[128,1024]{1,0:T(8,128)(2,1)S(1)}, bf16[128,1024]{1,0:T(8,128)(2,1)S(1)}, u32[]{:S(2)}, u32[]{:S(2)}) collective-permute-start(bf16[128,1024]{1,0:T(8,128)(2,1)S(1)} %get-tuple-element.90), channel_id=1, source_target_pairs={{0,4},{1,5},{2,6},{3,7},{4,0},{5,1},{6,2},{7,3},{8,12},{9,13},{10,... | collective-permute-start | bytes 786440 | tf_op jit(solution)/shard_map/ppermute | solution.py:314
  32.6 12.0 %collective-permute-start.11 = (bf16[128,1024]{1,0:T(8,128)(2,1)S(1)}, bf16[128,1024]{1,0:T(8,128)(2,1)S(1)}, u32[]{:S(2)}, u32[]{:S(2)}) collective-permute-start(bf16[128,1024]{1,0:T(8,128)(2,1)S(1)} %get-tuple-element.108), channel_id=1, source_target_pairs={{0,2},{1,3},{2,0},{3,1},{4,6},{5,7},{6,4},{7,5},{8,10},{9,11},{10,... | collective-permute-start | bytes 786440 | tf_op jit(solution)/shard_map/ppermute | solution.py:314
  42.0 6.4 %collective-permute-start.16 = (bf16[128,1024]{1,0:T(8,128)(2,1)S(1)}, bf16[128,1024]{1,0:T(8,128)(2,1)S(1)}, u32[]{:S(2)}, u32[]{:S(2)}) collective-permute-start(bf16[128,1024]{1,0:T(8,128)(2,1)S(1)} %get-tuple-element.77), channel_id=1, source_target_pairs={{0,8},{1,17},{2,10},{3,19},{4,12},{5,21},{6,14},{7,23},{8,0},{9,25... | collective-permute-start | bytes 786440 | tf_op jit(solution)/shard_map/ppermute | solution.py:303
  44.0 8.6 %collective-permute-start.17 = (bf16[128,1024]{1,0:T(8,128)(2,1)S(1)}, bf16[128,1024]{1,0:T(8,128)(2,1)S(1)}, u32[]{:S(2)}, u32[]{:S(2)}) collective-permute-start(bf16[128,1024]{1,0:T(8,128)(2,1)S(1)} %collective-permute-done.15.refs_0_), channel_id=1, source_target_pairs={{0,8},{1,17},{2,10},{3,19},{4,12},{5,21},{6,14},{7,23},{8,0},{9,25... | collective-permute-start | bytes 786440 | tf_op jit(solution)/shard_map/ppermute | solution.py:303
  44.6 11.6 %collective-permute-start.12 = (bf16[128,1024]{1,0:T(8,128)(2,1)S(1)}, bf16[128,1024]{1,0:T(8,128)(2,1)S(1)}, u32[]{:S(2)}, u32[]{:S(2)}) collective-permute-start(bf16[128,1024]{1,0:T(8,128)(2,1)S(1)} %collective-permute-done.11.refs_0_), channel_id=1, source_target_pairs={{0,8},{1,17},{2,10},{3,19},{4,12},{5,21},{6,14},{7,23},{8,0},{9,25... | collective-permute-start | bytes 786440 | tf_op jit(solution)/shard_map/ppermute | solution.py:303
  46.1 12.8 %collective-permute-start.9 = (bf16[128,1024]{1,0:T(8,128)(2,1)S(1)}, bf16[128,1024]{1,0:T(8,128)(2,1)S(1)}, u32[]{:S(2)}, u32[]{:S(2)}) collective-permute-start(bf16[128,1024]{1,0:T(8,128)(2,1)S(1)} %get-tuple-element.78.refs_0_), channel_id=1, source_target_pairs={{0,8},{1,17},{2,10},{3,19},{4,12},{5,21},{6,14},{7,23},{8,0},{9,25... | collective-permute-start | bytes 786440 | tf_op jit(solution)/shard_map/ppermute | solution.py:303
  48.5 13.9 %collective-permute-start.19 = (bf16[128,1024]{1,0:T(8,128)(2,1)S(1)}, bf16[128,1024]{1,0:T(8,128)(2,1)S(1)}, u32[]{:S(2)}, u32[]{:S(2)}) collective-permute-start(bf16[128,1024]{1,0:T(8,128)(2,1)S(1)} %shard_map.104), channel_id=1, source_target_pairs={{0,6},{1,7},{2,4},{3,5},{4,2},{5,3},{6,0},{7,1},{8,14},{9,15},{10,... | collective-permute-start | bytes 786440 | tf_op jit(solution)/shard_map/ppermute | solution.py:314
  54.7 7.8 %collective-permute-start.18 = (bf16[128,1024]{1,0:T(8,128)(2,1)S(1)}, bf16[128,1024]{1,0:T(8,128)(2,1)S(1)}, u32[]{:S(2)}, u32[]{:S(2)}) collective-permute-start(bf16[128,1024]{1,0:T(8,128)(2,1)S(1)} %get-tuple-element.97), channel_id=1, source_target_pairs={{0,8},{1,17},{2,10},{3,19},{4,12},{5,21},{6,14},{7,23},{8,0},{9,25... | collective-permute-start | bytes 786440 | tf_op jit(solution)/shard_map/ppermute | solution.py:303
  58.2 6.4 %collective-permute-start.13 = (bf16[128,1024]{1,0:T(8,128)(2,1)S(1)}, bf16[128,1024]{1,0:T(8,128)(2,1)S(1)}, u32[]{:S(2)}, u32[]{:S(2)}) collective-permute-start(bf16[128,1024]{1,0:T(8,128)(2,1)S(1)} %get-tuple-element.88), channel_id=1, source_target_pairs={{0,8},{1,17},{2,10},{3,19},{4,12},{5,21},{6,14},{7,23},{8,0},{9,25... | collective-permute-start | bytes 786440 | tf_op jit(solution)/shard_map/ppermute | solution.py:303
  60.8 6.6 %collective-permute-start.10 = (bf16[128,1024]{1,0:T(8,128)(2,1)S(1)}, bf16[128,1024]{1,0:T(8,128)(2,1)S(1)}, u32[]{:S(2)}, u32[]{:S(2)}) collective-permute-start(bf16[128,1024]{1,0:T(8,128)(2,1)S(1)} %get-tuple-element.82), channel_id=1, source_target_pairs={{0,8},{1,17},{2,10},{3,19},{4,12},{5,21},{6,14},{7,23},{8,0},{9,25... | collective-permute-start | bytes 786440 | tf_op jit(solution)/shard_map/ppermute | solution.py:303
  62.5 11.9 %collective-permute-start.20 = (bf16[128,1024]{1,0:T(8,128)(2,1)S(1)}, bf16[128,1024]{1,0:T(8,128)(2,1)S(1)}, u32[]{:S(2)}, u32[]{:S(2)}) collective-permute-start(bf16[128,1024]{1,0:T(8,128)(2,1)S(1)} %shard_map.107), channel_id=1, source_target_pairs={{0,4},{1,5},{2,6},{3,7},{4,0},{5,1},{6,2},{7,3},{8,12},{9,13},{10,... | collective-permute-start | bytes 786440 | tf_op jit(solution)/shard_map/ppermute | solution.py:314
  64.7 10.2 %collective-permute-start.14 = (bf16[128,1024]{1,0:T(8,128)(2,1)S(1)}, bf16[128,1024]{1,0:T(8,128)(2,1)S(1)}, u32[]{:S(2)}, u32[]{:S(2)}) collective-permute-start(bf16[128,1024]{1,0:T(8,128)(2,1)S(1)} %shard_map.102), channel_id=1, source_target_pairs={{0,2},{1,3},{2,0},{3,1},{4,6},{5,7},{6,4},{7,5},{8,10},{9,11},{10,... | collective-permute-start | bytes 786440 | tf_op jit(solution)/shard_map/ppermute | solution.py:314
  67.6 7.4 %collective-permute-start.21 = (bf16[128,1024]{1,0:T(8,128)(2,1)S(1)}, bf16[128,1024]{1,0:T(8,128)(2,1)S(1)}, u32[]{:S(2)}, u32[]{:S(2)}) collective-permute-start(bf16[128,1024]{1,0:T(8,128)(2,1)S(1)} %pad_maximum_fusion.1), channel_id=1, source_target_pairs={{0,1},{1,0},{2,3},{3,2},{4,5},{5,4},{6,7},{7,6},{8,9},{9,8},{10,11... | collective-permute-start | bytes 786440 | tf_op jit(solution)/shard_map/ppermute | solution.py:317
  74.9 1.6 %collective-permute-start.22 = (bf16[128,1024]{1,0:T(8,128)(2,1)S(1)}, bf16[128,1024]{1,0:T(8,128)(2,1)S(1)}, u32[]{:S(2)}, u32[]{:S(2)}) collective-permute-start(bf16[128,1024]{1,0:T(8,128)(2,1)S(1)} %pad_maximum_fusion.2), channel_id=1, source_target_pairs={{0,1},{1,0},{2,3},{3,2},{4,5},{5,4},{6,7},{7,6},{8,9},{9,8},{10,11... | collective-permute-start | bytes 786440 | tf_op jit(solution)/shard_map/ppermute | solution.py:317

commit v7 on v6

--- a/solution.py
+++ b/solution.py
@@ -322,13 +322,11 @@
         kernel_weight.T,
         expert_ids[0].reshape(1, count),
         expert_capacity[None, :],
-        norm_gain,
-        router.T,
         expert_down[0],
     ]
     half = (width // 2, expert_down.shape[2])
     hidden = expert_gate.shape[2]
-    local, kernel_rows, ids, capacity, gain, columns, *down, near_edge, cross_edge = call(
+    local, kernel_rows, ids, capacity, *down, near_edge, cross_edge = call(
         fetch_kernel,
         [pltpu.VMEM(array.shape, array.dtype) for array in sources[:-1]]
         + [pltpu.VMEM(half, BF16)] * 2
@@ -366,7 +364,17 @@
             pltpu.VMEM((count, width), BF16),
         ),
         in_specs=[SMEM] + [VMEM] * 8,
-    )(place, local, near_edge, cross_edge, probs, onehot, slot_row, gain, columns)
+    )(
+        place,
+        local,
+        near_edge,
+        cross_edge,
+        probs,
+        onehot,
+        slot_row,
+        norm_gain[None, :],
+        router.T,
+    )
     crossed = to_core(packed[1])
     both = jnp.concatenate([packed[0], crossed], axis=1)
     size = 2 * depth
@@ -417,6 +425,7 @@
         arrive(apart, None)
         work(apart, sums[order[0]][1])
         finish(apart)
+
     def combine(total, places, arrays, dtype):
         return call(
             functools.partial(combine_kernel, tuple(places)),

time: 77.8 us -> 77.8 us (level)
  no operation moved by 1% of the time
where the time goes in v7:
time: 77.8 us; the launch traced here: 77.7 us
  starting transfers between devices  34.8 us (45%)
  waiting for transfers between devices  27.9 us (36%)
  Pallas kernels  14.5 us (19%)
    ppermute x12, starting transfers between devices, across(): return lax.ppermute(array, ('blk', 'seq'), pairs)  16.4 us
    ppermute x6, starting transfers between devices, to_chip(): lax.ppermute(array, 'seq', [(i, i ^ 2 * apart) for i in range(blocks)])  14.4 us
    ppermute x12, waiting for transfers between devices, across(): return lax.ppermute(array, ('blk', 'seq'), pairs)  12.7 us
    ppermute x6, waiting for transfers between devices, to_chip(): lax.ppermute(array, 'seq', [(i, i ^ 2 * apart) for i in range(blocks)])  12.7 us
    pallas_call x4, Pallas kernels, work(): call(functools.partial(act_kernel, pieces, 1), [shape((2 * size, hidden),...  5.03 us
    ppermute x4, starting transfers between devices, to_core(): return lax.ppermute(array, 'seq', [(i, i ^ 1) for i in range(blocks)])  3.41 us
    pallas_call x4, Pallas kernels, work(): call(functools.partial(down_kernel, pieces), (shape((size, width), F32),...  2.96 us
    ppermute x4, waiting for transfers between devices, to_core(): return lax.ppermute(array, 'seq', [(i, i ^ 1) for i in range(blocks)])  2.57 us
  transfers between devices with their start and end apart: 23, of which 11 were waited for; matrix products, arithmetic and copies ran while one was open for 0% of the time, Pallas kernels for 17%

profile of v7, /device:TPU:0, one launch (start us, length us, event | category | flops | bytes accessed | tf_op | source)
XLA Modules:
  0.0 77.7 jit_solution(4329779897044667896)
XLA Ops:
  0.0 3.0 %collective-permute-start.6 = (bf16[1024,512]{1,0:T(8,128)(2,1)}, bf16[1024,512]{1,0:T(8,128)(2,1)S(1)}, u32[]{:S(2)}, u32[]{:S(2)}) collective-permute-start(bf16[1024,512]{1,0:T(8,128)(2,1)} %bitcast.22), channel_id=1, source_target_pairs={{0,16},{1,9},{2,18},{3,11},{4,20},{5,13},{6,22},{7,15},{8,24},{9,1... | collective-permute-start | bytes 3145736 | tf_op jit(solution)/shard_map/ppermute | solution.py:303
  3.0 1.8 %shard_map.91 = (bf16[256,1024]{1,0:T(8,128)(2,1)S(1)}, bf16[496,1024]{1,0:T(8,128)(2,1)S(1)}, s32[1,256]{1,0:T(1,128)S(1)}, s32[1,8]{1,0:T(1,128)S(1)}, bf16[51...) custom-call(s32[1]{0:T(128)} %bitcast.place_ref, ...), custom_call_target="tpu_custom_call" | custom-call | tf_op jit(solution)/shard_map/pallas_call | solution.py:329
  4.8 0.1 collective-permute-start
  4.9 0.7 collective-permute-start.1
  5.6 1.1 %collective-permute-start.4 = (bf16[1024,512]{1,0:T(8,128)(2,1)S(1)}, bf16[1024,512]{1,0:T(8,128)(2,1)S(1)}, u32[]{:S(2)}, u32[]{:S(2)}) collective-permute-start(bf16[1024,512]{1,0:T(8,128)(2,1)S(1)} %bitcast.27), channel_id=1, source_target_pairs={{0,16},{1,9},{2,18},{3,11},{4,20},{5,13},{6,22},{7,15},{8,24},{9,1... | collective-permute-start | bytes 3145736 | tf_op jit(solution)/shard_map/ppermute | solution.py:303
  6.7 1.2 %shard_map.92 = (bf16[256,512]{1,0:T(8,128)(2,1)S(1)}, f32[256,8]{1,0:T(8,128)S(1)}, s32[256,8]{1,0:T(8,128)S(1)}, s32[1,256]{1,0:T(1,128)S(1)}) custom-call(bf16[256,1024]{1,0:T(8,128)(2,1)S(1)} %get-tuple-element.53.tokens_ref, bf16[496,1024]{1,0:T(8,128)(2,1)S(1)} %get-tuple-element.56.weight_ref, s32[1,256]{1,0:T(1,128)S(1)} %get-tuple-element.57.ids_ref, ...), custom_call_target="tpu_custom_call" | custom-call | tf_op jit(solution)/shard_map/pallas_call | solution.py:345
  8.0 1.5 %shard_map.93 = (f32[256,1024]{1,0:T(8,128)S(1)}, bf16[2,4,64,1024]{3,2,1,0:T(8,128)(2,1)S(1)}, f32[256,1]{1,0:T(8,128)S(1)}) custom-call(s32[1]{0:T(128)} %bitcast.place_ref, bf16[256,1024]{1,0:T(8,128)(2,1)S(1)} %get-tuple-element.53.tokens_ref, bf16[16,1024]{1,0:T(8,128)(2,1)S(1)} %collective-permute-done.near_ref, ...), custom_call_target="tpu_custom_call" | custom-call | tf_op jit(solution)/shard_map/pallas_call | solution.py:355
  9.5 0.1 slice_bitcast_fusion
  9.6 3.2 %collective-permute-start.2 = (bf16[4,64,1024]{2,1,0:T(8,128)(2,1)S(1)}, bf16[4,64,1024]{2,1,0:T(8,128)(2,1)S(1)}, u32[]{:S(2)}, u32[]{:S(2)}) collective-permute-start(bf16[4,64,1024]{2,1,0:T(8,128)(2,1)S(1)} %get-tuple-element.105), channel_id=1, source_target_pairs={{0,1},{1,0},{2,3},{3,2},{4,5},{5,4},{6,7},{7,6},{8,9},{9,8},{10,11... | collective-permute-start | bytes 1572872 | tf_op jit(solution)/shard_map/ppermute | solution.py:317
  12.8 1.5 %collective-permute-done.2 = bf16[4,64,1024]{2,1,0:T(8,128)(2,1)S(1)} collective-permute-done((bf16[4,64,1024]{2,1,0:T(8,128)(2,1)S(1)}, bf16[4,64,1024]{2,1,0:T(8,128)(2,1)S(1)}, u32[]{:S(2)}, u32[]{:S(2)}) %collective-permute-start.2) | collective-permute-done | bytes 524320 | tf_op jit(solution)/shard_map/ppermute | solution.py:317
  14.4 3.1 %collective-permute-start.3 = (bf16[128,1024]{1,0:T(8,128)(2,1)S(1)}, bf16[128,1024]{1,0:T(8,128)(2,1)S(1)}, u32[]{:S(2)}, u32[]{:S(2)}) collective-permute-start(bf16[128,1024]{1,0:T(8,128)(2,1)S(1)} %get-tuple-element.103), channel_id=1, source_target_pairs={{0,6},{1,7},{2,4},{3,5},{4,2},{5,3},{6,0},{7,1},{8,14},{9,15},{10,... | collective-permute-start | bytes 786440 | tf_op jit(solution)/shard_map/ppermute | solution.py:314
  17.5 1.0 %collective-permute-start.7 = (bf16[512,512]{1,0:T(8,128)(2,1)S(1)}, bf16[512,512]{1,0:T(8,128)(2,1)S(1)}, u32[]{:S(2)}, u32[]{:S(2)}) collective-permute-start(bf16[512,512]{1,0:T(8,128)(2,1)S(1)} %get-tuple-element.71.refs_2_), channel_id=1, source_target_pairs={{0,16},{1,9},{2,18},{3,11},{4,20},{5,13},{6,22},{7,15},{8,24},{9,1... | collective-permute-start | bytes 1572872 | tf_op jit(solution)/shard_map/ppermute | solution.py:303
  18.5 1.0 %collective-permute-start.8 = (bf16[512,512]{1,0:T(8,128)(2,1)S(1)}, bf16[512,512]{1,0:T(8,128)(2,1)S(1)}, u32[]{:S(2)}, u32[]{:S(2)}) collective-permute-start(bf16[512,512]{1,0:T(8,128)(2,1)S(1)} %get-tuple-element.72.refs_3_), channel_id=1, source_target_pairs={{0,16},{1,9},{2,18},{3,11},{4,20},{5,13},{6,22},{7,15},{8,24},{9,1... | collective-permute-start | bytes 1572872 | tf_op jit(solution)/shard_map/ppermute | solution.py:303
  19.5 5.4 %collective-permute-done.3.refs_0_ = bf16[128,1024]{1,0:T(8,128)(2,1)S(1)} collective-permute-done((bf16[128,1024]{1,0:T(8,128)(2,1)S(1)}, bf16[128,1024]{1,0:T(8,128)(2,1)S(1)}, u32[]{:S(2)}, u32[]{:S(2)}) %collective-permute-start.3) | collective-permute-done | bytes 262176 | tf_op jit(solution)/shard_map/ppermute | solution.py:314
  24.9 2.2 %collective-permute-done.4.refs_5_ = bf16[1024,512]{1,0:T(8,128)(2,1)S(1)} collective-permute-done((bf16[1024,512]{1,0:T(8,128)(2,1)S(1)}, bf16[1024,512]{1,0:T(8,128)(2,1)S(1)}, u32[]{:S(2)}, u32[]{:S(2)}) %collective-permute-start.4) | collective-permute-done | bytes 1048608 | tf_op jit(solution)/shard_map/ppermute | solution.py:303
  27.2 2.0 %collective-permute-start.5 = (bf16[128,1024]{1,0:T(8,128)(2,1)S(1)}, bf16[128,1024]{1,0:T(8,128)(2,1)S(1)}, u32[]{:S(2)}, u32[]{:S(2)}) collective-permute-start(bf16[128,1024]{1,0:T(8,128)(2,1)S(1)} %collective-permute-done.3.refs_0_), channel_id=1, source_target_pairs={{0,8},{1,17},{2,10},{3,19},{4,12},{5,21},{6,14},{7,23},{8,0},{9,25... | collective-permute-start | bytes 786440 | tf_op jit(solution)/shard_map/ppermute | solution.py:303
  29.2 3.4 %collective-permute-start.15 = (bf16[128,1024]{1,0:T(8,128)(2,1)S(1)}, bf16[128,1024]{1,0:T(8,128)(2,1)S(1)}, u32[]{:S(2)}, u32[]{:S(2)}) collective-permute-start(bf16[128,1024]{1,0:T(8,128)(2,1)S(1)} %get-tuple-element.86), channel_id=1, source_target_pairs={{0,4},{1,5},{2,6},{3,7},{4,0},{5,1},{6,2},{7,3},{8,12},{9,13},{10,... | collective-permute-start | bytes 786440 | tf_op jit(solution)/shard_map/ppermute | solution.py:314
  32.6 0.8 %collective-permute-start.11 = (bf16[128,1024]{1,0:T(8,128)(2,1)S(1)}, bf16[128,1024]{1,0:T(8,128)(2,1)S(1)}, u32[]{:S(2)}, u32[]{:S(2)}) collective-permute-start(bf16[128,1024]{1,0:T(8,128)(2,1)S(1)} %get-tuple-element.104), channel_id=1, source_target_pairs={{0,2},{1,3},{2,0},{3,1},{4,6},{5,7},{6,4},{7,5},{8,10},{9,11},{10,... | collective-permute-start | bytes 786440 | tf_op jit(solution)/shard_map/ppermute | solution.py:314
  33.4 3.1 %collective-permute-done.5.refs_1_ = bf16[128,1024]{1,0:T(8,128)(2,1)S(1)} collective-permute-done((bf16[128,1024]{1,0:T(8,128)(2,1)S(1)}, bf16[128,1024]{1,0:T(8,128)(2,1)S(1)}, u32[]{:S(2)}, u32[]{:S(2)}) %collective-permute-start.5) | collective-permute-done | bytes 262176 | tf_op jit(solution)/shard_map/ppermute | solution.py:303
  36.4 1.3 %shard_map.94 = (bf16[256,512]{1,0:T(8,128)(2,1)S(1)}, bf16[256,512]{1,0:T(8,128)(2,1)S(1)}) custom-call(bf16[128,1024]{1,0:T(8,128)(2,1)S(1)} %collective-permute-done.3.refs_0_, bf16[128,1024]{1,0:T(8,128)(2,1)S(1)} %collective-permute-done.5.refs_1_, bf16[1024,512]{1,0:T(8,128)(2,1)S(1)} %bitcast.23, bf16[1024,512]{1,0:T(8,128)(2,1)S(1)} %bitcast.28, ...), custom_call_target="tpu_custom_call" | custom-call | tf_op jit(solution)/shard_map/pallas_call | solution.py:394
  37.7 3.5 %collective-permute-done.8.refs_5_ = bf16[512,512]{1,0:T(8,128)(2,1)S(1)} collective-permute-done((bf16[512,512]{1,0:T(8,128)(2,1)S(1)}, bf16[512,512]{1,0:T(8,128)(2,1)S(1)}, u32[]{:S(2)}, u32[]{:S(2)}) %collective-permute-start.8) | collective-permute-done | bytes 524320 | tf_op jit(solution)/shard_map/ppermute | solution.py:303
  41.2 0.7 shard_map.95
  42.0 2.1 %collective-permute-start.16 = (bf16[128,1024]{1,0:T(8,128)(2,1)S(1)}, bf16[128,1024]{1,0:T(8,128)(2,1)S(1)}, u32[]{:S(2)}, u32[]{:S(2)}) collective-permute-start(bf16[128,1024]{1,0:T(8,128)(2,1)S(1)} %get-tuple-element.73), channel_id=1, source_target_pairs={{0,8},{1,17},{2,10},{3,19},{4,12},{5,21},{6,14},{7,23},{8,0},{9,25... | collective-permute-start | bytes 786440 | tf_op jit(solution)/shard_map/ppermute | solution.py:303
  44.0 0.5 collective-permute-start.17
  44.6 1.5 %collective-permute-start.12 = (bf16[128,1024]{1,0:T(8,128)(2,1)S(1)}, bf16[128,1024]{1,0:T(8,128)(2,1)S(1)}, u32[]{:S(2)}, u32[]{:S(2)}) collective-permute-start(bf16[128,1024]{1,0:T(8,128)(2,1)S(1)} %collective-permute-done.11.refs_0_), channel_id=1, source_target_pairs={{0,8},{1,17},{2,10},{3,19},{4,12},{5,21},{6,14},{7,23},{8,0},{9,25... | collective-permute-start | bytes 786440 | tf_op jit(solution)/shard_map/ppermute | solution.py:303
  46.1 0.5 collective-permute-start.9
  46.6 1.8 %collective-permute-done.16.other_ref = bf16[128,1024]{1,0:T(8,128)(2,1)S(1)} collective-permute-done((bf16[128,1024]{1,0:T(8,128)(2,1)S(1)}, bf16[128,1024]{1,0:T(8,128)(2,1)S(1)}, u32[]{:S(2)}, u32[]{:S(2)}) %collective-permute-start.16) | collective-permute-done | bytes 262176 | tf_op jit(solution)/shard_map/ppermute | solution.py:303
  48.5 4.2 %collective-permute-start.19 = (bf16[128,1024]{1,0:T(8,128)(2,1)S(1)}, bf16[128,1024]{1,0:T(8,128)(2,1)S(1)}, u32[]{:S(2)}, u32[]{:S(2)}) collective-permute-start(bf16[128,1024]{1,0:T(8,128)(2,1)S(1)} %shard_map.104), channel_id=1, source_target_pairs={{0,6},{1,7},{2,4},{3,5},{4,2},{5,3},{6,0},{7,1},{8,14},{9,15},{10,... | collective-permute-start | bytes 786440 | tf_op jit(solution)/shard_map/ppermute | solution.py:314
  52.6 1.3 %shard_map.105 = (bf16[256,512]{1,0:T(8,128)(2,1)S(1)}, bf16[256,512]{1,0:T(8,128)(2,1)S(1)}) custom-call(bf16[128,1024]{1,0:T(8,128)(2,1)S(1)} %collective-permute-done.15.refs_0_, bf16[128,1024]{1,0:T(8,128)(2,1)S(1)} %collective-permute-done.17.refs_1_, bf16[1024,512]{1,0:T(8,128)(2,1)S(1)} %bitcast.24, bf16[1024,512]{1,0:T(8,128)(2,1)S(1)} %bitcast.29, ...), custom_call_target="tpu_custom_call" | custom-call | tf_op jit(solution)/shard_map/pallas_call | solution.py:394
  53.9 0.7 shard_map.106
  54.7 1.6 %collective-permute-start.18 = (bf16[128,1024]{1,0:T(8,128)(2,1)S(1)}, bf16[128,1024]{1,0:T(8,128)(2,1)S(1)}, u32[]{:S(2)}, u32[]{:S(2)}) collective-permute-start(bf16[128,1024]{1,0:T(8,128)(2,1)S(1)} %get-tuple-element.93), channel_id=1, source_target_pairs={{0,8},{1,17},{2,10},{3,19},{4,12},{5,21},{6,14},{7,23},{8,0},{9,25... | collective-permute-start | bytes 786440 | tf_op jit(solution)/shard_map/ppermute | solution.py:303
  56.2 1.3 %shard_map.100 = (bf16[256,512]{1,0:T(8,128)(2,1)S(1)}, bf16[256,512]{1,0:T(8,128)(2,1)S(1)}) custom-call(bf16[128,1024]{1,0:T(8,128)(2,1)S(1)} %collective-permute-done.11.refs_0_, bf16[128,1024]{1,0:T(8,128)(2,1)S(1)} %collective-permute-done.12.refs_1_, bf16[1024,512]{1,0:T(8,128)(2,1)S(1)} %bitcast.25, bf16[1024,512]{1,0:T(8,128)(2,1)S(1)} %bitcast.30, ...), custom_call_target="tpu_custom_call" | custom-call | tf_op jit(solution)/shard_map/pallas_call | solution.py:394
  57.5 0.7 shard_map.101
  58.2 0.6 collective-permute-start.13
  58.8 1.3 %shard_map.96 = (bf16[256,512]{1,0:T(8,128)(2,1)S(1)}, bf16[256,512]{1,0:T(8,128)(2,1)S(1)}) custom-call(bf16[128,1024]{1,0:T(8,128)(2,1)S(1)} %get-tuple-element.74.refs_0_, bf16[128,1024]{1,0:T(8,128)(2,1)S(1)} %collective-permute-done.9.refs_1_, bf16[1024,512]{1,0:T(8,128)(2,1)S(1)} %bitcast.26, bf16[1024,512]{1,0:T(8,128)(2,1)S(1)} %bitcast.31, ...), custom_call_target="tpu_custom_call" | custom-call | tf_op jit(solution)/shard_map/pallas_call | solution.py:394
  60.1 0.7 shard_map.97
  60.8 1.6 %collective-permute-start.10 = (bf16[128,1024]{1,0:T(8,128)(2,1)S(1)}, bf16[128,1024]{1,0:T(8,128)(2,1)S(1)}, u32[]{:S(2)}, u32[]{:S(2)}) collective-permute-start(bf16[128,1024]{1,0:T(8,128)(2,1)S(1)} %get-tuple-element.78), channel_id=1, source_target_pairs={{0,8},{1,17},{2,10},{3,19},{4,12},{5,21},{6,14},{7,23},{8,0},{9,25... | collective-permute-start | bytes 786440 | tf_op jit(solution)/shard_map/ppermute | solution.py:303
  62.5 1.7 %collective-permute-start.20 = (bf16[128,1024]{1,0:T(8,128)(2,1)S(1)}, bf16[128,1024]{1,0:T(8,128)(2,1)S(1)}, u32[]{:S(2)}, u32[]{:S(2)}) collective-permute-start(bf16[128,1024]{1,0:T(8,128)(2,1)S(1)} %shard_map.107), channel_id=1, source_target_pairs={{0,4},{1,5},{2,6},{3,7},{4,0},{5,1},{6,2},{7,3},{8,12},{9,13},{10,... | collective-permute-start | bytes 786440 | tf_op jit(solution)/shard_map/ppermute | solution.py:314
  64.2 0.4 collective-permute-done.13.other_ref
  64.7 1.2 %collective-permute-start.14 = (bf16[128,1024]{1,0:T(8,128)(2,1)S(1)}, bf16[128,1024]{1,0:T(8,128)(2,1)S(1)}, u32[]{:S(2)}, u32[]{:S(2)}) collective-permute-start(bf16[128,1024]{1,0:T(8,128)(2,1)S(1)} %shard_map.102), channel_id=1, source_target_pairs={{0,2},{1,3},{2,0},{3,1},{4,6},{5,7},{6,4},{7,5},{8,10},{9,11},{10,... | collective-permute-start | bytes 786440 | tf_op jit(solution)/shard_map/ppermute | solution.py:314
  65.9 1.5 %collective-permute-done.10.other_ref = bf16[128,1024]{1,0:T(8,128)(2,1)S(1)} collective-permute-done((bf16[128,1024]{1,0:T(8,128)(2,1)S(1)}, bf16[128,1024]{1,0:T(8,128)(2,1)S(1)}, u32[]{:S(2)}, u32[]{:S(2)}) %collective-permute-start.10) | collective-permute-done | bytes 262176 | tf_op jit(solution)/shard_map/ppermute | solution.py:303
  67.6 0.1 collective-permute-start.21
  67.7 6.8 %collective-permute-done.20.back_ref = bf16[128,1024]{1,0:T(8,128)(2,1)S(1)} collective-permute-done((bf16[128,1024]{1,0:T(8,128)(2,1)S(1)}, bf16[128,1024]{1,0:T(8,128)(2,1)S(1)}, u32[]{:S(2)}, u32[]{:S(2)}) %collective-permute-start.20) | collective-permute-done | bytes 262176 | tf_op jit(solution)/shard_map/ppermute | solution.py:314
  74.4 0.4 collective-permute-done.14.back_ref
  74.9 0.1 collective-permute-start.22
  75.0 0.5 shard_map.110.total_ref
  75.5 1.0 %collective-permute-done.22.refs_0_ = bf16[128,1024]{1,0:T(8,128)(2,1)S(1)} collective-permute-done((bf16[128,1024]{1,0:T(8,128)(2,1)S(1)}, bf16[128,1024]{1,0:T(8,128)(2,1)S(1)}, u32[]{:S(2)}, u32[]{:S(2)}) %collective-permute-start.22) | collective-permute-done | bytes 262176 | tf_op jit(solution)/shard_map/ppermute | solution.py:317
  76.5 1.1 %shard_map.111 = bf16[256,1024]{1,0:T(8,128)(2,1)} custom-call(f32[256,1024]{1,0:T(8,128)S(1)} %shard_map.110.total_ref, f32[256,1]{1,0:T(8,128)S(1)} %get-tuple-element.63.gate_ref, s32[256,8]{1,0:T(8,128)S(1)} %get-tuple-element.64.slot_ref, bf16[128,1024]{1,0:T(8,128)(2,1)S(1)} %collective-permute-done.22.refs_0_), custom_call_target="tpu_custom_call" | custom-call | tf_op jit(solution)/shard_map/pallas_call | solution.py:430
  (32 shorter events, 0.4 us)
Async XLA Ops:
  0.0 17.5 %collective-permute-start.6 = (bf16[1024,512]{1,0:T(8,128)(2,1)}, bf16[1024,512]{1,0:T(8,128)(2,1)S(1)}, u32[]{:S(2)}, u32[]{:S(2)}) collective-permute-start(bf16[1024,512]{1,0:T(8,128)(2,1)} %bitcast.22), channel_id=1, source_target_pairs={{0,16},{1,9},{2,18},{3,11},{4,20},{5,13},{6,22},{7,15},{8,24},{9,1... | collective-permute-start | bytes 3145736 | tf_op jit(solution)/shard_map/ppermute | solution.py:303
  3.0 2.6 %copy-start.1 = (bf16[1,1024,512]{2,1,0:T(8,128)(2,1)S(1)}, bf16[1,1024,512]{2,1,0:T(8,128)(2,1)}, u32[]{:S(2)}) copy-start(bf16[1,1024,512]{2,1,0:T(8,128)(2,1)} %param.16) | copy-start | bytes 3145732
  4.8 1.9 %copy-start.3 = (bf16[1024]{0:T(1024)(128)(2,1)S(1)}, bf16[1024]{0:T(1024)(128)(2,1)}, u32[]{:S(2)}) copy-start(bf16[1024]{0:T(1024)(128)(2,1)} %param.13) | copy-start | bytes 6148
  4.8 3.1 %collective-permute-start = (bf16[16,1024]{1,0:T(8,128)(2,1)S(1)}, bf16[16,1024]{1,0:T(8,128)(2,1)S(1)}, u32[]{:S(2)}, u32[]{:S(2)}) collective-permute-start(bf16[16,1024]{1,0:T(8,128)(2,1)S(1)} %get-tuple-element.54), channel_id=1, source_target_pairs={{0,1},{1,0},{2,3},{3,2},{4,5},{5,4},{6,7},{7,6},{8,9},{9,8},{10,11... | collective-permute-start | bytes 98312 | tf_op jit(solution)/shard_map/ppermute | solution.py:317
  4.9 3.0 %collective-permute-start.1 = (bf16[16,1024]{1,0:T(8,128)(2,1)S(1)}, bf16[16,1024]{1,0:T(8,128)(2,1)S(1)}, u32[]{:S(2)}, u32[]{:S(2)}) collective-permute-start(bf16[16,1024]{1,0:T(8,128)(2,1)S(1)} %get-tuple-element.55), channel_id=1, source_target_pairs={{1,2},{3,4},{5,6},{2,1},{4,3},{6,5},{9,10},{11,12},{13,14},{10,9},... | collective-permute-start | bytes 98312 | tf_op jit(solution)/shard_map/ppermute | solution.py:344
  5.6 21.6 %collective-permute-start.4 = (bf16[1024,512]{1,0:T(8,128)(2,1)S(1)}, bf16[1024,512]{1,0:T(8,128)(2,1)S(1)}, u32[]{:S(2)}, u32[]{:S(2)}) collective-permute-start(bf16[1024,512]{1,0:T(8,128)(2,1)S(1)} %bitcast.27), channel_id=1, source_target_pairs={{0,16},{1,9},{2,18},{3,11},{4,20},{5,13},{6,22},{7,15},{8,24},{9,1... | collective-permute-start | bytes 3145736 | tf_op jit(solution)/shard_map/ppermute | solution.py:303
  6.7 1.3 %copy-start.2 = (bf16[1024,8]{0,1:T(8,128)(2,1)S(1)}, bf16[1024,8]{0,1:T(8,128)(2,1)}, u32[]{:S(2)}) copy-start(bf16[1024,8]{0,1:T(8,128)(2,1)} %param.14) | copy-start | bytes 49156
  9.6 4.7 %collective-permute-start.2 = (bf16[4,64,1024]{2,1,0:T(8,128)(2,1)S(1)}, bf16[4,64,1024]{2,1,0:T(8,128)(2,1)S(1)}, u32[]{:S(2)}, u32[]{:S(2)}) collective-permute-start(bf16[4,64,1024]{2,1,0:T(8,128)(2,1)S(1)} %get-tuple-element.105), channel_id=1, source_target_pairs={{0,1},{1,0},{2,3},{3,2},{4,5},{5,4},{6,7},{7,6},{8,9},{9,8},{10,11... | collective-permute-start | bytes 1572872 | tf_op jit(solution)/shard_map/ppermute | solution.py:317
  14.3 22.1 %copy-start = (bf16[1,1024,512]{2,1,0:T(8,128)(2,1)S(1)}, bf16[1,1024,512]{2,1,0:T(8,128)(2,1)}, u32[]{:S(2)}) copy-start(bf16[1,1024,512]{2,1,0:T(8,128)(2,1)} %param.15) | copy-start | bytes 3145732
  14.4 10.6 %collective-permute-start.3 = (bf16[128,1024]{1,0:T(8,128)(2,1)S(1)}, bf16[128,1024]{1,0:T(8,128)(2,1)S(1)}, u32[]{:S(2)}, u32[]{:S(2)}) collective-permute-start(bf16[128,1024]{1,0:T(8,128)(2,1)S(1)} %get-tuple-element.103), channel_id=1, source_target_pairs={{0,6},{1,7},{2,4},{3,5},{4,2},{5,3},{6,0},{7,1},{8,14},{9,15},{10,... | collective-permute-start | bytes 786440 | tf_op jit(solution)/shard_map/ppermute | solution.py:314
  17.5 20.2 %collective-permute-start.7 = (bf16[512,512]{1,0:T(8,128)(2,1)S(1)}, bf16[512,512]{1,0:T(8,128)(2,1)S(1)}, u32[]{:S(2)}, u32[]{:S(2)}) collective-permute-start(bf16[512,512]{1,0:T(8,128)(2,1)S(1)} %get-tuple-element.71.refs_2_), channel_id=1, source_target_pairs={{0,16},{1,9},{2,18},{3,11},{4,20},{5,13},{6,22},{7,15},{8,24},{9,1... | collective-permute-start | bytes 1572872 | tf_op jit(solution)/shard_map/ppermute | solution.py:303
  18.5 22.7 %collective-permute-start.8 = (bf16[512,512]{1,0:T(8,128)(2,1)S(1)}, bf16[512,512]{1,0:T(8,128)(2,1)S(1)}, u32[]{:S(2)}, u32[]{:S(2)}) collective-permute-start(bf16[512,512]{1,0:T(8,128)(2,1)S(1)} %get-tuple-element.72.refs_3_), channel_id=1, source_target_pairs={{0,16},{1,9},{2,18},{3,11},{4,20},{5,13},{6,22},{7,15},{8,24},{9,1... | collective-permute-start | bytes 1572872 | tf_op jit(solution)/shard_map/ppermute | solution.py:303
  27.2 9.2 %collective-permute-start.5 = (bf16[128,1024]{1,0:T(8,128)(2,1)S(1)}, bf16[128,1024]{1,0:T(8,128)(2,1)S(1)}, u32[]{:S(2)}, u32[]{:S(2)}) collective-permute-start(bf16[128,1024]{1,0:T(8,128)(2,1)S(1)} %collective-permute-done.3.refs_0_), channel_id=1, source_target_pairs={{0,8},{1,17},{2,10},{3,19},{4,12},{5,21},{6,14},{7,23},{8,0},{9,25... | collective-permute-start | bytes 786440 | tf_op jit(solution)/shard_map/ppermute | solution.py:303
  29.2 14.9 %collective-permute-start.15 = (bf16[128,1024]{1,0:T(8,128)(2,1)S(1)}, bf16[128,1024]{1,0:T(8,128)(2,1)S(1)}, u32[]{:S(2)}, u32[]{:S(2)}) collective-permute-start(bf16[128,1024]{1,0:T(8,128)(2,1)S(1)} %get-tuple-element.86), channel_id=1, source_target_pairs={{0,4},{1,5},{2,6},{3,7},{4,0},{5,1},{6,2},{7,3},{8,12},{9,13},{10,... | collective-permute-start | bytes 786440 | tf_op jit(solution)/shard_map/ppermute | solution.py:314
  32.6 12.0 %collective-permute-start.11 = (bf16[128,1024]{1,0:T(8,128)(2,1)S(1)}, bf16[128,1024]{1,0:T(8,128)(2,1)S(1)}, u32[]{:S(2)}, u32[]{:S(2)}) collective-permute-start(bf16[128,1024]{1,0:T(8,128)(2,1)S(1)} %get-tuple-element.104), channel_id=1, source_target_pairs={{0,2},{1,3},{2,0},{3,1},{4,6},{5,7},{6,4},{7,5},{8,10},{9,11},{10,... | collective-permute-start | bytes 786440 | tf_op jit(solution)/shard_map/ppermute | solution.py:314
  42.0 6.4 %collective-permute-start.16 = (bf16[128,1024]{1,0:T(8,128)(2,1)S(1)}, bf16[128,1024]{1,0:T(8,128)(2,1)S(1)}, u32[]{:S(2)}, u32[]{:S(2)}) collective-permute-start(bf16[128,1024]{1,0:T(8,128)(2,1)S(1)} %get-tuple-element.73), channel_id=1, source_target_pairs={{0,8},{1,17},{2,10},{3,19},{4,12},{5,21},{6,14},{7,23},{8,0},{9,25... | collective-permute-start | bytes 786440 | tf_op jit(solution)/shard_map/ppermute | solution.py:303
  44.0 8.6 %collective-permute-start.17 = (bf16[128,1024]{1,0:T(8,128)(2,1)S(1)}, bf16[128,1024]{1,0:T(8,128)(2,1)S(1)}, u32[]{:S(2)}, u32[]{:S(2)}) collective-permute-start(bf16[128,1024]{1,0:T(8,128)(2,1)S(1)} %collective-permute-done.15.refs_0_), channel_id=1, source_target_pairs={{0,8},{1,17},{2,10},{3,19},{4,12},{5,21},{6,14},{7,23},{8,0},{9,25... | collective-permute-start | bytes 786440 | tf_op jit(solution)/shard_map/ppermute | solution.py:303
  44.6 11.7 %collective-permute-start.12 = (bf16[128,1024]{1,0:T(8,128)(2,1)S(1)}, bf16[128,1024]{1,0:T(8,128)(2,1)S(1)}, u32[]{:S(2)}, u32[]{:S(2)}) collective-permute-start(bf16[128,1024]{1,0:T(8,128)(2,1)S(1)} %collective-permute-done.11.refs_0_), channel_id=1, source_target_pairs={{0,8},{1,17},{2,10},{3,19},{4,12},{5,21},{6,14},{7,23},{8,0},{9,25... | collective-permute-start | bytes 786440 | tf_op jit(solution)/shard_map/ppermute | solution.py:303
  46.1 12.8 %collective-permute-start.9 = (bf16[128,1024]{1,0:T(8,128)(2,1)S(1)}, bf16[128,1024]{1,0:T(8,128)(2,1)S(1)}, u32[]{:S(2)}, u32[]{:S(2)}) collective-permute-start(bf16[128,1024]{1,0:T(8,128)(2,1)S(1)} %get-tuple-element.74.refs_0_), channel_id=1, source_target_pairs={{0,8},{1,17},{2,10},{3,19},{4,12},{5,21},{6,14},{7,23},{8,0},{9,25... | collective-permute-start | bytes 786440 | tf_op jit(solution)/shard_map/ppermute | solution.py:303
  48.5 13.9 %collective-permute-start.19 = (bf16[128,1024]{1,0:T(8,128)(2,1)S(1)}, bf16[128,1024]{1,0:T(8,128)(2,1)S(1)}, u32[]{:S(2)}, u32[]{:S(2)}) collective-permute-start(bf16[128,1024]{1,0:T(8,128)(2,1)S(1)} %shard_map.104), channel_id=1, source_target_pairs={{0,6},{1,7},{2,4},{3,5},{4,2},{5,3},{6,0},{7,1},{8,14},{9,15},{10,... | collective-permute-start | bytes 786440 | tf_op jit(solution)/shard_map/ppermute | solution.py:314
  54.7 7.8 %collective-permute-start.18 = (bf16[128,1024]{1,0:T(8,128)(2,1)S(1)}, bf16[128,1024]{1,0:T(8,128)(2,1)S(1)}, u32[]{:S(2)}, u32[]{:S(2)}) collective-permute-start(bf16[128,1024]{1,0:T(8,128)(2,1)S(1)} %get-tuple-element.93), channel_id=1, source_target_pairs={{0,8},{1,17},{2,10},{3,19},{4,12},{5,21},{6,14},{7,23},{8,0},{9,25... | collective-permute-start | bytes 786440 | tf_op jit(solution)/shard_map/ppermute | solution.py:303
  58.2 6.4 %collective-permute-start.13 = (bf16[128,1024]{1,0:T(8,128)(2,1)S(1)}, bf16[128,1024]{1,0:T(8,128)(2,1)S(1)}, u32[]{:S(2)}, u32[]{:S(2)}) collective-permute-start(bf16[128,1024]{1,0:T(8,128)(2,1)S(1)} %get-tuple-element.84), channel_id=1, source_target_pairs={{0,8},{1,17},{2,10},{3,19},{4,12},{5,21},{6,14},{7,23},{8,0},{9,25... | collective-permute-start | bytes 786440 | tf_op jit(solution)/shard_map/ppermute | solution.py:303
  60.8 6.6 %collective-permute-start.10 = (bf16[128,1024]{1,0:T(8,128)(2,1)S(1)}, bf16[128,1024]{1,0:T(8,128)(2,1)S(1)}, u32[]{:S(2)}, u32[]{:S(2)}) collective-permute-start(bf16[128,1024]{1,0:T(8,128)(2,1)S(1)} %get-tuple-element.78), channel_id=1, source_target_pairs={{0,8},{1,17},{2,10},{3,19},{4,12},{5,21},{6,14},{7,23},{8,0},{9,25... | collective-permute-start | bytes 786440 | tf_op jit(solution)/shard_map/ppermute | solution.py:303
  62.5 11.9 %collective-permute-start.20 = (bf16[128,1024]{1,0:T(8,128)(2,1)S(1)}, bf16[128,1024]{1,0:T(8,128)(2,1)S(1)}, u32[]{:S(2)}, u32[]{:S(2)}) collective-permute-start(bf16[128,1024]{1,0:T(8,128)(2,1)S(1)} %shard_map.107), channel_id=1, source_target_pairs={{0,4},{1,5},{2,6},{3,7},{4,0},{5,1},{6,2},{7,3},{8,12},{9,13},{10,... | collective-permute-start | bytes 786440 | tf_op jit(solution)/shard_map/ppermute | solution.py:314
  64.7 10.2 %collective-permute-start.14 = (bf16[128,1024]{1,0:T(8,128)(2,1)S(1)}, bf16[128,1024]{1,0:T(8,128)(2,1)S(1)}, u32[]{:S(2)}, u32[]{:S(2)}) collective-permute-start(bf16[128,1024]{1,0:T(8,128)(2,1)S(1)} %shard_map.102), channel_id=1, source_target_pairs={{0,2},{1,3},{2,0},{3,1},{4,6},{5,7},{6,4},{7,5},{8,10},{9,11},{10,... | collective-permute-start | bytes 786440 | tf_op jit(solution)/shard_map/ppermute | solution.py:314
  67.6 7.4 %collective-permute-start.21 = (bf16[128,1024]{1,0:T(8,128)(2,1)S(1)}, bf16[128,1024]{1,0:T(8,128)(2,1)S(1)}, u32[]{:S(2)}, u32[]{:S(2)}) collective-permute-start(bf16[128,1024]{1,0:T(8,128)(2,1)S(1)} %pad_maximum_fusion.1), channel_id=1, source_target_pairs={{0,1},{1,0},{2,3},{3,2},{4,5},{5,4},{6,7},{7,6},{8,9},{9,8},{10,11... | collective-permute-start | bytes 786440 | tf_op jit(solution)/shard_map/ppermute | solution.py:317
  74.9 1.6 %collective-permute-start.22 = (bf16[128,1024]{1,0:T(8,128)(2,1)S(1)}, bf16[128,1024]{1,0:T(8,128)(2,1)S(1)}, u32[]{:S(2)}, u32[]{:S(2)}) collective-permute-start(bf16[128,1024]{1,0:T(8,128)(2,1)S(1)} %pad_maximum_fusion.2), channel_id=1, source_target_pairs={{0,1},{1,0},{2,3},{3,2},{4,5},{5,4},{6,7},{7,6},{8,9},{9,8},{10,11... | collective-permute-start | bytes 786440 | tf_op jit(solution)/shard_map/ppermute | solution.py:317
